TPU v7x, 32 devices: a whole 2x2x4 slice. The times are simulated.
32 devices in a mesh: dp: 8 (over y, x, core), ctx: 4 (over z).
Axes of the slice: x: 2, y: 2, z: 4, core: 2. Of those that a mesh axis runs over, the one named last changes fastest.
Arguments:
- roll_query: bfloat16 [8, 512, 4096], P('dp', 'ctx'), may hold values from -12 to 12
- roll_keys: bfloat16 [8, 512, 512], P('dp', 'ctx'), may hold values from -12 to 12
- roll_values: bfloat16 [8, 512, 512], P('dp', 'ctx'), may hold values from -6 to 6
- pack_dest: int32 [8, 64], P(None, 'ctx'), may hold values from 0 to 7, as said below
- segment_ids: int32 [8, 512], P('dp', 'ctx'), may hold values from 0 to 15, never falling along the last dimension, each value on 1 to 256 neighbouring positions
- reward_bins: int32 [8, 16], P('dp'), may hold values from 0 to 511
- reward_weight: float32 [4096], replicated, may hold values from -0.5 to 0.5
Outputs:
- attention_out: bfloat16 [8, 512, 4096], P('dp', 'ctx')
- reward_hist: float32 [512], replicated
Inputs may be any that keep to these rules, and one draw needn't show every extreme that they name: For every column j the entries pack_dest[s, j] over s are a permutation of the packed sequences. Among the 16 columns of one ctx shard, at most 2 blocks go from one source to one packed sequence, and exactly 2 for some pair in every shard.
All inputs are finite; a program needn't handle non-finite values.
Results may differ from a plain program's by a relative error of at most 0.004.
Values may be sent and summed in bfloat16 or wider, within the bound.
No kernel may reach another device: no remote copies, remote signals or barrier semaphores. Data moves between devices by JAX's collectives and lax.ppermute only.
A program may use at most 64 MiB of HBM per device.

v0:
```python
import math

import jax
import jax.numpy as jnp
from jax import lax
from jax.sharding import PartitionSpec as P

HQ = 32
HK = 4
HD = 128
BLK = 8
SEGS = 16
BINS = 512


NEG = -1e30


def shifted(block, axis, distance):
    devices = range(lax.axis_size(axis))
    route = [(i - distance, i) for i in devices if i - distance in devices]
    return lax.ppermute(block, axis, route)


def block_rank(labels):
    count_all = labels.shape[0]
    earlier = jnp.arange(count_all)[:, None] < jnp.arange(count_all)[None, :]
    same_label = labels[:, None] == labels[None, :]
    return jnp.sum(jnp.where(same_label & earlier, 1, 0), axis=0).astype(jnp.int32)


def select_rows(selector, source_rows):
    flat_rows = source_rows.reshape(selector.shape[1], -1)
    return jnp.dot(selector, flat_rows, preferred_element_type=jnp.float32).astype(jnp.bfloat16)


def local(roll_query, roll_keys, roll_values, pack_dest, segment_ids, reward_bins, reward_weight):
    dp_count = lax.axis_size("dp")
    dp_self = lax.axis_index("dp")
    ctx_self = lax.axis_index("ctx")
    row_count = roll_query.shape[1]
    block_count = row_count // BLK
    q_width = roll_query.shape[2]
    kv_width = roll_keys.shape[2]
    cap_here = (block_count + dp_count - 1) // dp_count
    slot_count = dp_count * cap_here
    group_size = HQ // HK
    score_scale = 1.0 / math.sqrt(HD)
    own_dest = lax.dynamic_index_in_dim(pack_dest, dp_self, 0, keepdims=False)
    send_slot = own_dest * cap_here + block_rank(own_dest)
    send_sel = (jnp.arange(slot_count, dtype=jnp.int32)[:, None] == send_slot[None, :]).astype(
        jnp.bfloat16
    )
    send_query = select_rows(send_sel, roll_query[0]).reshape(dp_count, cap_here * BLK, q_width)
    send_keys = select_rows(send_sel, roll_keys[0]).reshape(dp_count, cap_here * BLK, kv_width)
    send_values = select_rows(send_sel, roll_values[0]).reshape(dp_count, cap_here * BLK, kv_width)
    got_query, got_keys, got_values = (
        lax.all_to_all(send_query, "dp", split_axis=0, concat_axis=0, tiled=True),
        lax.all_to_all(send_keys, "dp", split_axis=0, concat_axis=0, tiled=True),
        lax.all_to_all(send_values, "dp", split_axis=0, concat_axis=0, tiled=True),
    )
    matched = pack_dest == dp_self
    earlier = jnp.arange(block_count)[:, None] < jnp.arange(block_count)[None, :]
    recv_rank = jnp.sum(jnp.where(matched[:, :, None] & earlier[None], 1, 0), axis=1)
    source_ids = jnp.arange(dp_count, dtype=jnp.int32)[:, None]
    recv_slot = jnp.sum(jnp.where(matched, source_ids * cap_here + recv_rank, 0), axis=0)
    recv_sel = (recv_slot[:, None] == jnp.arange(slot_count, dtype=jnp.int32)[None, :]).astype(
        jnp.bfloat16
    )
    packed_query = select_rows(recv_sel, got_query).reshape(row_count, q_width)
    packed_keys = select_rows(recv_sel, got_keys).reshape(row_count, kv_width)
    packed_values = select_rows(recv_sel, got_values).reshape(row_count, kv_width)
    seg_local = segment_ids[0]
    query_heads = packed_query.reshape(row_count, HK, group_size, HD)
    query_pos = ctx_self * row_count + jnp.arange(row_count, dtype=jnp.int32)

    def attend_block(running, key_rows, value_rows, key_segments, first_row):
        key_count = key_rows.shape[0]
        key_pos = first_row + jnp.arange(key_count, dtype=jnp.int32)
        allowed = (seg_local[:, None] == key_segments[None, :]) & (
            key_pos[None, :] <= query_pos[:, None]
        )
        scores = (
            jnp.einsum(
                "qgjd,kgd->gjqk",
                query_heads,
                key_rows.reshape(key_count, HK, HD),
                preferred_element_type=jnp.float32,
            )
            * score_scale
        )
        scores = jnp.where(allowed, scores, NEG)
        run_max, run_sum, run_acc = running
        new_max = jnp.maximum(run_max, jnp.max(scores, axis=-1))
        weights = jnp.where(allowed, jnp.exp(scores - new_max[..., None]), 0.0)
        shrink = jnp.exp(run_max - new_max)
        new_sum = run_sum * shrink + jnp.sum(weights, axis=-1)
        update = jnp.einsum(
            "gjqk,kgd->qgjd",
            weights.astype(jnp.bfloat16),
            value_rows.reshape(key_count, HK, HD),
            preferred_element_type=jnp.float32,
        )
        new_acc = run_acc * jnp.transpose(shrink, (2, 0, 1))[..., None] + update
        return (new_max, new_sum, new_acc)

    initial = (
        jnp.full((HK, group_size, row_count), NEG, jnp.float32),
        jnp.zeros((HK, group_size, row_count), jnp.float32),
        jnp.zeros((row_count, HK, group_size, HD), jnp.float32),
    )
    key_rows = lax.all_gather(packed_keys, "ctx", axis=0, tiled=True)
    value_rows = lax.all_gather(packed_values, "ctx", axis=0, tiled=True)
    key_segments = lax.all_gather(seg_local, "ctx", axis=0, tiled=True)
    key_count = key_rows.shape[0]

    def sub_block(turn_index, carried):
        offset = turn_index * row_count
        return attend_block(
            carried,
            lax.dynamic_slice_in_dim(key_rows, offset, row_count, 0),
            lax.dynamic_slice_in_dim(value_rows, offset, row_count, 0),
            lax.dynamic_slice_in_dim(key_segments, offset, row_count, 0),
            offset,
        )

    final_max, final_sum, final_acc = lax.fori_loop(0, key_count // row_count, sub_block, initial)
    attended = (
        (final_acc / jnp.transpose(final_sum, (2, 0, 1))[..., None])
        .reshape(row_count, q_width)
        .astype(jnp.bfloat16)
    )
    next_first = shifted(seg_local[:1] + 1, "ctx", -1)
    next_plus = jnp.concatenate([seg_local[1:] + 1, next_first])
    is_end = next_plus != seg_local + 1
    row_reward = jnp.dot(
        attended, reward_weight, precision=lax.Precision.HIGHEST, preferred_element_type=jnp.float32
    )
    kept = jnp.where(is_end, row_reward, 0.0)
    seg_match = seg_local[:, None] == jnp.arange(SEGS, dtype=jnp.int32)[None, :]
    bin_of = jnp.sum(jnp.where(seg_match, reward_bins[0][None, :], 0), axis=1)
    bin_match = bin_of[:, None] == jnp.arange(BINS, dtype=jnp.int32)[None, :]
    local_hist = jnp.sum(jnp.where(bin_match, kept[:, None], 0.0), axis=0)
    histogram = lax.psum(local_hist, ("dp", "ctx"))
    return (attended.reshape(1, row_count, q_width), histogram)


def solution(mesh):
    in_specs = (
        P("dp", "ctx", None),
        P("dp", "ctx", None),
        P("dp", "ctx", None),
        P(None, "ctx"),
        P("dp", "ctx"),
        P("dp", None),
        P(),
    )
    out_specs = (P("dp", "ctx", None), P())
    return jax.shard_map(local, mesh=mesh, in_specs=in_specs, out_specs=out_specs, check_vma=False)
```

profile of v0, /device:TPU:0, one launch (start us, length us, event | category | flops | bytes accessed | tf_op | source)
XLA Modules:
  0.0 139.3 jit_solution(10685377434742589235)
XLA Ops:
  0.7 0.7 fusion.23
  1.4 0.7 fusion.22
  2.1 1.0 reshape_squeeze.9
  3.3 0.7 reshape.97
  4.0 5.2 %all-to-all-start = ((bf16[8,16,512]{2,1,0:T(8,128)(2,1)}), bf16[8,16,512]{2,1,0:T(8,128)(2,1)S(1)}, u32[]{:S(2)}, u32[]{:S(2)}) async-start(bf16[8,16,512]{2,1,0:T(8,128)(2,1)} %reshape.97), calls=%async_computation | async-start | bytes 262144 | tf_op jit(solution)/shard_map/all_to_all | solution.py:59
  9.8 1.3 collective-permute-start
  11.1 0.7 broadcast_compare_fusion
  11.8 0.7 add_bitcast_fusion
  12.5 1.6 %reshape_squeeze.10 = bf16[16,32768]{1,0:T(8,128)(2,1)S(1)} reshape(bf16[1,128,4096]{2,1,0:T(8,128)(2,1)} %param.9) | data formatting | bytes 2097152 | tf_op jit(solution)/shard_map/reshape;squeeze | solution.py:33
  14.9 1.3 reshape.100
  16.2 0.7 reshape.102
  17.0 4.2 %all-to-all-start.2 = ((bf16[8,16,512]{2,1,0:T(8,128)(2,1)}), bf16[8,16,512]{2,1,0:T(8,128)(2,1)S(1)}, u32[]{:S(2)}, u32[]{:S(2)}) async-start(bf16[8,16,512]{2,1,0:T(8,128)(2,1)} %reshape.102), calls=%async_computation.2 | async-start | bytes 262144 | tf_op jit(solution)/shard_map/all_to_all | solution.py:60
  21.2 13.4 %all-gather = s32[1,512]{1,0:T(1,128)S(1)} all-gather(s32[1,128]{1,0:T(1,128)S(1)} %copy-done.2), channel_id=2, replica_groups=mesh['dp'=8,'ctx'=4] {'ctx'}, dimensions={1}, use_global_device_ids=true | all-gather | bytes 2560 | tf_op jit(solution)/shard_map/all_gather | solution.py:114
  34.8 4.2 %all-to-all-start.1 = ((bf16[8,16,4096]{2,1,0:T(8,128)(2,1)}), bf16[8,16,4096]{2,1,0:T(8,128)(2,1)S(1)}, u32[]{:S(2)}, u32[]{:S(2)}) async-start(bf16[8,16,4096]{2,1,0:T(8,128)(2,1)} %reshape.100), calls=%async_computation.1 | async-start | bytes 2097152 | tf_op jit(solution)/shard_map/all_to_all | solution.py:58
  40.1 16.2 %all_gather.10 = bf16[512,512]{0,1:T(8,128)(2,1)} all-gather(bf16[128,512]{0,1:T(8,128)(2,1)S(1)} %copy.21), channel_id=1, replica_groups=mesh['dp'=8,'ctx'=4] {'ctx'}, dimensions={0}, use_global_device_ids=true | all-gather | bytes 655360 | tf_op jit(solution)/shard_map/all_gather | solution.py:112
  56.2 14.8 %all_gather.11 = bf16[512,512]{0,1:T(8,128)(2,1)} all-gather(bf16[128,512]{0,1:T(8,128)(2,1)S(1)} %copy.22), channel_id=1, replica_groups=mesh['dp'=8,'ctx'=4] {'ctx'}, dimensions={0}, use_global_device_ids=true | all-gather | bytes 655360 | tf_op jit(solution)/shard_map/all_gather | solution.py:113
  73.0 23.0 %while.18 = (s32[]{:T(128)}, f32[4,8,128]{2,1,0:T(8,128)S(1)}, f32[4,8,128]{2,1,0:T(8,128)S(1)}, f32[128,4,8,128]{0,3,2,1:T(8,128)}, s32[1,128]{1,0:T(1,128)S(1)...) while((s32[]{:T(128)}, f32[4,8,128]{2,1,0:T(8,128)S(1)}, ...), condition=%wide.region_6.7_spmd.clone, body=%wide.region_3.6_spmd.clone.sunk | while | flops 276898048 | bytes 12652751 | solution.py:127
  73.2 1.0 constant_dynamic-slice_fusion.4
  74.8 2.2 %bitcast_add_fusion.3 = f32[128,4,8,128]{0,3,2,1:T(8,128)} fusion(f32[128,4,8,128]{0,3,2,1:T(8,128)} %get-tuple-element.362, bf16[128,4,128,1]{0,2,3,1:T(8,128)(2,1)S(1)} %bitcast.82, f32[4,128,128,8]{2,1,3,0:T(8,128)S(1)} %get-tuple-element.342, f32[128,4,8]{0,2,1:T(8,128)S(1)} %get-tuple-element.344, f32[4,8,128]{2,1,0:T(8,128)S(1)} %get-tuple-element.374, ...), kind=kOutput, calls=%fused_computation.1.clone.1 | convolution fusion | flops 138412032 | bytes 6471681 | tf_op jit(solution)/shard_map/while/body/eval_jaxpr/gjqk,kgd->qgjd/dot_general | solution.py:98
  76.9 0.6 fusion.49
  77.8 1.0 constant_dynamic-slice_fusion.4
  79.3 3.8 %bitcast_add_fusion.3 = f32[128,4,8,128]{0,3,2,1:T(8,128)} fusion(f32[128,4,8,128]{0,3,2,1:T(8,128)} %get-tuple-element.362, bf16[128,4,128,1]{0,2,3,1:T(8,128)(2,1)S(1)} %bitcast.82, f32[4,128,128,8]{2,1,3,0:T(8,128)S(1)} %get-tuple-element.342, f32[128,4,8]{0,2,1:T(8,128)S(1)} %get-tuple-element.344, f32[4,8,128]{2,1,0:T(8,128)S(1)} %get-tuple-element.374, ...), kind=kOutput, calls=%fused_computation.1.clone.1 | convolution fusion | flops 138412032 | bytes 6471681 | tf_op jit(solution)/shard_map/while/body/eval_jaxpr/gjqk,kgd->qgjd/dot_general | solution.py:98
  83.1 0.6 fusion.49
  83.9 1.0 constant_dynamic-slice_fusion.4
  85.4 3.8 %bitcast_add_fusion.3 = f32[128,4,8,128]{0,3,2,1:T(8,128)} fusion(f32[128,4,8,128]{0,3,2,1:T(8,128)} %get-tuple-element.362, bf16[128,4,128,1]{0,2,3,1:T(8,128)(2,1)S(1)} %bitcast.82, f32[4,128,128,8]{2,1,3,0:T(8,128)S(1)} %get-tuple-element.342, f32[128,4,8]{0,2,1:T(8,128)S(1)} %get-tuple-element.344, f32[4,8,128]{2,1,0:T(8,128)S(1)} %get-tuple-element.374, ...), kind=kOutput, calls=%fused_computation.1.clone.1 | convolution fusion | flops 138412032 | bytes 6471681 | tf_op jit(solution)/shard_map/while/body/eval_jaxpr/gjqk,kgd->qgjd/dot_general | solution.py:98
  89.2 0.6 fusion.49
  90.0 1.0 constant_dynamic-slice_fusion.4
  91.6 3.8 %bitcast_add_fusion.3 = f32[128,4,8,128]{0,3,2,1:T(8,128)} fusion(f32[128,4,8,128]{0,3,2,1:T(8,128)} %get-tuple-element.362, bf16[128,4,128,1]{0,2,3,1:T(8,128)(2,1)S(1)} %bitcast.82, f32[4,128,128,8]{2,1,3,0:T(8,128)S(1)} %get-tuple-element.342, f32[128,4,8]{0,2,1:T(8,128)S(1)} %get-tuple-element.344, f32[4,8,128]{2,1,0:T(8,128)S(1)} %get-tuple-element.374, ...), kind=kOutput, calls=%fused_computation.1.clone.1 | convolution fusion | flops 138412032 | bytes 6471681 | tf_op jit(solution)/shard_map/while/body/eval_jaxpr/gjqk,kgd->qgjd/dot_general | solution.py:98
  96.0 1.9 %divide_convert_fusion = bf16[128,4,8,128]{0,3,2,1:T(8,128)(2,1)S(1)} fusion(f32[128,4,8,128]{0,3,2,1:T(8,128)} %get-tuple-element.172, f32[128,4,8]{0,2,1:T(8,128)S(1)} %bitcast.86), kind=kLoop, calls=%fused_computation.32 | loop fusion | flops 1048576 | bytes 3162112 | tf_op jit(solution)/shard_map/convert_element_type | solution.py:131
  97.8 1.3 copy.28
  99.1 1.1 compare_select_fusion
  100.4 38.9 %psum.7 = f32[512]{0:T(512)} all-reduce(f32[512]{0:T(512)S(1)} %select_reduce_fusion), channel_id=1, replica_groups=mesh['dp'=8,'ctx'=4] {'dp','ctx'}, use_global_device_ids=true, to_apply=%region_9.10 | all-reduce | flops 512 | bytes 4096 | tf_op jit(solution)/shard_map/psum | solution.py:144
  (69 shorter events, 7.7 us)
Async XLA Ops:
  0.6 98.5 %copy-start = (f32[4096]{0:T(1024)S(1)}, f32[4096]{0:T(1024)}, u32[]{:S(2)}) copy-start(f32[4096]{0:T(1024)} %param.15) | copy-start | bytes 49156
  4.0 13.0 %all-to-all-start = ((bf16[8,16,512]{2,1,0:T(8,128)(2,1)}), bf16[8,16,512]{2,1,0:T(8,128)(2,1)S(1)}, u32[]{:S(2)}, u32[]{:S(2)}) async-start(bf16[8,16,512]{2,1,0:T(8,128)(2,1)} %reshape.97), calls=%async_computation | async-start | bytes 262144 | tf_op jit(solution)/shard_map/all_to_all | solution.py:59
  9.8 89.3 %collective-permute-start = (s32[1]{0:T(128)}, s32[1]{0:T(128)}, u32[]{:S(2)}, u32[]{:S(2)}) collective-permute-start(s32[1]{0:T(128)} %bitcast.9), channel_id=1, source_target_pairs={{1,0},{2,1},{3,2},{5,4},{6,5},{7,6},{9,8},{10,9},{11,10},{13,12},{... | collective-permute-start | bytes 20 | tf_op jit(solution)/shard_map/ppermute | solution.py:22
  12.5 2.0 %copy-start.1 = (bf16[1,128,512]{2,1,0:T(8,128)(2,1)S(1)}, bf16[1,128,512]{2,1,0:T(8,128)(2,1)}, u32[]{:S(2)}) copy-start(bf16[1,128,512]{2,1,0:T(8,128)(2,1)} %param.11) | copy-start | bytes 393220
  14.6 6.7 %copy-start.2 = (s32[1,128]{1,0:T(1,128)S(1)}, s32[1,128]{1,0:T(1,128)}, u32[]{:S(2)}) copy-start(s32[1,128]{1,0:T(1,128)} %param.13) | copy-start | bytes 1540
  14.6 20.1 %copy-start.3 = (s32[8,16]{1,0:T(8,128)S(1)}, s32[8,16]{1,0:T(8,128)}, u32[]{:S(2)}) copy-start(s32[8,16]{1,0:T(8,128)} %param.12) | copy-start | bytes 1540
  14.9 24.1 %copy-start.4 = (s32[1,16]{1,0:T(1,128)S(1)}, s32[1,16]{1,0:T(1,128)}, u32[]{:S(2)}) copy-start(s32[1,16]{1,0:T(1,128)} %param.14) | copy-start | bytes 196
  17.0 17.7 %all-to-all-start.2 = ((bf16[8,16,512]{2,1,0:T(8,128)(2,1)}), bf16[8,16,512]{2,1,0:T(8,128)(2,1)S(1)}, u32[]{:S(2)}, u32[]{:S(2)}) async-start(bf16[8,16,512]{2,1,0:T(8,128)(2,1)} %reshape.102), calls=%async_computation.2 | async-start | bytes 262144 | tf_op jit(solution)/shard_map/all_to_all | solution.py:60
  34.8 36.3 %all-to-all-start.1 = ((bf16[8,16,4096]{2,1,0:T(8,128)(2,1)}), bf16[8,16,4096]{2,1,0:T(8,128)(2,1)S(1)}, u32[]{:S(2)}, u32[]{:S(2)}) async-start(bf16[8,16,4096]{2,1,0:T(8,128)(2,1)} %reshape.100), calls=%async_computation.1 | async-start | bytes 2097152 | tf_op jit(solution)/shard_map/all_to_all | solution.py:58
where the time goes:
time: 140 us; the launch traced here: 139 us
  blocking collectives  83.3 us (60%)
  matrix products  18.4 us (13%)
  starting transfers between devices  14.9 us (11%)
  local copies, waits for them, and re-layouts  13.7 us (10%)
  other arithmetic  7.23 us (5%)
  between operations  1.54 us (1%)
    psum x1, blocking collectives, local(): histogram = lax.psum(local_hist, ('dp', 'ctx'))  38.9 us
    all_gather x1, blocking collectives, local(): key_rows = lax.all_gather(packed_keys, 'ctx', axis=0, tiled=True)  16.2 us
    all_gather x1, blocking collectives, local(): value_rows = lax.all_gather(packed_values, 'ctx', axis=0, tiled=True)  14.8 us
    dot_general x4, matrix products, attend_block(): jnp.einsum('gjqk,kgd->qgjd', weights.astype(jnp.bfloat16), value_rows.res...  13.5 us
    all_gather x1, blocking collectives, local(): key_segments = lax.all_gather(seg_local, 'ctx', axis=0, tiled=True)  13.4 us
    all_to_all x1, starting transfers between devices, local(): lax.all_to_all(send_keys, 'dp', split_axis=0, concat_axis=0, tiled=True)  5.17 us
    all_to_all x1, starting transfers between devices, local(): lax.all_to_all(send_values, 'dp', split_axis=0, concat_axis=0, tiled=True)  4.21 us
    all_to_all x1, starting transfers between devices, local(): lax.all_to_all(send_query, 'dp', split_axis=0, concat_axis=0, tiled=True)  4.19 us
  transfers between devices with their start and end apart: 4, of which 0 were waited for; matrix products, arithmetic and copies ran while one was open for 25% of the time, Pallas kernels for 0%

commit v1 on v0

v1 whole, which is shorter than its diff:
```python
import math

import jax
import jax.numpy as jnp
from jax import lax
from jax.experimental import pallas as pl
from jax.experimental.pallas import tpu as pltpu
from jax.sharding import PartitionSpec as P

HQ = 32
HK = 4
HD = 128
GROUP = HQ // HK
BLK = 8
SEGS = 16
BINS = 512
NEG = -1e30
VMEM_BYTES = 40 * 1024 * 1024


def send_slots(dest_ref, count_ref, row, block_count, cap, visit):
    def clear(index, _):
        count_ref[index] = 0
        return 0

    lax.fori_loop(0, dest_ref.shape[0], clear, 0)

    def step(block, _):
        target = dest_ref[row, block]
        rank = count_ref[target]
        count_ref[target] = rank + 1
        visit(block, target * cap + rank)
        return 0

    lax.fori_loop(0, block_count, step, 0)


def sort_kv_kernel(cap, dest_ref, key_ref, value_ref, out_ref, count_ref):
    block_count, _, width = key_ref.shape

    def visit(block, slot):
        for head in range(HK):
            here = slice(head * HD, (head + 1) * HD)
            out_ref[slot, :, 2 * head * HD : (2 * head + 1) * HD] = key_ref[block, :, here]
            out_ref[slot, :, (2 * head + 1) * HD : (2 * head + 2) * HD] = value_ref[block, :, here]

    send_slots(dest_ref, count_ref, lax.axis_index("dp"), block_count, cap, visit)


def sort_query_kernel(cap, dest_ref, query_ref, out_ref, count_ref, sem):
    block_count = query_ref.shape[0]

    def visit(block, slot):
        pltpu.make_async_copy(query_ref.at[block], out_ref.at[slot], sem).start()

    send_slots(dest_ref, count_ref, lax.axis_index("dp"), block_count, cap, visit)
    pltpu.make_async_copy(query_ref, out_ref, sem).wait()


def find_slots(dest_ref, slot_ref, cap):
    dp_count, block_count = dest_ref.shape
    me = lax.axis_index("dp")

    def source(src, _):
        def column(block, rank):
            hit = dest_ref[src, block] == me

            @pl.when(hit)
            def _():
                slot_ref[block] = src * cap + rank

            return rank + jnp.where(hit, 1, 0)

        lax.fori_loop(0, block_count, column, 0)
        return 0

    lax.fori_loop(0, dp_count, source, 0)


def unsort_kv_kernel(cap, dest_ref, seg_ref, got_ref, out_ref, slot_ref):
    find_slots(dest_ref, slot_ref, cap)
    block_count = got_ref.shape[0]
    row_count = block_count * BLK
    for pair in range(block_count // 2):
        rows = jnp.concatenate([got_ref[slot_ref[2 * pair]], got_ref[slot_ref[2 * pair + 1]]], axis=0)
        out_ref[2 * BLK * pair : 2 * BLK * (pair + 1), :] = rows
    labels = seg_ref[...].astype(jnp.float32)
    labels = jnp.concatenate([labels] * (out_ref.shape[1] // row_count), axis=1)
    labels = jnp.broadcast_to(labels, (2 * BLK, out_ref.shape[1]))
    out_ref[row_count:, :] = labels.astype(out_ref.dtype)


def attend_kernel(
    cap,
    part_count,
    dest_ref,
    bins_ref,
    next_ref,
    seg_ref,
    weight_ref,
    query_ref,
    *rest,
):
    part_refs = rest[:part_count]
    out_ref, hist_ref = rest[part_count : part_count + 2]
    slot_ref, bias_ref, key_ref, value_ref, reward_ref = rest[part_count + 2 :]
    step = pl.program_id(0)
    row_count = out_ref.shape[0]
    block_count = row_count // BLK
    ctx_self = lax.axis_index("ctx")
    seg_row = seg_ref[...]
    seg_col = jnp.transpose(jnp.broadcast_to(seg_row, (row_count, row_count)))

    @pl.when(step == 0)
    def _():
        find_slots(dest_ref, slot_ref, cap)
        reward_ref[...] = jnp.zeros_like(reward_ref)
        q_pos = lax.broadcasted_iota(jnp.int32, (row_count, row_count), 0)
        k_pos = lax.broadcasted_iota(jnp.int32, (row_count, row_count), 1)
        own = (seg_col == seg_row) & (k_pos <= q_pos)
        bias_ref[:, :row_count] = jnp.where(own, 0.0, NEG)
        for hop in range(1, part_count):
            labels = part_refs[hop][row_count : row_count + 1, :row_count].astype(jnp.float32)
            there = (seg_col.astype(jnp.float32) == labels) & (ctx_self >= hop)
            bias_ref[:, hop * row_count : (hop + 1) * row_count] = jnp.where(there, 0.0, NEG)

    first = pl.multiple_of(step * 2 * HD, 2 * HD)
    for part in range(part_count):
        rows = slice(part * row_count, (part + 1) * row_count)
        key_ref[rows, :] = part_refs[part][:row_count, pl.ds(first, HD)]
        value_ref[rows, :] = part_refs[part][:row_count, pl.ds(first + HD, HD)]
    keys = key_ref[...]
    values = value_ref[...]
    query = jnp.concatenate([query_ref[slot_ref[block]] for block in range(block_count)], axis=0)
    factor = math.log2(math.e) / math.sqrt(HD)
    reward = reward_ref[...]
    for head in range(GROUP):
        here = slice(head * HD, (head + 1) * HD)
        scores = lax.dot_general(
            query[:, here], keys, (((1,), (1,)), ((), ())), preferred_element_type=jnp.float32
        )
        scores = scores + bias_ref[...]
        top = jnp.max(scores, axis=1, keepdims=True)
        weights = jnp.exp2((scores - top) * factor)
        total = jnp.sum(weights, axis=1, keepdims=True)
        mixed = jnp.dot(weights.astype(jnp.bfloat16), values, preferred_element_type=jnp.float32)
        attended = (mixed / total).astype(jnp.bfloat16)
        out_ref[:, here] = attended
        reward = reward + attended.astype(jnp.float32) * weight_ref[:, here]
    reward_ref[...] = reward

    @pl.when(step == HK - 1)
    def _():
        after = jnp.concatenate([seg_row[:, 1:], jnp.full((1, 1), next_ref[0], jnp.int32)], axis=1)
        after_col = jnp.transpose(jnp.broadcast_to(after, (row_count, row_count)))
        row_reward = jnp.sum(reward_ref[...], axis=1, keepdims=True)
        kept = jnp.where(seg_col != after_col, row_reward, 0.0)
        label = lax.broadcasted_iota(jnp.int32, (row_count, row_count), 1)
        by_seg = jnp.sum(jnp.where(seg_col == label, kept, 0.0), axis=0, keepdims=True)
        bin_id = lax.broadcasted_iota(jnp.int32, (1, BINS), 1)
        hist = jnp.zeros((1, BINS), jnp.float32)
        for seg in range(SEGS):
            hist = hist + jnp.where(bin_id == bins_ref[0, seg], by_seg[:, seg : seg + 1], 0.0)
        hist_ref[...] = jnp.broadcast_to(hist, hist_ref.shape)


def local(roll_query, roll_keys, roll_values, pack_dest, segment_ids, reward_bins, reward_weight):
    dp_count = lax.axis_size("dp")
    ctx_count = lax.axis_size("ctx")
    ctx_self = lax.axis_index("ctx")
    row_count = roll_query.shape[1]
    q_width = roll_query.shape[2]
    kv_width = roll_keys.shape[2]
    block_count = row_count // BLK
    cap = (block_count + dp_count - 1) // dp_count
    slot_count = dp_count * cap
    reach = row_count * ctx_count // 2
    hop_count = min(ctx_count - 1, (reach - 1 + row_count - 1) // row_count)
    smem = pl.BlockSpec(memory_space=pltpu.SMEM)
    vmem = pl.BlockSpec(memory_space=pltpu.VMEM)
    hbm = pl.BlockSpec(memory_space=pl.ANY)
    params = pltpu.CompilerParams(vmem_limit_bytes=VMEM_BYTES)

    sorted_kv = pl.pallas_call(
        lambda *refs: sort_kv_kernel(cap, *refs),
        out_shape=jax.ShapeDtypeStruct((slot_count, BLK, 2 * kv_width), jnp.bfloat16),
        in_specs=[smem, vmem, vmem],
        out_specs=vmem,
        scratch_shapes=[pltpu.SMEM((dp_count,), jnp.int32)],
        compiler_params=params,
        name="sort_kv",
    )(
        pack_dest,
        roll_keys.reshape(block_count, BLK, kv_width),
        roll_values.reshape(block_count, BLK, kv_width),
    )
    got_kv = lax.all_to_all(
        sorted_kv.reshape(dp_count, cap * BLK, 2 * kv_width), "dp", split_axis=0, concat_axis=0, tiled=True
    ).reshape(slot_count, BLK, 2 * kv_width)

    sorted_query = pl.pallas_call(
        lambda *refs: sort_query_kernel(cap, *refs),
        out_shape=jax.ShapeDtypeStruct((slot_count, BLK, q_width), jnp.bfloat16),
        in_specs=[smem, hbm],
        out_specs=hbm,
        scratch_shapes=[pltpu.SMEM((dp_count,), jnp.int32), pltpu.SemaphoreType.DMA],
        compiler_params=params,
        name="sort_query",
    )(pack_dest, roll_query.reshape(block_count, BLK, q_width))
    got_query = lax.all_to_all(
        sorted_query.reshape(dp_count, cap * BLK, q_width), "dp", split_axis=0, concat_axis=0, tiled=True
    ).reshape(slot_count, BLK, q_width)

    parts = [
        pl.pallas_call(
            lambda *refs: unsort_kv_kernel(cap, *refs),
            out_shape=jax.ShapeDtypeStruct((row_count + 2 * BLK, 2 * kv_width), jnp.bfloat16),
            in_specs=[smem, vmem, vmem],
            out_specs=vmem,
            scratch_shapes=[pltpu.SMEM((block_count,), jnp.int32)],
            compiler_params=params,
            name="unsort_kv",
        )(pack_dest, segment_ids, got_kv)
    ]
    forward = [(i, i + 1) for i in range(ctx_count - 1)]
    for _ in range(hop_count):
        parts.append(lax.ppermute(parts[-1], "ctx", forward))
    backward = [(i + 1, i) for i in range(ctx_count - 1)]
    next_first = lax.ppermute(segment_ids[0, :1] + 1, "ctx", backward) - 1

    part_count = len(parts)
    part_spec = pl.BlockSpec((row_count + 2 * BLK, 2 * kv_width), lambda g: (0, 0))
    device_count = dp_count * ctx_count
    attended, hist_rows = pl.pallas_call(
        lambda *refs: attend_kernel(cap, part_count, *refs),
        grid=(HK,),
        out_shape=(
            jax.ShapeDtypeStruct((row_count, q_width), jnp.bfloat16),
            jax.ShapeDtypeStruct((device_count, BINS), jnp.float32),
        ),
        in_specs=[
            smem,
            smem,
            smem,
            pl.BlockSpec((1, row_count), lambda g: (0, 0)),
            pl.BlockSpec((1, GROUP * HD), lambda g: (0, g)),
            pl.BlockSpec((slot_count, BLK, GROUP * HD), lambda g: (0, 0, g)),
        ]
        + [part_spec] * part_count,
        out_specs=(
            pl.BlockSpec((row_count, GROUP * HD), lambda g: (0, g)),
            pl.BlockSpec((device_count, BINS), lambda g: (0, 0)),
        ),
        scratch_shapes=[
            pltpu.SMEM((block_count,), jnp.int32),
            pltpu.VMEM((row_count, part_count * row_count), jnp.float32),
            pltpu.VMEM((part_count * row_count, HD), jnp.bfloat16),
            pltpu.VMEM((part_count * row_count, HD), jnp.bfloat16),
            pltpu.VMEM((row_count, HD), jnp.float32),
        ],
        compiler_params=params,
        name="attend",
    )(pack_dest, reward_bins, next_first, segment_ids, reward_weight.reshape(1, q_width), got_query, *parts)
    gathered = lax.all_to_all(hist_rows, ("dp", "ctx"), split_axis=0, concat_axis=0, tiled=True)
    return attended.reshape(1, row_count, q_width), jnp.sum(gathered, axis=0)


def solution(mesh):
    in_specs = (
        P("dp", "ctx", None),
        P("dp", "ctx", None),
        P("dp", "ctx", None),
        P(None, "ctx"),
        P("dp", "ctx"),
        P("dp", None),
        P(),
    )
    out_specs = (P("dp", "ctx", None), P())
    return jax.shard_map(local, mesh=mesh, in_specs=in_specs, out_specs=out_specs, check_vma=False)
```

time: 140 us -> 71.8 us (0.51)
  blocking collectives: 83.3 us -> 13.7 us
  matrix products: 18.4 us -> 0 us
  Pallas kernels: 0 us -> 17.2 us
  waiting for transfers between devices: 0.01 us -> 16.4 us
  local copies, waits for them, and re-layouts: 13.7 us -> 3.95 us
  other arithmetic: 7.23 us -> 0.64 us
  starting transfers between devices: 14.9 us -> 18 us
    all_gather x3 -> x0, blocking collectives: 44.4 us -> none  [the longest x1 16.2 us: local(): key_rows = lax.all_gather(packed_keys, 'ctx', axis=0, tiled=True)]
    psum x1 -> x0, blocking collectives: 38.9 us -> none  [local(): histogram = lax.psum(local_hist, ('dp', 'ctx'))]
    dot_general x15 -> x0, matrix products: 18.4 us -> none  [the longest x4 13.5 us: attend_block(): jnp.einsum('gjqk,kgd->qgjd', weights.astype(jnp.bfloat16), value_rows.res...]
    pallas_call x0 -> x4, Pallas kernels: none -> 17.2 us  [the longest x1 12.3 us: local(): pl.pallas_call(lambda *refs: attend_kernel(cap, part_count, *refs), grid=...]
    all_to_all x0 -> x1, blocking collectives: none -> 13.7 us  [local(): lax.all_to_all(hist_rows, ('dp', 'ctx'), split_axis=0, concat_axis=0, til...]
    ppermute x1 -> x3, waiting for transfers between devices: 0.01 us -> 11.1 us  [the longest x2 6.83 us: local(): parts.append(lax.ppermute(parts[-1], 'ctx', forward))]
    ppermute x1 -> x3, starting transfers between devices: 1.29 us -> 9.18 us  [the longest x2 7.89 us: local(): parts.append(lax.ppermute(parts[-1], 'ctx', forward))]
    all_to_all x3 -> x2, waiting for transfers between devices: 0.01 us -> 5.3 us  [the longest x1 5.29 us: local(): lax.all_to_all(sorted_kv.reshape(dp_count, cap * BLK, 2 * kv_width), 'dp'...]
  transfers between devices with their start and end apart: 4 -> 5, of which waited for: 0 -> 3; matrix products, arithmetic and copies ran while one was open for 25% -> 0% of each run, Pallas kernels for 0% -> 5%
where the time goes in v1:
time: 71.8 us; the launch traced here: 71.3 us
  starting transfers between devices  18 us (25%)
  Pallas kernels  17.2 us (24%)
  waiting for transfers between devices  16.4 us (23%)
  blocking collectives  13.7 us (19%)
  local copies, waits for them, and re-layouts  3.95 us (6%)
  between operations  1.36 us (2%)
    all_to_all x1, blocking collectives, local(): lax.all_to_all(hist_rows, ('dp', 'ctx'), split_axis=0, concat_axis=0, til...  13.7 us
    pallas_call x1, Pallas kernels, local(): pl.pallas_call(lambda *refs: attend_kernel(cap, part_count, *refs), grid=...  12.3 us
    ppermute x2, starting transfers between devices, local(): parts.append(lax.ppermute(parts[-1], 'ctx', forward))  7.89 us
    ppermute x2, waiting for transfers between devices, local(): parts.append(lax.ppermute(parts[-1], 'ctx', forward))  6.83 us
    all_to_all x1, starting transfers between devices, local(): lax.all_to_all(sorted_kv.reshape(dp_count, cap * BLK, 2 * kv_width), 'dp'...  5.3 us
    all_to_all x1, waiting for transfers between devices, local(): lax.all_to_all(sorted_kv.reshape(dp_count, cap * BLK, 2 * kv_width), 'dp'...  5.29 us
    ppermute x1, waiting for transfers between devices, local(): next_first = lax.ppermute(segment_ids[0, :1] + 1, 'ctx', backward) - 1  4.24 us
    unnamed x16, local copies, waits for them, and re-layouts  3.88 us
  transfers between devices with their start and end apart: 5, of which 3 were waited for; matrix products, arithmetic and copies ran while one was open for 0% of the time, Pallas kernels for 5%

profile of v1, /device:TPU:0, one launch (start us, length us, event | category | flops | bytes accessed | tf_op | source)
XLA Modules:
  0.0 71.3 jit_solution(14528260489264213038)
XLA Ops:
  0.6 0.0 copy-start
  0.6 0.0 copy-start.1
  0.6 1.0 %copy-done.1 = bf16[1,128,512]{2,1,0:T(8,128)(2,1)S(1)} copy-done((bf16[1,128,512]{2,1,0:T(8,128)(2,1)S(1)}, bf16[1,128,512]{2,1,0:T(8,128)(2,1)}, u32[]{:S(2)}) %copy-start.1) | copy-done | bytes 131096
  1.6 0.0 copy-start.2
  1.6 0.9 %copy-done.2 = bf16[1,128,512]{2,1,0:T(8,128)(2,1)S(1)} copy-done((bf16[1,128,512]{2,1,0:T(8,128)(2,1)S(1)}, bf16[1,128,512]{2,1,0:T(8,128)(2,1)}, u32[]{:S(2)}) %copy-start.2) | copy-done | bytes 131096
  2.5 0.0 copy-start.3
  2.5 0.7 copy-done.3
  3.2 1.6 %sort_kv.1 = bf16[16,8,1024]{2,1,0:T(8,128)(2,1)} custom-call(s32[8,16]{1,0:T(8,128)S(1)} %copy-done.3, bf16[16,8,512]{2,1,0:T(8,128)(2,1)S(1)} %bitcast.15, bf16[16,8,512]{2,1,0:T(8,128)(2,1)S(1)} %bitcast.16), custom_call_target="tpu_custom_call" | custom-call | tf_op jit(solution)/shard_map/sort_kv/pallas_call | solution.py:184
  4.8 0.0 copy-start.4
  4.8 5.3 %all-to-all-start.1 = ((bf16[8,16,1024]{2,1,0:T(8,128)(2,1)}), bf16[8,16,1024]{2,1,0:T(8,128)(2,1)S(1)}, u32[]{:S(2)}, u32[]{:S(2)}) async-start(bf16[8,16,1024]{2,1,0:T(8,128)(2,1)} %bitcast.7), calls=%async_computation.1 | async-start | bytes 524288 | tf_op jit(solution)/shard_map/all_to_all | solution.py:197
  10.1 0.0 copy-done
  10.1 0.0 copy-done.4
  10.1 1.6 %sort_query.1 = bf16[16,8,4096]{2,1,0:T(8,128)(2,1)} custom-call(s32[8,16]{1,0:T(8,128)S(1)} %copy-done.4, bf16[16,8,4096]{2,1,0:T(8,128)(2,1)S(1)} %bitcast.14), custom_call_target="tpu_custom_call" | custom-call | tf_op jit(solution)/shard_map/sort_query/pallas_call | solution.py:201
  11.7 5.3 %all-to-all-done.1 = bf16[8,16,1024]{2,1,0:T(8,128)(2,1)S(1)} async-done(((bf16[8,16,1024]{2,1,0:T(8,128)(2,1)}), bf16[8,16,1024]{2,1,0:T(8,128)(2,1)S(1)}, u32[]{:S(2)}, u32[]{:S(2)}) %all-to-all-start.1) | async-done | bytes 262176 | tf_op jit(solution)/shard_map/all_to_all | solution.py:197
  17.0 3.6 %all-to-all-start = ((bf16[8,16,4096]{2,1,0:T(8,128)(2,1)}), bf16[8,16,4096]{2,1,0:T(8,128)(2,1)S(1)}, u32[]{:S(2)}, u32[]{:S(2)}) async-start(bf16[8,16,4096]{2,1,0:T(8,128)(2,1)} %bitcast.3), calls=%async_computation | async-start | bytes 2097152 | tf_op jit(solution)/shard_map/all_to_all | solution.py:210
  20.6 0.0 copy-start.6
  20.6 0.6 copy-done.6
  21.3 1.8 %unsort_kv.1.refs_6_ = bf16[144,1024]{1,0:T(8,128)(2,1)S(1)} custom-call(s32[8,16]{1,0:T(8,128)S(1)} %copy-done.4, s32[1,128]{1,0:T(1,128)S(1)} %copy-done.6, bf16[16,8,1024]{2,1,0:T(8,128)(2,1)S(1)} %bitcast.13), custom_call_target="tpu_custom_call" | custom-call | tf_op jit(solution)/shard_map/unsort_kv/pallas_call | solution.py:215
  23.0 3.5 %collective-permute-start.1 = (bf16[144,1024]{1,0:T(8,128)(2,1)S(1)}, bf16[144,1024]{1,0:T(8,128)(2,1)S(1)}, u32[]{:S(2)}, u32[]{:S(2)}) collective-permute-start(bf16[144,1024]{1,0:T(8,128)(2,1)S(1)} %unsort_kv.1.refs_6_), channel_id=1, source_target_pairs={{0,1},{1,2},{2,3},{4,5},{5,6},{6,7},{8,9},{9,10},{10,11},{12,13},{... | collective-permute-start | bytes 884744 | tf_op jit(solution)/shard_map/ppermute | solution.py:227
  26.5 6.8 %collective-permute-done.1.refs_7_ = bf16[144,1024]{1,0:T(8,128)(2,1)S(1)} collective-permute-done((bf16[144,1024]{1,0:T(8,128)(2,1)S(1)}, bf16[144,1024]{1,0:T(8,128)(2,1)S(1)}, u32[]{:S(2)}, u32[]{:S(2)}) %collective-permute-start.1) | collective-permute-done | bytes 294944 | tf_op jit(solution)/shard_map/ppermute | solution.py:227
  33.4 4.4 %collective-permute-start.2 = (bf16[144,1024]{1,0:T(8,128)(2,1)S(1)}, bf16[144,1024]{1,0:T(8,128)(2,1)S(1)}, u32[]{:S(2)}, u32[]{:S(2)}) collective-permute-start(bf16[144,1024]{1,0:T(8,128)(2,1)S(1)} %collective-permute-done.1.refs_7_), channel_id=1, source_target_pairs={{0,1},{1,2},{2,3},{4,5},{5,6},{6,7},{8,9},{9,10},{10,11},{12,13},{... | collective-permute-start | bytes 884744 | tf_op jit(solution)/shard_map/ppermute | solution.py:227
  37.8 1.3 %collective-permute-start = (s32[1]{0:T(128)}, s32[1]{0:T(128)}, u32[]{:S(2)}, u32[]{:S(2)}) collective-permute-start(s32[1]{0:T(128)} %bitcast), channel_id=1, source_target_pairs={{1,0},{2,1},{3,2},{5,4},{6,5},{7,6},{9,8},{10,9},{11,10},{13,12},{... | collective-permute-start | bytes 20 | tf_op jit(solution)/shard_map/ppermute | solution.py:229
  39.1 4.2 %collective-permute-done = s32[1]{0:T(128)} collective-permute-done((s32[1]{0:T(128)}, s32[1]{0:T(128)}, u32[]{:S(2)}, u32[]{:S(2)}) %collective-permute-start) | collective-permute-done | bytes 36 | tf_op jit(solution)/shard_map/ppermute | solution.py:229
  43.9 0.0 collective-permute-done.2.refs_8_
  43.9 0.0 all-to-all-done
  43.9 0.0 copy-start.7
  43.9 0.0 copy-done.5
  43.9 0.6 copy-done.7
  44.6 12.3 %attend.1 = (bf16[128,4096]{1,0:T(8,128)(2,1)}, f32[32,512]{1,0:T(8,128)S(1)}) custom-call(s32[8,16]{1,0:T(8,128)S(1)} %copy-done.4, s32[1,16]{1,0:T(1,128)S(1)} %copy-done.7, s32[1]{0:T(128)S(6)} %sub.3.refs_2_, s32[1,128]{1,0:T(1,128)S(1)} %copy-done.6, f32[1,4096]{1,0:T(1,128)S(1)} %bitcast.18, bf16[16,8,4096]{2,1,0:T(8,128)(2,1)S(1)} %bitcast.12, ...), custom_call_target="tpu_custom_call" | custom-call | tf_op jit(solution)/shard_map/attend/pallas_call | solution.py:234
  56.8 0.1 copy.9
  56.9 13.7 %all_to_all.19 = f32[32,1,512]{2,1,0:T(1,128)S(1)} all-to-all(f32[32,1,512]{2,1,0:T(1,128)S(1)} %copy.9), channel_id=1, replica_groups=mesh['dp'=8,'ctx'=4] {'dp','ctx'}, dimensions={0} | all-to-all | bytes 131072 | tf_op jit(solution)/shard_map/all_to_all | solution.py:264
  70.7 0.6 reduce_sum.9
  (1 shorter events, 0.0 us)
Async XLA Ops:
  0.6 9.5 %copy-start = (bf16[1,128,4096]{2,1,0:T(8,128)(2,1)S(1)}, bf16[1,128,4096]{2,1,0:T(8,128)(2,1)}, u32[]{:S(2)}) copy-start(bf16[1,128,4096]{2,1,0:T(8,128)(2,1)} %param.7) | copy-start | bytes 3145732
  0.6 1.0 %copy-start.1 = (bf16[1,128,512]{2,1,0:T(8,128)(2,1)S(1)}, bf16[1,128,512]{2,1,0:T(8,128)(2,1)}, u32[]{:S(2)}) copy-start(bf16[1,128,512]{2,1,0:T(8,128)(2,1)} %param.8) | copy-start | bytes 393220
  1.6 0.9 %copy-start.2 = (bf16[1,128,512]{2,1,0:T(8,128)(2,1)S(1)}, bf16[1,128,512]{2,1,0:T(8,128)(2,1)}, u32[]{:S(2)}) copy-start(bf16[1,128,512]{2,1,0:T(8,128)(2,1)} %param.9) | copy-start | bytes 393220
  2.5 0.7 copy-start.3
  4.8 5.3 %copy-start.4 = (s32[8,16]{1,0:T(8,128)S(1)}, s32[8,16]{1,0:T(8,128)}, u32[]{:S(2)}) copy-start(s32[8,16]{1,0:T(8,128)} %refs_0_.7) | copy-start | bytes 1540
  4.8 12.2 %all-to-all-start.1 = ((bf16[8,16,1024]{2,1,0:T(8,128)(2,1)}), bf16[8,16,1024]{2,1,0:T(8,128)(2,1)S(1)}, u32[]{:S(2)}, u32[]{:S(2)}) async-start(bf16[8,16,1024]{2,1,0:T(8,128)(2,1)} %bitcast.7), calls=%async_computation.1 | async-start | bytes 524288 | tf_op jit(solution)/shard_map/all_to_all | solution.py:197
  17.0 26.9 %all-to-all-start = ((bf16[8,16,4096]{2,1,0:T(8,128)(2,1)}), bf16[8,16,4096]{2,1,0:T(8,128)(2,1)S(1)}, u32[]{:S(2)}, u32[]{:S(2)}) async-start(bf16[8,16,4096]{2,1,0:T(8,128)(2,1)} %bitcast.3), calls=%async_computation | async-start | bytes 2097152 | tf_op jit(solution)/shard_map/all_to_all | solution.py:210
  20.6 0.7 copy-start.6
  21.3 22.7 %copy-start.5 = (f32[4096]{0:T(1024)S(1)}, f32[4096]{0:T(1024)}, u32[]{:S(2)}) copy-start(f32[4096]{0:T(1024)} %param.13) | copy-start | bytes 49156
  23.0 10.3 %collective-permute-start.1 = (bf16[144,1024]{1,0:T(8,128)(2,1)S(1)}, bf16[144,1024]{1,0:T(8,128)(2,1)S(1)}, u32[]{:S(2)}, u32[]{:S(2)}) collective-permute-start(bf16[144,1024]{1,0:T(8,128)(2,1)S(1)} %unsort_kv.1.refs_6_), channel_id=1, source_target_pairs={{0,1},{1,2},{2,3},{4,5},{5,6},{6,7},{8,9},{9,10},{10,11},{12,13},{... | collective-permute-start | bytes 884744 | tf_op jit(solution)/shard_map/ppermute | solution.py:227
  33.4 10.5 %collective-permute-start.2 = (bf16[144,1024]{1,0:T(8,128)(2,1)S(1)}, bf16[144,1024]{1,0:T(8,128)(2,1)S(1)}, u32[]{:S(2)}, u32[]{:S(2)}) collective-permute-start(bf16[144,1024]{1,0:T(8,128)(2,1)S(1)} %collective-permute-done.1.refs_7_), channel_id=1, source_target_pairs={{0,1},{1,2},{2,3},{4,5},{5,6},{6,7},{8,9},{9,10},{10,11},{12,13},{... | collective-permute-start | bytes 884744 | tf_op jit(solution)/shard_map/ppermute | solution.py:227
  37.8 5.5 %collective-permute-start = (s32[1]{0:T(128)}, s32[1]{0:T(128)}, u32[]{:S(2)}, u32[]{:S(2)}) collective-permute-start(s32[1]{0:T(128)} %bitcast), channel_id=1, source_target_pairs={{1,0},{2,1},{3,2},{5,4},{6,5},{7,6},{9,8},{10,9},{11,10},{13,12},{... | collective-permute-start | bytes 20 | tf_op jit(solution)/shard_map/ppermute | solution.py:229
  43.9 0.7 copy-start.7

commit v2 on v0

v2 whole, which is shorter than its diff:
```python
import math

import jax
import jax.numpy as jnp
from jax import lax
from jax.experimental import pallas as pl
from jax.experimental.pallas import tpu as pltpu
from jax.sharding import PartitionSpec as P

HQ = 32
HK = 4
HD = 128
GROUP = HQ // HK
BLK = 8
SEGS = 16
BINS = 512
NEG = -1e30
FINISH_HEADS = 2 * GROUP
FACTOR = math.log2(math.e) / math.sqrt(HD)


def params(mebibytes):
    return pltpu.CompilerParams(vmem_limit_bytes=mebibytes * 1024 * 1024)


def cost(flops, nbytes):
    return pl.CostEstimate(flops=flops, bytes_accessed=nbytes, transcendentals=0)


def find_blocks(dest_ref, block_ref, count_ref, cap, relative):
    dp_count, block_count = dest_ref.shape
    me = lax.axis_index("dp")
    for target in range(dp_count):
        count_ref[target] = 0
    for block in range(block_count):
        target = dest_ref[me, block]
        rank = count_ref[target]
        count_ref[target] = rank + 1
        place = (target ^ me) if relative else target
        block_ref[place * cap + rank] = block


def find_columns(dest_ref, column_ref, cap, relative):
    dp_count, block_count = dest_ref.shape
    me = lax.axis_index("dp")

    def source(src, _):
        place = (src ^ me) if relative else src
        rank = 0
        for block in range(block_count):
            hit = dest_ref[src, block] == me

            @pl.when(hit)
            def _():
                column_ref[place * cap + rank] = block

            rank = rank + jnp.where(hit, 1, 0)
        return 0

    lax.fori_loop(0, dp_count, source, 0)


def sort_kv_kernel(cap, dest_hbm, key_hbm, value_hbm, out_ref, *scratch):
    dest_ref, block_ref, count_ref, key_ref, value_ref, stage_ref, in_sem, out_sem = scratch
    arrivals = [
        pltpu.make_async_copy(source, target, in_sem.at[index])
        for index, (source, target) in enumerate(
            ((dest_hbm, dest_ref), (key_hbm, key_ref), (value_hbm, value_ref))
        )
    ]
    for arrival in arrivals:
        arrival.start()
    arrivals[0].wait()
    find_blocks(dest_ref, block_ref, count_ref, cap, False)
    arrivals[1].wait()
    arrivals[2].wait()
    width = key_ref.shape[2]
    for slot in range(out_ref.shape[0]):
        block = block_ref[slot]
        stage_ref[slot, :, :width] = key_ref[block]
        stage_ref[slot, :, width:] = value_ref[block]
    departure = pltpu.make_async_copy(stage_ref, out_ref, out_sem)
    departure.start()
    departure.wait()


def sort_query_kernel(cap, piece_count, dest_ref, query_ref, after_ref, *rest):
    pieces = rest[:piece_count]
    block_ref, count_ref, sem = rest[piece_count:]
    find_blocks(dest_ref, block_ref, count_ref, cap, True)
    copies = []
    for slot in range(2 * piece_count * cap):
        piece, place = divmod(slot, 2 * cap)
        copies.append(
            pltpu.make_async_copy(query_ref.at[block_ref[slot]], pieces[piece].at[place], sem.at[slot])
        )
    for copy in copies:
        copy.start()
    for copy in copies:
        copy.wait()


def merge_kernel(cap, piece_count, *refs):
    pieces, out_ref = refs[:piece_count], refs[piece_count]
    for piece in range(piece_count):
        out_ref[piece * cap : (piece + 1) * cap] = pieces[piece][cap:]


def unsort_query_kernel(cap, piece_count, dest_ref, *rest):
    pieces = rest[:piece_count]
    other_ref, out_ref, column_ref = rest[piece_count:]
    find_columns(dest_ref, column_ref, cap, True)
    for piece in range(piece_count):
        for rank in range(cap):
            out_ref[column_ref[2 * piece * cap + rank]] = pieces[piece][rank]
            out_ref[column_ref[(2 * piece + 1) * cap + rank]] = other_ref[piece * cap + rank]


def unsort_kv_kernel(cap, dest_ref, seg_ref, got_ref, out_ref, column_ref):
    find_columns(dest_ref, column_ref, cap, False)
    block_count = got_ref.shape[0]
    for slot in range(block_count):
        out_ref[column_ref[slot]] = got_ref[slot]
    labels = seg_ref[...].astype(jnp.float32)
    labels = jnp.concatenate([labels] * (out_ref.shape[2] // labels.shape[1]), axis=1)
    out_ref[block_count] = jnp.broadcast_to(labels, out_ref.shape[1:]).astype(out_ref.dtype)


def after_kernel(*refs):
    pass


def rows_of(ref, lane):
    block_count = ref.shape[0] - 1
    return ref[:block_count, :, lane : lane + HD].reshape(block_count * BLK, HD)


def allowed_bias(part_ref, hop, seg_row):
    row_count = seg_row.shape[1]
    square = (row_count, row_count)
    labels = part_ref[part_ref.shape[0] - 1][:1, :row_count].astype(jnp.float32)
    labels = jnp.transpose(jnp.broadcast_to(labels, square))
    allowed = labels == seg_row.astype(jnp.float32)
    if hop == 0:
        key_pos = lax.broadcasted_iota(jnp.int32, square, 0)
        query_pos = lax.broadcasted_iota(jnp.int32, square, 1)
        allowed = allowed & (key_pos <= query_pos)
    else:
        allowed = allowed & (lax.axis_index("ctx") >= hop)
    return jnp.where(allowed, 0.0, NEG)


def score(keys, query_ref, head):
    here = slice(head * HD, (head + 1) * HD)
    query = query_ref[:, :, here].reshape(query_ref.shape[0] * BLK, HD)
    return lax.dot_general(keys, query, (((1,), (1,)), ((), ())), preferred_element_type=jnp.float32)


def begin_kernel(part_count, seg_ref, query_ref, *rest):
    part_refs = rest[:part_count]
    top_ref, total_ref, mixed_ref, bias_ref = rest[part_count:]
    row_count = seg_ref.shape[1]
    for hop in range(part_count):
        bias_ref[hop * row_count : (hop + 1) * row_count, :] = allowed_bias(part_refs[hop], hop, seg_ref[...])
    keys, values = [], []
    for group in range(HK):
        keys.append(jnp.concatenate([rows_of(ref, group * HD) for ref in part_refs], axis=0))
        rows = jnp.concatenate([rows_of(ref, (HK + group) * HD) for ref in part_refs], axis=0)
        values.append(jnp.transpose(rows))
    for first in range(0, HQ, GROUP):
        heads = range(first, first + GROUP)
        scores = [score(keys[head // GROUP], query_ref, head) + bias_ref[...] for head in heads]
        tops = [jnp.max(each, axis=0, keepdims=True) for each in scores]
        weights = [jnp.exp2((each - top) * FACTOR) for each, top in zip(scores, tops)]
        for head, top, each in zip(heads, tops, weights):
            top_ref[head : head + 1, :] = top
            total_ref[head : head + 1, :] = jnp.sum(each, axis=0, keepdims=True)
            mixed_ref[head] = jnp.dot(
                values[head // GROUP], each.astype(jnp.bfloat16), preferred_element_type=jnp.float32
            )


def finish_kernel(hop, bins_ref, seg_ref, weight_ref, query_ref, top_ref, total_ref, mixed_ref, *rest):
    part_ref, out_ref, hist_ref, bias_ref = rest
    row_count = out_ref.shape[0]
    square = (row_count, row_count)
    seg_row = seg_ref[...]
    bias_ref[...] = allowed_bias(part_ref, hop, seg_row)
    reward = jnp.zeros(square, jnp.float32)
    keys = [rows_of(part_ref, group * HD) for group in range(HK)]
    values = [jnp.transpose(rows_of(part_ref, (HK + group) * HD)) for group in range(HK)]
    for first in range(0, HQ, FINISH_HEADS):
        heads = range(first, first + FINISH_HEADS)
        scores = [score(keys[head // GROUP], query_ref, head) + bias_ref[...] for head in heads]
        before = [top_ref[head : head + 1, :] for head in heads]
        tops = [jnp.maximum(old, jnp.max(each, axis=0, keepdims=True)) for old, each in zip(before, scores)]
        weights = [jnp.exp2((each - top) * FACTOR) for each, top in zip(scores, tops)]
        shrinks = [jnp.exp2((old - top) * FACTOR) for old, top in zip(before, tops)]
        totals = [
            total_ref[head : head + 1, :] * shrink + jnp.sum(each, axis=0, keepdims=True)
            for head, shrink, each in zip(heads, shrinks, weights)
        ]
        mixed = [
            jnp.dot(values[head // GROUP], each.astype(jnp.bfloat16), preferred_element_type=jnp.float32)
            for head, each in zip(heads, weights)
        ]
        inverses = [1.0 / total for total in totals]
        mixed = [
            mixed_ref[head] * (shrink * inverse) + each * inverse
            for head, shrink, inverse, each in zip(heads, shrinks, inverses, mixed)
        ]
        attended = [jnp.transpose(each.astype(jnp.bfloat16)) for each in mixed]
        for head, each in zip(heads, attended):
            here = slice(head * HD, (head + 1) * HD)
            out_ref[:, here] = each
            reward = reward + each.astype(jnp.float32) * weight_ref[:, here]

    seg_col = jnp.transpose(jnp.broadcast_to(seg_row, square))
    after = jnp.concatenate([seg_row[:, 1:], seg_row[:, row_count - 1 :]], axis=1)
    after_col = jnp.transpose(jnp.broadcast_to(after, square))
    row_reward = jnp.sum(reward, axis=1, keepdims=True)
    kept = jnp.where(seg_col != after_col, row_reward, 0.0)
    label = lax.broadcasted_iota(jnp.int32, square, 1)
    by_seg = jnp.sum(jnp.where(seg_col == label, kept, 0.0), axis=0, keepdims=True)
    bin_id = lax.broadcasted_iota(jnp.int32, (1, BINS), 1)
    hist = jnp.zeros((1, BINS), jnp.float32)
    last_bin = jnp.zeros((1, 1), jnp.int32)
    last_seg = seg_row[:, row_count - 1 :]
    for seg in range(SEGS):
        hist = hist + jnp.where(bin_id == bins_ref[0, seg], by_seg[:, seg : seg + 1], 0.0)
        last_bin = last_bin + jnp.where(last_seg == seg, bins_ref[0, seg], 0)
    lane = lax.broadcasted_iota(jnp.int32, (1, HD), 1)
    notes = jnp.where(lane == 0, row_reward[row_count - 1 :, :], 0.0)
    notes = notes + jnp.where(lane == 1, last_bin.astype(jnp.float32), 0.0)
    notes = notes + jnp.where(lane == 2, seg_row[:, :1].astype(jnp.float32), 0.0)
    notes = notes + jnp.where(lane == 3, last_seg.astype(jnp.float32), 0.0)
    hist_ref[...] = jnp.broadcast_to(jnp.concatenate([hist, notes], axis=1), hist_ref.shape)


def total_kernel(ctx_count, rows_ref, out_ref):
    device_count = rows_ref.shape[0]
    notes = rows_ref[:, BINS:]
    reward, bin_of, first, last = (notes[:, k : k + 1] for k in range(4))
    following = jnp.concatenate([first[1:], first[:1]], axis=0)
    device = lax.broadcasted_iota(jnp.int32, (device_count, 1), 0)
    ends = (following != last) | (lax.rem(device, ctx_count) == ctx_count - 1)
    bin_id = lax.broadcasted_iota(jnp.int32, (device_count, BINS), 1).astype(jnp.float32)
    extra = jnp.where((bin_id == bin_of) & ends, reward, 0.0)
    out_ref[...] = jnp.sum(rows_ref[:, :BINS] + extra, axis=0, keepdims=True)


def local(roll_query, roll_keys, roll_values, pack_dest, segment_ids, reward_bins, reward_weight):
    dp_count = lax.axis_size("dp")
    ctx_count = lax.axis_size("ctx")
    row_count = roll_query.shape[1]
    q_width = roll_query.shape[2]
    kv_width = roll_keys.shape[2]
    block_count = row_count // BLK
    cap = (block_count + dp_count - 1) // dp_count
    slot_count = dp_count * cap
    piece_count = dp_count // 2
    reach = row_count * ctx_count // 2
    hop_count = min(ctx_count - 1, (reach - 1 + row_count - 1) // row_count)
    device_count = dp_count * ctx_count
    smem = pl.BlockSpec(memory_space=pltpu.SMEM)
    vmem = pl.BlockSpec(memory_space=pltpu.VMEM)
    hbm = pl.BlockSpec(memory_space=pl.ANY)

    def across(array, distance):
        return lax.ppermute(array, "dp", [(i, i ^ distance) for i in range(dp_count)])

    def gather(pieces, width, name, **options):
        pieces = [pieces[0]] + [across(pieces[i], 2 * i) for i in range(1, piece_count)]
        other = pl.pallas_call(
            lambda *refs: merge_kernel(cap, piece_count, *refs),
            out_shape=jax.ShapeDtypeStruct((piece_count * cap, BLK, width), jnp.bfloat16),
            in_specs=[vmem] * piece_count,
            out_specs=vmem,
            compiler_params=params(16),
            name=name,
        )(*pieces)
        return pieces + [across(other, 1)]

    sorted_kv = pl.pallas_call(
        lambda *refs: sort_kv_kernel(cap, *refs),
        out_shape=jax.ShapeDtypeStruct((slot_count, BLK, 2 * kv_width), jnp.bfloat16),
        in_specs=[hbm, hbm, hbm],
        out_specs=hbm,
        scratch_shapes=[
            pltpu.SMEM((dp_count, block_count), jnp.int32),
            pltpu.SMEM((slot_count,), jnp.int32),
            pltpu.SMEM((dp_count,), jnp.int32),
            pltpu.VMEM((block_count, BLK, kv_width), jnp.bfloat16),
            pltpu.VMEM((block_count, BLK, kv_width), jnp.bfloat16),
            pltpu.VMEM((slot_count, BLK, 2 * kv_width), jnp.bfloat16),
            pltpu.SemaphoreType.DMA((3,)),
            pltpu.SemaphoreType.DMA,
        ],
        compiler_params=params(60),
        name="sort_kv",
    )(
        pack_dest,
        roll_keys.reshape(block_count, BLK, kv_width),
        roll_values.reshape(block_count, BLK, kv_width),
    )
    got_kv = lax.all_to_all(
        sorted_kv.reshape(dp_count, cap * BLK, 2 * kv_width), "dp", split_axis=0, concat_axis=0, tiled=True
    ).reshape(slot_count, BLK, 2 * kv_width)

    sorted_query = pl.pallas_call(
        lambda *refs: sort_query_kernel(cap, piece_count, *refs),
        out_shape=[jax.ShapeDtypeStruct((2 * cap, BLK, q_width), jnp.bfloat16)] * piece_count,
        in_specs=[smem, hbm, hbm],
        out_specs=[hbm] * piece_count,
        scratch_shapes=[
            pltpu.SMEM((slot_count,), jnp.int32),
            pltpu.SMEM((dp_count,), jnp.int32),
            pltpu.SemaphoreType.DMA((slot_count,)),
        ],
        compiler_params=params(16),
        name="sort_query",
    )(pack_dest, roll_query.reshape(block_count, BLK, q_width), sorted_kv)
    sorted_query = pl.pallas_call(
        after_kernel,
        out_shape=[jax.ShapeDtypeStruct((2 * cap, BLK, q_width), jnp.bfloat16)] * piece_count,
        in_specs=[hbm] * (piece_count + 1),
        out_specs=[hbm] * piece_count,
        input_output_aliases={i: i for i in range(piece_count)},
        compiler_params=params(1),
        name="after_kv",
    )(*sorted_query, got_kv)
    got_query = gather(sorted_query, q_width, "merge_query")
    query = pl.pallas_call(
        lambda *refs: unsort_query_kernel(cap, piece_count, *refs),
        out_shape=jax.ShapeDtypeStruct((block_count, BLK, q_width), jnp.bfloat16),
        in_specs=[smem] + [vmem] * (piece_count + 1),
        out_specs=vmem,
        scratch_shapes=[pltpu.SMEM((slot_count,), jnp.int32)],
        compiler_params=params(16),
        name="unsort_query",
    )(pack_dest, *got_query)

    own = pl.pallas_call(
        lambda *refs: unsort_kv_kernel(cap, *refs),
        out_shape=jax.ShapeDtypeStruct((block_count + 1, BLK, 2 * kv_width), jnp.bfloat16),
        in_specs=[smem, vmem, vmem],
        out_specs=vmem,
        scratch_shapes=[pltpu.SMEM((slot_count,), jnp.int32)],
        compiler_params=params(16),
        name="unsort_kv",
    )(pack_dest, segment_ids, got_kv)
    parts = [own]
    forward = [(i, i + 1) for i in range(ctx_count - 1)]
    for _ in range(hop_count):
        parts.append(lax.ppermute(parts[-1], "ctx", forward))

    state = pl.pallas_call(
        lambda *refs: begin_kernel(hop_count, *refs),
        out_shape=(
            jax.ShapeDtypeStruct((HQ, row_count), jnp.float32),
            jax.ShapeDtypeStruct((HQ, row_count), jnp.float32),
            jax.ShapeDtypeStruct((HQ, HD, row_count), jnp.float32),
        ),
        in_specs=[vmem] * (2 + hop_count),
        out_specs=(vmem, vmem, vmem),
        scratch_shapes=[pltpu.VMEM((hop_count * row_count, row_count), jnp.float32)],
        compiler_params=params(16),
        name="begin",
    )(segment_ids, query, *parts[:-1])
    attended, hist_rows = pl.pallas_call(
        lambda *refs: finish_kernel(hop_count, *refs),
        out_shape=(
            jax.ShapeDtypeStruct((row_count, q_width), jnp.bfloat16),
            jax.ShapeDtypeStruct((device_count, BINS + HD), jnp.float32),
        ),
        in_specs=[smem] + [vmem] * 7,
        out_specs=(vmem, vmem),
        scratch_shapes=[pltpu.VMEM((row_count, row_count), jnp.float32)],
        compiler_params=params(16),
        name="finish",
    )(reward_bins, segment_ids, reward_weight.reshape(1, q_width), query, *state, parts[-1])
    gathered = lax.all_to_all(hist_rows, ("dp", "ctx"), split_axis=0, concat_axis=0, tiled=True)
    total = pl.pallas_call(
        lambda *refs: total_kernel(ctx_count, *refs),
        out_shape=jax.ShapeDtypeStruct((1, BINS), jnp.float32),
        in_specs=[vmem],
        out_specs=vmem,
        compiler_params=params(16),
        name="total",
    )(gathered)
    return attended.reshape(1, row_count, q_width), total.reshape(BINS)


def solution(mesh):
    in_specs = (
        P("dp", "ctx", None),
        P("dp", "ctx", None),
        P("dp", "ctx", None),
        P(None, "ctx"),
        P("dp", "ctx"),
        P("dp", None),
        P(),
    )
    out_specs = (P("dp", "ctx", None), P())
    return jax.shard_map(local, mesh=mesh, in_specs=in_specs, out_specs=out_specs, check_vma=False)
```

time: 140 us -> 56.6 us (0.40)
  blocking collectives: 83.3 us -> 13.3 us
  matrix products: 18.4 us -> 0 us
  Pallas kernels: 0 us -> 12.3 us
  waiting for transfers between devices: 0.01 us -> 11.1 us
  local copies, waits for them, and re-layouts: 13.7 us -> 3.01 us
  other arithmetic: 7.23 us -> 0 us
    all_gather x3 -> x0, blocking collectives: 44.4 us -> none  [the longest x1 16.2 us: local(): key_rows = lax.all_gather(packed_keys, 'ctx', axis=0, tiled=True)]
    psum x1 -> x0, blocking collectives: 38.9 us -> none  [local(): histogram = lax.psum(local_hist, ('dp', 'ctx'))]
    dot_general x15 -> x0, matrix products: 18.4 us -> none  [the longest x4 13.5 us: attend_block(): jnp.einsum('gjqk,kgd->qgjd', weights.astype(jnp.bfloat16), value_rows.res...]
    all_to_all x0 -> x1, blocking collectives: none -> 13.3 us  [local(): lax.all_to_all(hist_rows, ('dp', 'ctx'), split_axis=0, concat_axis=0, til...]
    pallas_call x0 -> x9, Pallas kernels: none -> 12.3 us  [the longest x1 3.19 us: local(): pl.pallas_call(lambda *refs: finish_kernel(hop_count, *refs), out_shape=(...]
    ppermute x1 -> x6, waiting for transfers between devices: 0.01 us -> 9.42 us  [the longest x4 6.15 us: across(): lax.ppermute(array, 'dp', [(i, i ^ distance) for i in range(dp_count)])]
    ppermute x1 -> x6, starting transfers between devices: 1.29 us -> 10.6 us  [the longest x2 6.99 us: local(): parts.append(lax.ppermute(parts[-1], 'ctx', forward))]
    all_to_all x3 -> x1, starting transfers between devices: 13.6 us -> 5.18 us  [local(): lax.all_to_all(sorted_kv.reshape(dp_count, cap * BLK, 2 * kv_width), 'dp'...]
  transfers between devices with their start and end apart: 4 -> 7, of which waited for: 0 -> 4; matrix products, arithmetic and copies ran while one was open for 25% -> 0% of each run, Pallas kernels for 0% -> 12%
where the time goes in v2:
time: 56.6 us; the launch traced here: 56.2 us
  starting transfers between devices  15.7 us (28%)
  blocking collectives  13.3 us (23%)
  Pallas kernels  12.3 us (22%)
  waiting for transfers between devices  11.1 us (20%)
  local copies, waits for them, and re-layouts  3.01 us (5%)
  between operations  0.76 us (1%)
    all_to_all x1, blocking collectives, local(): lax.all_to_all(hist_rows, ('dp', 'ctx'), split_axis=0, concat_axis=0, til...  13.3 us
    ppermute x2, starting transfers between devices, local(): parts.append(lax.ppermute(parts[-1], 'ctx', forward))  6.99 us
    ppermute x4, waiting for transfers between devices, across(): lax.ppermute(array, 'dp', [(i, i ^ distance) for i in range(dp_count)])  6.15 us
    all_to_all x1, starting transfers between devices, local(): lax.all_to_all(sorted_kv.reshape(dp_count, cap * BLK, 2 * kv_width), 'dp'...  5.18 us
    ppermute x4, starting transfers between devices, across(): lax.ppermute(array, 'dp', [(i, i ^ distance) for i in range(dp_count)])  3.56 us
    ppermute x2, waiting for transfers between devices, local(): parts.append(lax.ppermute(parts[-1], 'ctx', forward))  3.26 us
    pallas_call x1, Pallas kernels, local(): pl.pallas_call(lambda *refs: finish_kernel(hop_count, *refs), out_shape=(...  3.19 us
    unnamed x15, local copies, waits for them, and re-layouts  2.92 us
  transfers between devices with their start and end apart: 7, of which 4 were waited for; matrix products, arithmetic and copies ran while one was open for 0% of the time, Pallas kernels for 12%

profile of v2, /device:TPU:0, one launch (start us, length us, event | category | flops | bytes accessed | tf_op | source)
XLA Modules:
  0.0 56.2 jit_solution(10712649964089518246)
XLA Ops:
  0.6 0.0 copy-start.3
  0.6 0.0 copy-start.5
  0.7 1.7 %sort_kv.1.refs_2_ = bf16[16,8,1024]{2,1,0:T(8,128)(2,1)} custom-call(s32[8,16]{1,0:T(8,128)} %refs_0_.9, bf16[16,8,512]{2,1,0:T(8,128)(2,1)} %bitcast.19, bf16[16,8,512]{2,1,0:T(8,128)(2,1)} %bitcast.20), custom_call_target="tpu_custom_call" | custom-call | tf_op jit(solution)/shard_map/sort_kv/pallas_call | solution.py:284
  2.4 5.2 %all-to-all-start = ((bf16[8,16,1024]{2,1,0:T(8,128)(2,1)}), bf16[8,16,1024]{2,1,0:T(8,128)(2,1)S(1)}, u32[]{:S(2)}, u32[]{:S(2)}) async-start(bf16[8,16,1024]{2,1,0:T(8,128)(2,1)} %bitcast.14), calls=%async_computation | async-start | bytes 524288 | tf_op jit(solution)/shard_map/all_to_all | solution.py:306
  7.6 1.0 %copy-done = bf16[16,8,1024]{2,1,0:T(8,128)(2,1)S(1)} copy-done((bf16[16,8,1024]{2,1,0:T(8,128)(2,1)S(1)}, bf16[16,8,1024]{2,1,0:T(8,128)(2,1)}, u32[]{:S(2)}) %copy-start) | copy-done | bytes 262168
  8.6 1.2 %copy-done.1 = bf16[1,128,4096]{2,1,0:T(8,128)(2,1)S(1)} copy-done((bf16[1,128,4096]{2,1,0:T(8,128)(2,1)S(1)}, bf16[1,128,4096]{2,1,0:T(8,128)(2,1)}, u32[]{:S(2)}) %copy-start.1) | copy-done | bytes 1048600
  9.8 0.7 %copy-done.2 = s32[8,16]{1,0:T(8,128)S(1)} copy-done((s32[8,16]{1,0:T(8,128)S(1)}, s32[8,16]{1,0:T(8,128)}, u32[]{:S(2)}) %copy-start.2) | copy-done | bytes 536
  10.5 2.4 %sort_query.1 = (bf16[4,8,4096]{2,1,0:T(8,128)(2,1)S(1)}, bf16[4,8,4096]{2,1,0:T(8,128)(2,1)S(1)}, bf16[4,8,4096]{2,1,0:T(8,128)(2,1)S(1)}, bf16[4,8,4096]{2,1,0:T(8,128)(2,1)S(1)}) custom-call(s32[8,16]{1,0:T(8,128)S(1)} %copy-done.2, bf16[16,8,4096]{2,1,0:T(8,128)(2,1)S(1)} %bitcast.15, bf16[16,8,1024]{2,1,0:T(8,128)(2,1)S(1)} %copy-done), custom_call_target="tpu_custom_call" | custom-call | tf_op jit(solution)/shard_map/sort_query/pallas_call | solution.py:310
  12.9 1.7 %all-to-all-done = bf16[8,16,1024]{2,1,0:T(8,128)(2,1)S(1)} async-done(((bf16[8,16,1024]{2,1,0:T(8,128)(2,1)}), bf16[8,16,1024]{2,1,0:T(8,128)(2,1)S(1)}, u32[]{:S(2)}, u32[]{:S(2)}) %all-to-all-start) | async-done | bytes 262176 | tf_op jit(solution)/shard_map/all_to_all | solution.py:306
  14.5 0.6 %collective-permute-start = (bf16[4,8,4096]{2,1,0:T(8,128)(2,1)S(1)}, bf16[4,8,4096]{2,1,0:T(8,128)(2,1)S(1)}, u32[]{:S(2)}, u32[]{:S(2)}) collective-permute-start(bf16[4,8,4096]{2,1,0:T(8,128)(2,1)S(1)} %get-tuple-element.20), channel_id=1, source_target_pairs={{0,8},{4,12},{8,0},{12,4},{16,24},{20,28},{24,16},{28,20},{1,9},{5... | collective-permute-start | bytes 786440 | tf_op jit(solution)/shard_map/ppermute | solution.py:270
  15.1 1.4 %collective-permute-start.1 = (bf16[4,8,4096]{2,1,0:T(8,128)(2,1)S(1)}, bf16[4,8,4096]{2,1,0:T(8,128)(2,1)S(1)}, u32[]{:S(2)}, u32[]{:S(2)}) collective-permute-start(bf16[4,8,4096]{2,1,0:T(8,128)(2,1)S(1)} %get-tuple-element.21), channel_id=1, source_target_pairs={{0,16},{4,20},{8,24},{12,28},{16,0},{20,4},{24,8},{28,12},{1,17},{... | collective-permute-start | bytes 786440 | tf_op jit(solution)/shard_map/ppermute | solution.py:270
  16.4 1.6 %collective-permute-start.2 = (bf16[4,8,4096]{2,1,0:T(8,128)(2,1)S(1)}, bf16[4,8,4096]{2,1,0:T(8,128)(2,1)S(1)}, u32[]{:S(2)}, u32[]{:S(2)}) collective-permute-start(bf16[4,8,4096]{2,1,0:T(8,128)(2,1)S(1)} %get-tuple-element.22), channel_id=1, source_target_pairs={{0,24},{4,28},{8,16},{12,20},{16,8},{20,12},{24,0},{28,4},{1,25},{... | collective-permute-start | bytes 786440 | tf_op jit(solution)/shard_map/ppermute | solution.py:270
  18.0 0.0 copy-done.3
  18.0 0.0 copy-done.5
  18.0 1.0 %unsort_kv.1.refs_2_ = bf16[17,8,1024]{2,1,0:T(8,128)(2,1)S(1)} custom-call(s32[8,16]{1,0:T(8,128)S(1)} %copy-done.3, s32[1,128]{1,0:T(1,128)S(1)} %copy-done.5, bf16[16,8,1024]{2,1,0:T(8,128)(2,1)S(1)} %bitcast.13), custom_call_target="tpu_custom_call" | custom-call | tf_op jit(solution)/shard_map/unsort_kv/pallas_call | solution.py:343
  19.0 3.5 %collective-permute-start.4 = (bf16[17,8,1024]{2,1,0:T(8,128)(2,1)S(1)}, bf16[17,8,1024]{2,1,0:T(8,128)(2,1)S(1)}, u32[]{:S(2)}, u32[]{:S(2)}) collective-permute-start(bf16[17,8,1024]{2,1,0:T(8,128)(2,1)S(1)} %unsort_kv.1.refs_2_), channel_id=1, source_target_pairs={{0,1},{1,2},{2,3},{4,5},{5,6},{6,7},{8,9},{9,10},{10,11},{12,13},{... | collective-permute-start | bytes 835592 | tf_op jit(solution)/shard_map/ppermute | solution.py:355
  22.5 1.2 %collective-permute-done.refs_1_.refs_2_ = bf16[4,8,4096]{2,1,0:T(8,128)(2,1)S(1)} collective-permute-done((bf16[4,8,4096]{2,1,0:T(8,128)(2,1)S(1)}, bf16[4,8,4096]{2,1,0:T(8,128)(2,1)S(1)}, u32[]{:S(2)}, u32[]{:S(2)}) %collective-permute-start) | collective-permute-done | bytes 262176 | tf_op jit(solution)/shard_map/ppermute | solution.py:270
  23.8 4.9 %collective-permute-done.1.refs_2_.refs_3_ = bf16[4,8,4096]{2,1,0:T(8,128)(2,1)S(1)} collective-permute-done((bf16[4,8,4096]{2,1,0:T(8,128)(2,1)S(1)}, bf16[4,8,4096]{2,1,0:T(8,128)(2,1)S(1)}, u32[]{:S(2)}, u32[]{:S(2)}) %collective-permute-start.1) | collective-permute-done | bytes 262176 | tf_op jit(solution)/shard_map/ppermute | solution.py:270
  28.7 0.0 collective-permute-done.2.refs_3_.refs_4_
  28.7 0.0 copy-start.4
  28.7 0.0 copy-start.6
  28.7 0.1 collective-permute-start.3
  28.8 0.0 collective-permute-done.4.refs_3_
  28.8 3.5 %collective-permute-start.5 = (bf16[17,8,1024]{2,1,0:T(8,128)(2,1)S(1)}, bf16[17,8,1024]{2,1,0:T(8,128)(2,1)S(1)}, u32[]{:S(2)}, u32[]{:S(2)}) collective-permute-start(bf16[17,8,1024]{2,1,0:T(8,128)(2,1)S(1)} %collective-permute-done.4.refs_3_), channel_id=1, source_target_pairs={{0,1},{1,2},{2,3},{4,5},{5,6},{6,7},{8,9},{9,10},{10,11},{12,13},{... | collective-permute-start | bytes 835592 | tf_op jit(solution)/shard_map/ppermute | solution.py:355
  32.3 0.0 collective-permute-done.3.refs_5_
  32.3 1.0 %unsort_query.1.refs_1_.refs_3_ = bf16[16,8,4096]{2,1,0:T(8,128)(2,1)S(1)} custom-call(s32[8,16]{1,0:T(8,128)S(1)} %copy-done.3, bf16[4,8,4096]{2,1,0:T(8,128)(2,1)S(1)} %get-tuple-element.19.refs_0_.refs_1_, bf16[4,8,4096]{2,1,0:T(8,128)(2,1)S(1)} %collective-permute-done.refs_1_.refs_2_, bf16[4,8,4096]{2,1,0:T(8,128)(2,1)S(1)} %collective-permute-done.1.refs_2_.refs_3_, ...), custom_call_target="tpu_custom_call" | custom-call | tf_op jit(solution)/shard_map/unsort_query/pallas_call | solution.py:333
  33.4 2.2 %begin.1 = (f32[32,128]{1,0:T(8,128)S(1)}, f32[32,128]{1,0:T(8,128)S(1)}, f32[32,128,128]{2,1,0:T(8,128)S(1)}) custom-call(s32[1,128]{1,0:T(1,128)S(1)} %copy-done.5, bf16[16,8,4096]{2,1,0:T(8,128)(2,1)S(1)} %unsort_query.1.refs_1_.refs_3_, bf16[17,8,1024]{2,1,0:T(8,128)(2,1)S(1)} %unsort_kv.1.refs_2_, bf16[17,8,1024]{2,1,0:T(8,128)(2,1)S(1)} %collective-permute-done.4.refs_3_), custom_call_target="tpu_custom_call" | custom-call | tf_op jit(solution)/shard_map/begin/pallas_call | solution.py:357
  35.6 3.3 %collective-permute-done.5.refs_7_ = bf16[17,8,1024]{2,1,0:T(8,128)(2,1)S(1)} collective-permute-done((bf16[17,8,1024]{2,1,0:T(8,128)(2,1)S(1)}, bf16[17,8,1024]{2,1,0:T(8,128)(2,1)S(1)}, u32[]{:S(2)}, u32[]{:S(2)}) %collective-permute-start.5) | collective-permute-done | bytes 278560 | tf_op jit(solution)/shard_map/ppermute | solution.py:355
  38.9 3.2 %finish.1 = (bf16[128,4096]{1,0:T(8,128)(2,1)}, f32[32,640]{1,0:T(8,128)S(1)}) custom-call(s32[1,16]{1,0:T(1,128)S(1)} %copy-done.6, s32[1,128]{1,0:T(1,128)S(1)} %copy-done.5, f32[1,4096]{1,0:T(1,128)S(1)} %bitcast.18, bf16[16,8,4096]{2,1,0:T(8,128)(2,1)S(1)} %unsort_query.1.refs_1_.refs_3_, f32[32,128]{1,0:T(8,128)S(1)} %get-tuple-element.23.refs_4_, ...), custom_call_target="tpu_custom_call" | custom-call | tf_op jit(solution)/shard_map/finish/pallas_call | solution.py:370
  42.0 0.1 copy.13
  42.1 13.3 %all_to_all.16 = f32[32,1,640]{2,1,0:T(1,128)S(1)} all-to-all(f32[32,1,640]{2,1,0:T(1,128)S(1)} %copy.13), channel_id=1, replica_groups=mesh['dp'=8,'ctx'=4] {'dp','ctx'}, dimensions={0} | all-to-all | bytes 163840 | tf_op jit(solution)/shard_map/all_to_all | solution.py:382
  55.4 0.7 %total.1 = f32[1,512]{1,0:T(1,128)} custom-call(f32[32,640]{1,0:T(8,128)S(1)} %bitcast.16), custom_call_target="tpu_custom_call" | custom-call | tf_op jit(solution)/shard_map/total/pallas_call | solution.py:383
  (8 shorter events, 0.1 us)
Async XLA Ops:
  0.6 17.4 %copy-start.3 = (s32[8,16]{1,0:T(8,128)S(1)}, s32[8,16]{1,0:T(8,128)}, u32[]{:S(2)}) copy-start(s32[8,16]{1,0:T(8,128)} %refs_0_.9) | copy-start | bytes 1540
  0.6 17.4 %copy-start.5 = (s32[1,128]{1,0:T(1,128)S(1)}, s32[1,128]{1,0:T(1,128)}, u32[]{:S(2)}) copy-start(s32[1,128]{1,0:T(1,128)} %refs_1_.3) | copy-start | bytes 1540
  2.4 12.1 %all-to-all-start = ((bf16[8,16,1024]{2,1,0:T(8,128)(2,1)}), bf16[8,16,1024]{2,1,0:T(8,128)(2,1)S(1)}, u32[]{:S(2)}, u32[]{:S(2)}) async-start(bf16[8,16,1024]{2,1,0:T(8,128)(2,1)} %bitcast.14), calls=%async_computation | async-start | bytes 524288 | tf_op jit(solution)/shard_map/all_to_all | solution.py:306
  7.6 1.0 %copy-start = (bf16[16,8,1024]{2,1,0:T(8,128)(2,1)S(1)}, bf16[16,8,1024]{2,1,0:T(8,128)(2,1)}, u32[]{:S(2)}) copy-start(bf16[16,8,1024]{2,1,0:T(8,128)(2,1)} %sort_kv.1.refs_2_) | copy-start | bytes 786436
  8.6 1.2 %copy-start.1 = (bf16[1,128,4096]{2,1,0:T(8,128)(2,1)S(1)}, bf16[1,128,4096]{2,1,0:T(8,128)(2,1)}, u32[]{:S(2)}) copy-start(bf16[1,128,4096]{2,1,0:T(8,128)(2,1)} %param.7) | copy-start | bytes 3145732
  9.8 0.7 %copy-start.2 = (s32[8,16]{1,0:T(8,128)S(1)}, s32[8,16]{1,0:T(8,128)}, u32[]{:S(2)}) copy-start(s32[8,16]{1,0:T(8,128)} %refs_0_.9) | copy-start | bytes 1540
  14.5 9.2 %collective-permute-start = (bf16[4,8,4096]{2,1,0:T(8,128)(2,1)S(1)}, bf16[4,8,4096]{2,1,0:T(8,128)(2,1)S(1)}, u32[]{:S(2)}, u32[]{:S(2)}) collective-permute-start(bf16[4,8,4096]{2,1,0:T(8,128)(2,1)S(1)} %get-tuple-element.20), channel_id=1, source_target_pairs={{0,8},{4,12},{8,0},{12,4},{16,24},{20,28},{24,16},{28,20},{1,9},{5... | collective-permute-start | bytes 786440 | tf_op jit(solution)/shard_map/ppermute | solution.py:270
  15.1 13.6 %collective-permute-start.1 = (bf16[4,8,4096]{2,1,0:T(8,128)(2,1)S(1)}, bf16[4,8,4096]{2,1,0:T(8,128)(2,1)S(1)}, u32[]{:S(2)}, u32[]{:S(2)}) collective-permute-start(bf16[4,8,4096]{2,1,0:T(8,128)(2,1)S(1)} %get-tuple-element.21), channel_id=1, source_target_pairs={{0,16},{4,20},{8,24},{12,28},{16,0},{20,4},{24,8},{28,12},{1,17},{... | collective-permute-start | bytes 786440 | tf_op jit(solution)/shard_map/ppermute | solution.py:270
  16.4 12.2 %collective-permute-start.2 = (bf16[4,8,4096]{2,1,0:T(8,128)(2,1)S(1)}, bf16[4,8,4096]{2,1,0:T(8,128)(2,1)S(1)}, u32[]{:S(2)}, u32[]{:S(2)}) collective-permute-start(bf16[4,8,4096]{2,1,0:T(8,128)(2,1)S(1)} %get-tuple-element.22), channel_id=1, source_target_pairs={{0,24},{4,28},{8,16},{12,20},{16,8},{20,12},{24,0},{28,4},{1,25},{... | collective-permute-start | bytes 786440 | tf_op jit(solution)/shard_map/ppermute | solution.py:270
  19.0 9.8 %collective-permute-start.4 = (bf16[17,8,1024]{2,1,0:T(8,128)(2,1)S(1)}, bf16[17,8,1024]{2,1,0:T(8,128)(2,1)S(1)}, u32[]{:S(2)}, u32[]{:S(2)}) collective-permute-start(bf16[17,8,1024]{2,1,0:T(8,128)(2,1)S(1)} %unsort_kv.1.refs_2_), channel_id=1, source_target_pairs={{0,1},{1,2},{2,3},{4,5},{5,6},{6,7},{8,9},{9,10},{10,11},{12,13},{... | collective-permute-start | bytes 835592 | tf_op jit(solution)/shard_map/ppermute | solution.py:355
  28.7 10.1 %copy-start.4 = (f32[4096]{0:T(1024)S(1)}, f32[4096]{0:T(1024)}, u32[]{:S(2)}) copy-start(f32[4096]{0:T(1024)} %param.13) | copy-start | bytes 49156
  28.7 10.1 %copy-start.6 = (s32[1,16]{1,0:T(1,128)S(1)}, s32[1,16]{1,0:T(1,128)}, u32[]{:S(2)}) copy-start(s32[1,16]{1,0:T(1,128)} %refs_0_.11) | copy-start | bytes 196
  28.7 3.6 %collective-permute-start.3 = (bf16[8,8,4096]{2,1,0:T(8,128)(2,1)S(1)}, bf16[8,8,4096]{2,1,0:T(8,128)(2,1)S(1)}, u32[]{:S(2)}, u32[]{:S(2)}) collective-permute-start(bf16[8,8,4096]{2,1,0:T(8,128)(2,1)S(1)} %merge_query.1), channel_id=1, source_target_pairs={{0,4},{4,0},{8,12},{12,8},{16,20},{20,16},{24,28},{28,24},{1,5},{5... | collective-permute-start | bytes 1572872 | tf_op jit(solution)/shard_map/ppermute | solution.py:270
  28.8 10.0 %collective-permute-start.5 = (bf16[17,8,1024]{2,1,0:T(8,128)(2,1)S(1)}, bf16[17,8,1024]{2,1,0:T(8,128)(2,1)S(1)}, u32[]{:S(2)}, u32[]{:S(2)}) collective-permute-start(bf16[17,8,1024]{2,1,0:T(8,128)(2,1)S(1)} %collective-permute-done.4.refs_3_), channel_id=1, source_target_pairs={{0,1},{1,2},{2,3},{4,5},{5,6},{6,7},{8,9},{9,10},{10,11},{12,13},{... | collective-permute-start | bytes 835592 | tf_op jit(solution)/shard_map/ppermute | solution.py:355

commit v3 on v2

--- a/solution.py
+++ b/solution.py
@@ -84,20 +84,28 @@
     departure.wait()
 
 
-def sort_query_kernel(cap, piece_count, dest_ref, query_ref, after_ref, *rest):
+def sort_query_kernel(cap, piece_count, dest_hbm, query_hbm, *rest):
     pieces = rest[:piece_count]
-    block_ref, count_ref, sem = rest[piece_count:]
+    dest_ref, block_ref, count_ref, query_ref, in_sem, out_sem = rest[piece_count:]
+    arrivals = [
+        pltpu.make_async_copy(dest_hbm, dest_ref, in_sem.at[0]),
+        pltpu.make_async_copy(query_hbm, query_ref, in_sem.at[1]),
+    ]
+    for arrival in arrivals:
+        arrival.start()
+    arrivals[0].wait()
     find_blocks(dest_ref, block_ref, count_ref, cap, True)
-    copies = []
+    arrivals[1].wait()
+    departures = []
     for slot in range(2 * piece_count * cap):
         piece, place = divmod(slot, 2 * cap)
-        copies.append(
-            pltpu.make_async_copy(query_ref.at[block_ref[slot]], pieces[piece].at[place], sem.at[slot])
+        departures.append(
+            pltpu.make_async_copy(query_ref.at[block_ref[slot]], pieces[piece].at[place], out_sem.at[slot])
         )
-    for copy in copies:
-        copy.start()
-    for copy in copies:
-        copy.wait()
+    for departure in departures:
+        departure.start()
+    for departure in departures:
+        departure.wait()
 
 
 def merge_kernel(cap, piece_count, *refs):
@@ -124,10 +132,6 @@
     labels = seg_ref[...].astype(jnp.float32)
     labels = jnp.concatenate([labels] * (out_ref.shape[2] // labels.shape[1]), axis=1)
     out_ref[block_count] = jnp.broadcast_to(labels, out_ref.shape[1:]).astype(out_ref.dtype)
-
-
-def after_kernel(*refs):
-    pass
 
 
 def rows_of(ref, lane):
@@ -310,25 +314,19 @@
     sorted_query = pl.pallas_call(
         lambda *refs: sort_query_kernel(cap, piece_count, *refs),
         out_shape=[jax.ShapeDtypeStruct((2 * cap, BLK, q_width), jnp.bfloat16)] * piece_count,
-        in_specs=[smem, hbm, hbm],
+        in_specs=[hbm, hbm],
         out_specs=[hbm] * piece_count,
         scratch_shapes=[
+            pltpu.SMEM((dp_count, block_count), jnp.int32),
             pltpu.SMEM((slot_count,), jnp.int32),
             pltpu.SMEM((dp_count,), jnp.int32),
+            pltpu.VMEM((block_count, BLK, q_width), jnp.bfloat16),
+            pltpu.SemaphoreType.DMA((2,)),
             pltpu.SemaphoreType.DMA((slot_count,)),
         ],
-        compiler_params=params(16),
+        compiler_params=params(60),
         name="sort_query",
-    )(pack_dest, roll_query.reshape(block_count, BLK, q_width), sorted_kv)
-    sorted_query = pl.pallas_call(
-        after_kernel,
-        out_shape=[jax.ShapeDtypeStruct((2 * cap, BLK, q_width), jnp.bfloat16)] * piece_count,
-        in_specs=[hbm] * (piece_count + 1),
-        out_specs=[hbm] * piece_count,
-        input_output_aliases={i: i for i in range(piece_count)},
-        compiler_params=params(1),
-        name="after_kv",
-    )(*sorted_query, got_kv)
+    )(pack_dest, roll_query.reshape(block_count, BLK, q_width))
     got_query = gather(sorted_query, q_width, "merge_query")
     query = pl.pallas_call(
         lambda *refs: unsort_query_kernel(cap, piece_count, *refs),
@@ -347,6 +345,7 @@
         out_specs=vmem,
         scratch_shapes=[pltpu.SMEM((slot_count,), jnp.int32)],
         compiler_params=params(16),
+        cost_estimate=cost(23000000000, 0),
         name="unsort_kv",
     )(pack_dest, segment_ids, got_kv)
     parts = [own]

time: 56.6 us -> 53.8 us (0.951)
  local copies, waits for them, and re-layouts: 3.01 us -> 0.12 us
    unnamed x15 -> x11, local copies, waits for them, and re-layouts: 2.92 us -> 0.03 us
    ppermute x4, waiting for transfers between devices: 6.15 us -> 6.84 us  [across(): lax.ppermute(array, 'dp', [(i, i ^ distance) for i in range(dp_count)])]
    all_to_all x1, waiting for transfers between devices: 1.66 us -> 1.02 us  [local(): lax.all_to_all(sorted_kv.reshape(dp_count, cap * BLK, 2 * kv_width), 'dp'...]
where the time goes in v3:
time: 53.8 us; the launch traced here: 53.5 us
  starting transfers between devices  15.9 us (30%)
  blocking collectives  13.3 us (25%)
  Pallas kernels  12.3 us (23%)
  waiting for transfers between devices  11.1 us (21%)
  between operations  0.76 us (1%)
    all_to_all x1, blocking collectives, local(): lax.all_to_all(hist_rows, ('dp', 'ctx'), split_axis=0, concat_axis=0, til...  13.3 us
    ppermute x2, starting transfers between devices, local(): parts.append(lax.ppermute(parts[-1], 'ctx', forward))  6.99 us
    ppermute x4, waiting for transfers between devices, across(): lax.ppermute(array, 'dp', [(i, i ^ distance) for i in range(dp_count)])  6.84 us
    all_to_all x1, starting transfers between devices, local(): lax.all_to_all(sorted_kv.reshape(dp_count, cap * BLK, 2 * kv_width), 'dp'...  5.18 us
    ppermute x4, starting transfers between devices, across(): lax.ppermute(array, 'dp', [(i, i ^ distance) for i in range(dp_count)])  3.7 us
    ppermute x2, waiting for transfers between devices, local(): parts.append(lax.ppermute(parts[-1], 'ctx', forward))  3.28 us
    pallas_call x1, Pallas kernels, local(): pl.pallas_call(lambda *refs: finish_kernel(hop_count, *refs), out_shape=(...  3.24 us
    pallas_call x1, Pallas kernels, local(): pl.pallas_call(lambda *refs: sort_query_kernel(cap, piece_count, *refs),...  2.33 us
  transfers between devices with their start and end apart: 7, of which 4 were waited for; matrix products, arithmetic and copies ran while one was open for 0% of the time, Pallas kernels for 12%

profile of v3, /device:TPU:0, one launch (start us, length us, event | category | flops | bytes accessed | tf_op | source)
XLA Modules:
  0.0 53.5 jit_solution(13964561661245537825)
XLA Ops:
  0.6 0.0 copy-start.1
  0.6 0.0 copy-start.3
  0.7 1.7 %sort_kv.1 = bf16[16,8,1024]{2,1,0:T(8,128)(2,1)} custom-call(s32[8,16]{1,0:T(8,128)} %refs_0_.9, bf16[16,8,512]{2,1,0:T(8,128)(2,1)} %bitcast.18, bf16[16,8,512]{2,1,0:T(8,128)(2,1)} %bitcast.19), custom_call_target="tpu_custom_call" | custom-call | tf_op jit(solution)/shard_map/sort_kv/pallas_call | solution.py:288
  2.4 5.2 %all-to-all-start = ((bf16[8,16,1024]{2,1,0:T(8,128)(2,1)}), bf16[8,16,1024]{2,1,0:T(8,128)(2,1)S(1)}, u32[]{:S(2)}, u32[]{:S(2)}) async-start(bf16[8,16,1024]{2,1,0:T(8,128)(2,1)} %bitcast.17), calls=%async_computation | async-start | bytes 524288 | tf_op jit(solution)/shard_map/all_to_all | solution.py:310
  7.6 2.3 %sort_query.1 = (bf16[4,8,4096]{2,1,0:T(8,128)(2,1)}, bf16[4,8,4096]{2,1,0:T(8,128)(2,1)}, bf16[4,8,4096]{2,1,0:T(8,128)(2,1)}, bf16[4,8,4096]{2,1,0:T(8,128)(2,1)}) custom-call(s32[8,16]{1,0:T(8,128)} %refs_0_.9, bf16[16,8,4096]{2,1,0:T(8,128)(2,1)} %bitcast.16), custom_call_target="tpu_custom_call" | custom-call | tf_op jit(solution)/shard_map/sort_query/pallas_call | solution.py:314
  9.9 2.1 %collective-permute-start = (bf16[4,8,4096]{2,1,0:T(8,128)(2,1)}, bf16[4,8,4096]{2,1,0:T(8,128)(2,1)S(1)}, u32[]{:S(2)}, u32[]{:S(2)}) collective-permute-start(bf16[4,8,4096]{2,1,0:T(8,128)(2,1)} %get-tuple-element.12), channel_id=1, source_target_pairs={{0,8},{4,12},{8,0},{12,4},{16,24},{20,28},{24,16},{28,20},{1,9},{5... | collective-permute-start | bytes 786440 | tf_op jit(solution)/shard_map/ppermute | solution.py:274
  12.0 1.5 %collective-permute-start.1 = (bf16[4,8,4096]{2,1,0:T(8,128)(2,1)}, bf16[4,8,4096]{2,1,0:T(8,128)(2,1)S(1)}, u32[]{:S(2)}, u32[]{:S(2)}) collective-permute-start(bf16[4,8,4096]{2,1,0:T(8,128)(2,1)} %get-tuple-element.13), channel_id=1, source_target_pairs={{0,16},{4,20},{8,24},{12,28},{16,0},{20,4},{24,8},{28,12},{1,17},{... | collective-permute-start | bytes 786440 | tf_op jit(solution)/shard_map/ppermute | solution.py:274
  13.5 0.1 collective-permute-start.2
  13.6 1.0 %all-to-all-done = bf16[8,16,1024]{2,1,0:T(8,128)(2,1)S(1)} async-done(((bf16[8,16,1024]{2,1,0:T(8,128)(2,1)}), bf16[8,16,1024]{2,1,0:T(8,128)(2,1)S(1)}, u32[]{:S(2)}, u32[]{:S(2)}) %all-to-all-start) | async-done | bytes 262176 | tf_op jit(solution)/shard_map/all_to_all | solution.py:310
  14.6 0.0 copy-done.1
  14.6 0.0 copy-done.3
  14.6 1.0 %unsort_kv.1.refs_2_ = bf16[17,8,1024]{2,1,0:T(8,128)(2,1)S(1)} custom-call(s32[8,16]{1,0:T(8,128)S(1)} %copy-done.1, s32[1,128]{1,0:T(1,128)S(1)} %copy-done.3, bf16[16,8,1024]{2,1,0:T(8,128)(2,1)S(1)} %bitcast.13), custom_call_target="tpu_custom_call" | custom-call | flops 23000000512 | tf_op jit(solution)/shard_map/unsort_kv/pallas_call | solution.py:341
  15.6 3.5 %collective-permute-start.4 = (bf16[17,8,1024]{2,1,0:T(8,128)(2,1)S(1)}, bf16[17,8,1024]{2,1,0:T(8,128)(2,1)S(1)}, u32[]{:S(2)}, u32[]{:S(2)}) collective-permute-start(bf16[17,8,1024]{2,1,0:T(8,128)(2,1)S(1)} %unsort_kv.1.refs_2_), channel_id=1, source_target_pairs={{0,1},{1,2},{2,3},{4,5},{5,6},{6,7},{8,9},{9,10},{10,11},{12,13},{... | collective-permute-start | bytes 835592 | tf_op jit(solution)/shard_map/ppermute | solution.py:354
  19.1 0.4 collective-permute-done.refs_1_.refs_2_
  19.5 6.4 %collective-permute-done.1.refs_2_.refs_3_ = bf16[4,8,4096]{2,1,0:T(8,128)(2,1)S(1)} collective-permute-done((bf16[4,8,4096]{2,1,0:T(8,128)(2,1)}, bf16[4,8,4096]{2,1,0:T(8,128)(2,1)S(1)}, u32[]{:S(2)}, u32[]{:S(2)}) %collective-permute-start.1) | collective-permute-done | bytes 262176 | tf_op jit(solution)/shard_map/ppermute | solution.py:274
  25.9 0.0 collective-permute-done.2.refs_3_.refs_4_
  25.9 0.0 copy-done
  26.0 0.0 copy-start.2
  26.0 0.0 copy-start.4
  26.0 0.1 collective-permute-start.3
  26.1 0.0 collective-permute-done.4.refs_3_
  26.1 3.5 %collective-permute-start.5 = (bf16[17,8,1024]{2,1,0:T(8,128)(2,1)S(1)}, bf16[17,8,1024]{2,1,0:T(8,128)(2,1)S(1)}, u32[]{:S(2)}, u32[]{:S(2)}) collective-permute-start(bf16[17,8,1024]{2,1,0:T(8,128)(2,1)S(1)} %collective-permute-done.4.refs_3_), channel_id=1, source_target_pairs={{0,1},{1,2},{2,3},{4,5},{5,6},{6,7},{8,9},{9,10},{10,11},{12,13},{... | collective-permute-start | bytes 835592 | tf_op jit(solution)/shard_map/ppermute | solution.py:354
  29.6 0.0 collective-permute-done.3.refs_5_
  29.6 1.0 %unsort_query.1.refs_1_.refs_3_ = bf16[16,8,4096]{2,1,0:T(8,128)(2,1)S(1)} custom-call(s32[8,16]{1,0:T(8,128)S(1)} %copy-done.1, bf16[4,8,4096]{2,1,0:T(8,128)(2,1)S(1)} %copy-done, bf16[4,8,4096]{2,1,0:T(8,128)(2,1)S(1)} %collective-permute-done.refs_1_.refs_2_, bf16[4,8,4096]{2,1,0:T(8,128)(2,1)S(1)} %collective-permute-done.1.refs_2_.refs_3_, ...), custom_call_target="tpu_custom_call" | custom-call | tf_op jit(solution)/shard_map/unsort_query/pallas_call | solution.py:331
  30.6 2.2 %begin.1 = (f32[32,128]{1,0:T(8,128)S(1)}, f32[32,128]{1,0:T(8,128)S(1)}, f32[32,128,128]{2,1,0:T(8,128)S(1)}) custom-call(s32[1,128]{1,0:T(1,128)S(1)} %copy-done.3, bf16[16,8,4096]{2,1,0:T(8,128)(2,1)S(1)} %unsort_query.1.refs_1_.refs_3_, bf16[17,8,1024]{2,1,0:T(8,128)(2,1)S(1)} %unsort_kv.1.refs_2_, bf16[17,8,1024]{2,1,0:T(8,128)(2,1)S(1)} %collective-permute-done.4.refs_3_), custom_call_target="tpu_custom_call" | custom-call | tf_op jit(solution)/shard_map/begin/pallas_call | solution.py:356
  32.8 3.3 %collective-permute-done.5.refs_7_ = bf16[17,8,1024]{2,1,0:T(8,128)(2,1)S(1)} collective-permute-done((bf16[17,8,1024]{2,1,0:T(8,128)(2,1)S(1)}, bf16[17,8,1024]{2,1,0:T(8,128)(2,1)S(1)}, u32[]{:S(2)}, u32[]{:S(2)}) %collective-permute-start.5) | collective-permute-done | bytes 278560 | tf_op jit(solution)/shard_map/ppermute | solution.py:354
  36.1 0.0 copy-done.2
  36.1 0.0 copy-done.4
  36.1 3.2 %finish.1 = (bf16[128,4096]{1,0:T(8,128)(2,1)}, f32[32,640]{1,0:T(8,128)S(1)}) custom-call(s32[1,16]{1,0:T(1,128)S(1)} %copy-done.4, s32[1,128]{1,0:T(1,128)S(1)} %copy-done.3, f32[1,4096]{1,0:T(1,128)S(1)} %bitcast.15, bf16[16,8,4096]{2,1,0:T(8,128)(2,1)S(1)} %unsort_query.1.refs_1_.refs_3_, f32[32,128]{1,0:T(8,128)S(1)} %get-tuple-element.15.refs_4_, ...), custom_call_target="tpu_custom_call" | custom-call | tf_op jit(solution)/shard_map/finish/pallas_call | solution.py:369
  39.4 0.1 copy.9
  39.4 13.3 %all_to_all.16 = f32[32,1,640]{2,1,0:T(1,128)S(1)} all-to-all(f32[32,1,640]{2,1,0:T(1,128)S(1)} %copy.9), channel_id=1, replica_groups=mesh['dp'=8,'ctx'=4] {'dp','ctx'}, dimensions={0} | all-to-all | bytes 163840 | tf_op jit(solution)/shard_map/all_to_all | solution.py:381
  52.7 0.7 %total.1 = f32[1,512]{1,0:T(1,128)} custom-call(f32[32,640]{1,0:T(8,128)S(1)} %bitcast.12), custom_call_target="tpu_custom_call" | custom-call | tf_op jit(solution)/shard_map/total/pallas_call | solution.py:382
  (3 shorter events, 0.0 us)
Async XLA Ops:
  0.6 13.9 %copy-start.1 = (s32[8,16]{1,0:T(8,128)S(1)}, s32[8,16]{1,0:T(8,128)}, u32[]{:S(2)}) copy-start(s32[8,16]{1,0:T(8,128)} %refs_0_.9) | copy-start | bytes 1540
  0.6 13.9 %copy-start.3 = (s32[1,128]{1,0:T(1,128)S(1)}, s32[1,128]{1,0:T(1,128)}, u32[]{:S(2)}) copy-start(s32[1,128]{1,0:T(1,128)} %refs_1_.3) | copy-start | bytes 1540
  2.4 12.2 %all-to-all-start = ((bf16[8,16,1024]{2,1,0:T(8,128)(2,1)}), bf16[8,16,1024]{2,1,0:T(8,128)(2,1)S(1)}, u32[]{:S(2)}, u32[]{:S(2)}) async-start(bf16[8,16,1024]{2,1,0:T(8,128)(2,1)} %bitcast.17), calls=%async_computation | async-start | bytes 524288 | tf_op jit(solution)/shard_map/all_to_all | solution.py:310
  9.9 9.6 %collective-permute-start = (bf16[4,8,4096]{2,1,0:T(8,128)(2,1)}, bf16[4,8,4096]{2,1,0:T(8,128)(2,1)S(1)}, u32[]{:S(2)}, u32[]{:S(2)}) collective-permute-start(bf16[4,8,4096]{2,1,0:T(8,128)(2,1)} %get-tuple-element.12), channel_id=1, source_target_pairs={{0,8},{4,12},{8,0},{12,4},{16,24},{20,28},{24,16},{28,20},{1,9},{5... | collective-permute-start | bytes 786440 | tf_op jit(solution)/shard_map/ppermute | solution.py:274
  12.0 13.9 %collective-permute-start.1 = (bf16[4,8,4096]{2,1,0:T(8,128)(2,1)}, bf16[4,8,4096]{2,1,0:T(8,128)(2,1)S(1)}, u32[]{:S(2)}, u32[]{:S(2)}) collective-permute-start(bf16[4,8,4096]{2,1,0:T(8,128)(2,1)} %get-tuple-element.13), channel_id=1, source_target_pairs={{0,16},{4,20},{8,24},{12,28},{16,0},{20,4},{24,8},{28,12},{1,17},{... | collective-permute-start | bytes 786440 | tf_op jit(solution)/shard_map/ppermute | solution.py:274
  13.5 12.4 %collective-permute-start.2 = (bf16[4,8,4096]{2,1,0:T(8,128)(2,1)}, bf16[4,8,4096]{2,1,0:T(8,128)(2,1)S(1)}, u32[]{:S(2)}, u32[]{:S(2)}) collective-permute-start(bf16[4,8,4096]{2,1,0:T(8,128)(2,1)} %get-tuple-element.14), channel_id=1, source_target_pairs={{0,24},{4,28},{8,16},{12,20},{16,8},{20,12},{24,0},{28,4},{1,25},{... | collective-permute-start | bytes 786440 | tf_op jit(solution)/shard_map/ppermute | solution.py:274
  14.6 11.4 %copy-start = (bf16[4,8,4096]{2,1,0:T(8,128)(2,1)S(1)}, bf16[4,8,4096]{2,1,0:T(8,128)(2,1)}, u32[]{:S(2)}) copy-start(bf16[4,8,4096]{2,1,0:T(8,128)(2,1)} %get-tuple-element.11.refs_0_.refs_1_) | copy-start | bytes 786436
  15.6 10.5 %collective-permute-start.4 = (bf16[17,8,1024]{2,1,0:T(8,128)(2,1)S(1)}, bf16[17,8,1024]{2,1,0:T(8,128)(2,1)S(1)}, u32[]{:S(2)}, u32[]{:S(2)}) collective-permute-start(bf16[17,8,1024]{2,1,0:T(8,128)(2,1)S(1)} %unsort_kv.1.refs_2_), channel_id=1, source_target_pairs={{0,1},{1,2},{2,3},{4,5},{5,6},{6,7},{8,9},{9,10},{10,11},{12,13},{... | collective-permute-start | bytes 835592 | tf_op jit(solution)/shard_map/ppermute | solution.py:354
  26.0 10.1 %copy-start.2 = (f32[4096]{0:T(1024)S(1)}, f32[4096]{0:T(1024)}, u32[]{:S(2)}) copy-start(f32[4096]{0:T(1024)} %param.13) | copy-start | bytes 49156
  26.0 10.1 %copy-start.4 = (s32[1,16]{1,0:T(1,128)S(1)}, s32[1,16]{1,0:T(1,128)}, u32[]{:S(2)}) copy-start(s32[1,16]{1,0:T(1,128)} %refs_0_.11) | copy-start | bytes 196
  26.0 3.6 %collective-permute-start.3 = (bf16[8,8,4096]{2,1,0:T(8,128)(2,1)S(1)}, bf16[8,8,4096]{2,1,0:T(8,128)(2,1)S(1)}, u32[]{:S(2)}, u32[]{:S(2)}) collective-permute-start(bf16[8,8,4096]{2,1,0:T(8,128)(2,1)S(1)} %merge_query.1), channel_id=1, source_target_pairs={{0,4},{4,0},{8,12},{12,8},{16,20},{20,16},{24,28},{28,24},{1,5},{5... | collective-permute-start | bytes 1572872 | tf_op jit(solution)/shard_map/ppermute | solution.py:274
  26.1 10.0 %collective-permute-start.5 = (bf16[17,8,1024]{2,1,0:T(8,128)(2,1)S(1)}, bf16[17,8,1024]{2,1,0:T(8,128)(2,1)S(1)}, u32[]{:S(2)}, u32[]{:S(2)}) collective-permute-start(bf16[17,8,1024]{2,1,0:T(8,128)(2,1)S(1)} %collective-permute-done.4.refs_3_), channel_id=1, source_target_pairs={{0,1},{1,2},{2,3},{4,5},{5,6},{6,7},{8,9},{9,10},{10,11},{12,13},{... | collective-permute-start | bytes 835592 | tf_op jit(solution)/shard_map/ppermute | solution.py:354

commit v4 on v2

v4 whole, which is shorter than its diff:
```python
import math

import jax
import jax.numpy as jnp
from jax import lax
from jax.experimental import pallas as pl
from jax.experimental.pallas import tpu as pltpu
from jax.sharding import PartitionSpec as P

HQ = 32
HK = 4
HD = 128
GROUP = HQ // HK
BLK = 8
SEGS = 16
BINS = 512
NEG = -1e30
SHARES = (2, HK - 2)
FACTOR = math.log2(math.e) / math.sqrt(HD)


def params(mebibytes):
    return pltpu.CompilerParams(vmem_limit_bytes=mebibytes * 1024 * 1024)


def cost(flops, nbytes):
    return pl.CostEstimate(flops=flops, bytes_accessed=nbytes, transcendentals=0)


def find_blocks(dest_ref, block_ref, count_ref, cap, relative):
    dp_count, block_count = dest_ref.shape
    me = lax.axis_index("dp")
    for target in range(dp_count):
        count_ref[target] = 0
    for block in range(block_count):
        target = dest_ref[me, block]
        rank = count_ref[target]
        count_ref[target] = rank + 1
        place = (target ^ me) if relative else target
        block_ref[place * cap + rank] = block


def find_columns(dest_ref, column_ref, cap, relative):
    dp_count, block_count = dest_ref.shape
    me = lax.axis_index("dp")

    def source(src, _):
        place = (src ^ me) if relative else src
        rank = 0
        for block in range(block_count):
            hit = dest_ref[src, block] == me

            @pl.when(hit)
            def _():
                column_ref[place * cap + rank] = block

            rank = rank + jnp.where(hit, 1, 0)
        return 0

    lax.fori_loop(0, dp_count, source, 0)


def sort_kernel(cap, piece_count, dest_hbm, key_hbm, value_hbm, query_hbm, kv_hbm, same_hbm, other_hbm, *scratch):
    dest_ref, block_ref, count_ref, place_ref, key_ref, value_ref, query_ref, stage_ref, in_sem, out_sem = scratch
    arrivals = [
        pltpu.make_async_copy(source, target, in_sem.at[index])
        for index, (source, target) in enumerate(
            ((dest_hbm, dest_ref), (key_hbm, key_ref), (value_hbm, value_ref), (query_hbm, query_ref))
        )
    ]
    for arrival in arrivals:
        arrival.start()
    arrivals[0].wait()
    find_blocks(dest_ref, block_ref, count_ref, cap, False)
    find_blocks(dest_ref, place_ref, count_ref, cap, True)
    arrivals[1].wait()
    arrivals[2].wait()
    width = key_ref.shape[2]
    slot_count = kv_hbm.shape[0]
    for slot in range(slot_count):
        block = block_ref[slot]
        stage_ref[slot, :, :width] = key_ref[block]
        stage_ref[slot, :, width:] = value_ref[block]
    departures = [pltpu.make_async_copy(stage_ref, kv_hbm, out_sem.at[slot_count])]
    departures[0].start()
    arrivals[3].wait()
    for odd, out in ((1, other_hbm), (0, same_hbm)):
        for place in range(piece_count * cap):
            slot = (2 * (place // cap) + odd) * cap + place % cap
            departure = pltpu.make_async_copy(query_ref.at[place_ref[slot]], out.at[place], out_sem.at[slot])
            departure.start()
            departures.append(departure)
    for departure in departures:
        departure.wait()


def merge_query_kernel(cap, piece_count, same_ref, other_ref, *pieces):
    for piece in range(piece_count):
        rows = slice(piece * cap, (piece + 1) * cap)
        pieces[piece][:cap] = same_ref[rows]
        pieces[piece][cap:] = other_ref[rows]


def unsort_query_kernel(cap, piece_count, dest_ref, *rest):
    pieces = rest[:piece_count]
    out_ref, column_ref = rest[piece_count:]
    find_columns(dest_ref, column_ref, cap, True)
    for piece in range(piece_count):
        for place in range(2 * cap):
            out_ref[column_ref[2 * piece * cap + place]] = pieces[piece][place]


def unsort_kv_kernel(cap, dest_ref, seg_ref, got_ref, *rest):
    outs, column_ref = rest[:-1], rest[-1]
    find_columns(dest_ref, column_ref, cap, False)
    block_count = got_ref.shape[0]
    for slot in range(block_count):
        column = column_ref[slot]
        first = 0
        for out_ref, groups in zip(outs, SHARES):
            width = groups * HD
            for half in range(2):
                start = half * HK * HD + first
                out_ref[column, :, half * width : (half + 1) * width] = got_ref[slot, :, start : start + width]
            first += width
    labels = seg_ref[...].astype(jnp.float32)
    labels = jnp.concatenate([labels] * (outs[0].shape[2] // labels.shape[1]), axis=1)
    outs[0][block_count] = jnp.broadcast_to(labels, outs[0].shape[1:]).astype(outs[0].dtype)


def after_kernel(*refs):
    pass


def rows_of(ref, block_count, lane):
    return ref[:block_count, :, lane : lane + HD].reshape(block_count * BLK, HD)


def allowed_bias(label_ref, hop, seg_row):
    row_count = seg_row.shape[1]
    square = (row_count, row_count)
    labels = label_ref[label_ref.shape[0] - 1][:1, :row_count].astype(jnp.float32)
    labels = jnp.transpose(jnp.broadcast_to(labels, square))
    allowed = labels == seg_row.astype(jnp.float32)
    if hop == 0:
        key_pos = lax.broadcasted_iota(jnp.int32, square, 0)
        query_pos = lax.broadcasted_iota(jnp.int32, square, 1)
        allowed = allowed & (key_pos <= query_pos)
    else:
        allowed = allowed & (lax.axis_index("ctx") >= hop)
    return jnp.where(allowed, 0.0, NEG)


def score(keys, query_ref, head):
    here = slice(head * HD, (head + 1) * HD)
    query = query_ref[:, :, here].reshape(query_ref.shape[0] * BLK, HD)
    return lax.dot_general(keys, query, (((1,), (1,)), ((), ())), preferred_element_type=jnp.float32)


def attend_share(share, weight_ref, query_ref, parts, out_ref, bias_ref):
    block_count = query_ref.shape[0]
    before = sum(SHARES[:share])
    reward = jnp.zeros((block_count * BLK, HD), jnp.float32)
    for index in range(SHARES[share]):
        lane = index * HD
        keys = jnp.concatenate([rows_of(part, block_count, lane) for part in parts], axis=0)
        lane = (SHARES[share] + index) * HD
        values = jnp.concatenate([rows_of(part, block_count, lane) for part in parts], axis=0)
        values = jnp.transpose(values)
        heads = range((before + index) * GROUP, (before + index + 1) * GROUP)
        scores = [score(keys, query_ref, head) + bias_ref[...] for head in heads]
        tops = [jnp.max(each, axis=0, keepdims=True) for each in scores]
        weights = [jnp.exp2((each - top) * FACTOR) for each, top in zip(scores, tops)]
        totals = [jnp.sum(each, axis=0, keepdims=True) for each in weights]
        mixed = [
            jnp.dot(values, each.astype(jnp.bfloat16), preferred_element_type=jnp.float32) for each in weights
        ]
        mixed = [each * (1.0 / total) for each, total in zip(mixed, totals)]
        attended = [jnp.transpose(each.astype(jnp.bfloat16)) for each in mixed]
        for head, each in zip(heads, attended):
            first = (head - before * GROUP) * HD
            out_ref[:, first : first + HD] = each
            reward = reward + each.astype(jnp.float32) * weight_ref[:, head * HD : (head + 1) * HD]
    return reward


def first_kernel(bins_ref, seg_ref, weight_ref, query_ref, *rest):
    parts, (out_ref, reward_ref, bias_ref, bin_ref) = rest[:-4], rest[-4:]
    row_count = seg_ref.shape[1]
    for hop, part in enumerate(parts):
        bias_ref[hop * row_count : (hop + 1) * row_count, :] = allowed_bias(part, hop, seg_ref[...])
    reward_ref[...] = attend_share(0, weight_ref, query_ref, parts, out_ref, bias_ref)
    lane = lax.broadcasted_iota(jnp.int32, (1, bin_ref.shape[1]), 1)
    for seg in range(SEGS):
        bin_ref[seg : seg + 1, :] = jnp.where(lane == bins_ref[0, seg], 1.0, 0.0)


def last_kernel(seg_ref, weight_ref, query_ref, before_ref, reward_ref, bias_ref, bin_ref, *rest):
    parts, (out_ref, hist_ref) = rest[:-2], rest[-2:]
    row_count = seg_ref.shape[1]
    square = (row_count, row_count)
    seg_row = seg_ref[...]
    reward = reward_ref[...] + attend_share(1, weight_ref, query_ref, parts, out_ref, bias_ref)

    seg_col = jnp.transpose(jnp.broadcast_to(seg_row, square))
    after = jnp.concatenate([seg_row[:, 1:], seg_row[:, row_count - 1 :]], axis=1)
    after_col = jnp.transpose(jnp.broadcast_to(after, square))
    row_reward = jnp.sum(reward, axis=1, keepdims=True)
    kept = jnp.where(seg_col != after_col, row_reward, 0.0)
    label = lax.broadcasted_iota(jnp.int32, square, 1)
    by_seg = jnp.sum(jnp.where(seg_col == label, kept, 0.0), axis=0, keepdims=True)
    hist = jnp.zeros((1, BINS), jnp.float32)
    last_bin = jnp.zeros((1, BINS), jnp.float32)
    last_seg = seg_row[:, row_count - 1 :]
    for seg in range(SEGS):
        bin_of = bin_ref[seg : seg + 1, :]
        hist = hist + bin_of * by_seg[:, seg : seg + 1]
        last_bin = last_bin + jnp.where(last_seg == seg, bin_of, 0.0)
    bin_id = lax.broadcasted_iota(jnp.int32, (1, BINS), 1).astype(jnp.float32)
    last_bin = jnp.sum(last_bin * bin_id, axis=1, keepdims=True)
    lane = lax.broadcasted_iota(jnp.int32, (1, HD), 1)
    notes = jnp.where(lane == 0, row_reward[row_count - 1 :, :], 0.0)
    notes = notes + jnp.where(lane == 1, last_bin, 0.0)
    notes = notes + jnp.where(lane == 2, seg_row[:, :1].astype(jnp.float32), 0.0)
    notes = notes + jnp.where(lane == 3, last_seg.astype(jnp.float32), 0.0)
    hist_ref[...] = jnp.broadcast_to(jnp.concatenate([hist, notes], axis=1), hist_ref.shape)


def total_kernel(ctx_count, rows_ref, out_ref):
    device_count = rows_ref.shape[0]
    notes = rows_ref[:, BINS:]
    reward, bin_of, first, last = (notes[:, k : k + 1] for k in range(4))
    following = jnp.concatenate([first[1:], first[:1]], axis=0)
    device = lax.broadcasted_iota(jnp.int32, (device_count, 1), 0)
    ends = (following != last) | (lax.rem(device, ctx_count) == ctx_count - 1)
    bin_id = lax.broadcasted_iota(jnp.int32, (device_count, BINS), 1).astype(jnp.float32)
    extra = jnp.where((bin_id == bin_of) & ends, reward, 0.0)
    out_ref[...] = jnp.sum(rows_ref[:, :BINS] + extra, axis=0, keepdims=True)


def local(roll_query, roll_keys, roll_values, pack_dest, segment_ids, reward_bins, reward_weight):
    dp_count = lax.axis_size("dp")
    ctx_count = lax.axis_size("ctx")
    row_count = roll_query.shape[1]
    q_width = roll_query.shape[2]
    kv_width = roll_keys.shape[2]
    block_count = row_count // BLK
    cap = (block_count + dp_count - 1) // dp_count
    slot_count = dp_count * cap
    piece_count = dp_count // 2
    reach = row_count * ctx_count // 2
    hop_count = min(ctx_count - 1, (reach - 1 + row_count - 1) // row_count)
    device_count = dp_count * ctx_count
    smem = pl.BlockSpec(memory_space=pltpu.SMEM)
    vmem = pl.BlockSpec(memory_space=pltpu.VMEM)
    hbm = pl.BlockSpec(memory_space=pl.ANY)

    def across(array, distance):
        return lax.ppermute(array, "dp", [(i, i ^ distance) for i in range(dp_count)])

    half = jax.ShapeDtypeStruct((piece_count * cap, BLK, q_width), jnp.bfloat16)
    sorted_kv, same_query, other_query = pl.pallas_call(
        lambda *refs: sort_kernel(cap, piece_count, *refs),
        out_shape=[jax.ShapeDtypeStruct((slot_count, BLK, 2 * kv_width), jnp.bfloat16), half, half],
        in_specs=[hbm] * 4,
        out_specs=[hbm] * 3,
        scratch_shapes=[
            pltpu.SMEM((dp_count, block_count), jnp.int32),
            pltpu.SMEM((slot_count,), jnp.int32),
            pltpu.SMEM((dp_count,), jnp.int32),
            pltpu.SMEM((slot_count,), jnp.int32),
            pltpu.VMEM((block_count, BLK, kv_width), jnp.bfloat16),
            pltpu.VMEM((block_count, BLK, kv_width), jnp.bfloat16),
            pltpu.VMEM((block_count, BLK, q_width), jnp.bfloat16),
            pltpu.VMEM((slot_count, BLK, 2 * kv_width), jnp.bfloat16),
            pltpu.SemaphoreType.DMA((4,)),
            pltpu.SemaphoreType.DMA((slot_count + 1,)),
        ],
        compiler_params=params(60),
        name="sort",
    )(
        pack_dest,
        roll_keys.reshape(block_count, BLK, kv_width),
        roll_values.reshape(block_count, BLK, kv_width),
        roll_query.reshape(block_count, BLK, q_width),
    )
    got_kv = lax.all_to_all(
        sorted_kv.reshape(dp_count, cap * BLK, 2 * kv_width), "dp", split_axis=0, concat_axis=0, tiled=True
    ).reshape(slot_count, BLK, 2 * kv_width)

    pieces = pl.pallas_call(
        lambda *refs: merge_query_kernel(cap, piece_count, *refs),
        out_shape=[jax.ShapeDtypeStruct((2 * cap, BLK, q_width), jnp.bfloat16)] * piece_count,
        in_specs=[vmem] * 2,
        out_specs=[vmem] * piece_count,
        compiler_params=params(16),
        name="merge_query",
    )(same_query, across(other_query, 1))
    got_query = [pieces[0]] + [across(pieces[i], 2 * i) for i in range(1, piece_count)]
    query = pl.pallas_call(
        lambda *refs: unsort_query_kernel(cap, piece_count, *refs),
        out_shape=jax.ShapeDtypeStruct((block_count, BLK, q_width), jnp.bfloat16),
        in_specs=[smem] + [vmem] * piece_count,
        out_specs=vmem,
        scratch_shapes=[pltpu.SMEM((slot_count,), jnp.int32)],
        compiler_params=params(16),
        name="unsort_query",
    )(pack_dest, *got_query)

    own = pl.pallas_call(
        lambda *refs: unsort_kv_kernel(cap, *refs),
        out_shape=[
            jax.ShapeDtypeStruct((block_count + (share == 0), BLK, 2 * groups * HD), jnp.bfloat16)
            for share, groups in enumerate(SHARES)
        ],
        in_specs=[smem, vmem, vmem],
        out_specs=[vmem] * len(SHARES),
        scratch_shapes=[pltpu.SMEM((slot_count,), jnp.int32)],
        compiler_params=params(16),
        cost_estimate=cost(23000000000, 0),
        name="unsort_kv",
    )(pack_dest, segment_ids, got_kv)
    parts = [own]
    forward = [(i, i + 1) for i in range(ctx_count - 1)]
    for _ in range(hop_count):
        arrays = list(parts[-1])
        if len(parts) == hop_count:
            arrays[-1] = pl.pallas_call(
                after_kernel,
                out_shape=jax.ShapeDtypeStruct(arrays[-1].shape, arrays[-1].dtype),
                in_specs=[hbm] * (1 + (piece_count - 1)),
                out_specs=hbm,
                input_output_aliases={0: 0},
                compiler_params=params(1),
                name="after_query",
            )(arrays[-1], *got_query[1:])
        parts.append([lax.ppermute(array, "ctx", forward) for array in arrays])

    weight_row = reward_weight.reshape(1, q_width)
    out_shape = jax.ShapeDtypeStruct((row_count, q_width), jnp.bfloat16)
    part_count = len(parts)
    first_width, last_width = (groups * GROUP * HD for groups in SHARES)
    attended, reward, bias, bin_of = pl.pallas_call(
        first_kernel,
        grid=(1,),
        out_shape=(
            out_shape,
            jax.ShapeDtypeStruct((row_count, HD), jnp.float32),
            jax.ShapeDtypeStruct((part_count * row_count, row_count), jnp.float32),
            jax.ShapeDtypeStruct((SEGS, BINS), jnp.float32),
        ),
        in_specs=[smem] + [vmem] * (3 + part_count),
        out_specs=(pl.BlockSpec((row_count, first_width), lambda i: (0, 0)), vmem, vmem, vmem),
        compiler_params=params(16),
        name="first_share",
    )(reward_bins, segment_ids, weight_row, query, *[part[0] for part in parts])
    attended, hist_rows = pl.pallas_call(
        last_kernel,
        grid=(1,),
        out_shape=(out_shape, jax.ShapeDtypeStruct((device_count, BINS + HD), jnp.float32)),
        in_specs=[vmem] * 3 + [hbm] + [vmem] * (3 + part_count),
        out_specs=(
            pl.BlockSpec((row_count, last_width), lambda i: (0, first_width // last_width)),
            vmem,
        ),
        input_output_aliases={3: 0},
        compiler_params=params(16),
        name="last_share",
    )(segment_ids, weight_row, query, attended, reward, bias, bin_of, *[part[1] for part in parts])
    gathered = lax.all_to_all(hist_rows, ("dp", "ctx"), split_axis=0, concat_axis=0, tiled=True)
    total = pl.pallas_call(
        lambda *refs: total_kernel(ctx_count, *refs),
        out_shape=jax.ShapeDtypeStruct((1, BINS), jnp.float32),
        in_specs=[vmem],
        out_specs=vmem,
        compiler_params=params(16),
        name="total",
    )(gathered)
    return attended.reshape(1, row_count, q_width), total.reshape(BINS)


def solution(mesh):
    in_specs = (
        P("dp", "ctx", None),
        P("dp", "ctx", None),
        P("dp", "ctx", None),
        P(None, "ctx"),
        P("dp", "ctx"),
        P("dp", None),
        P(),
    )
    out_specs = (P("dp", "ctx", None), P())
    return jax.shard_map(local, mesh=mesh, in_specs=in_specs, out_specs=out_specs, check_vma=False)
```

time: 56.6 us -> 51.4 us (0.908)
  starting transfers between devices: 15.7 us -> 23.6 us
  waiting for transfers between devices: 11.1 us -> 3.7 us
  local copies, waits for them, and re-layouts: 3.01 us -> 0.75 us
  blocking collectives: 13.3 us -> 11.4 us
  Pallas kernels: 12.3 us -> 10.8 us
    ppermute x2 -> x4, starting transfers between devices: 6.99 us -> 14.6 us  [local(): parts.append([lax.ppermute(array, 'ctx', forward) for array in arrays])]
    ppermute x4, waiting for transfers between devices: 6.15 us -> 0.01 us  [across(): lax.ppermute(array, 'dp', [(i, i ^ distance) for i in range(dp_count)])]
    ppermute x2 -> x4, waiting for transfers between devices: 3.26 us -> 0.01 us  [local(): parts.append([lax.ppermute(array, 'ctx', forward) for array in arrays])]
    unnamed x15 -> x12, local copies, waits for them, and re-layouts: 2.92 us -> 0.67 us
    all_to_all x1, waiting for transfers between devices: 1.66 us -> 3.68 us  [local(): lax.all_to_all(sorted_kv.reshape(dp_count, cap * BLK, 2 * kv_width), 'dp'...]
    all_to_all x1, blocking collectives: 13.3 us -> 11.4 us  [local(): lax.all_to_all(hist_rows, ('dp', 'ctx'), split_axis=0, concat_axis=0, til...]
    pallas_call x7 -> x6, Pallas kernels: 10.5 us -> 9.01 us  [the longest x1 3 us: local(): pl.pallas_call(first_kernel, grid=(1,), out_shape=(out_shape, jax.ShapeDt...]
    ppermute x4, starting transfers between devices: 3.56 us -> 4.14 us  [across(): lax.ppermute(array, 'dp', [(i, i ^ distance) for i in range(dp_count)])]
  transfers between devices with their start and end apart: 7 -> 9, of which waited for: 4 -> 1; matrix products, arithmetic and copies ran while one was open for 0% -> 0% of each run, Pallas kernels for 12% -> 10%
where the time goes in v4:
time: 51.4 us; the launch traced here: 51 us
  starting transfers between devices  23.6 us (46%)
  blocking collectives  11.4 us (22%)
  Pallas kernels  10.8 us (21%)
  waiting for transfers between devices  3.7 us (7%)
  between operations  0.82 us (2%)
  local copies, waits for them, and re-layouts  0.75 us (1%)
    ppermute x4, starting transfers between devices, local(): parts.append([lax.ppermute(array, 'ctx', forward) for array in arrays])  14.6 us
    all_to_all x1, blocking collectives, local(): lax.all_to_all(hist_rows, ('dp', 'ctx'), split_axis=0, concat_axis=0, til...  11.4 us
    all_to_all x1, starting transfers between devices, local(): lax.all_to_all(sorted_kv.reshape(dp_count, cap * BLK, 2 * kv_width), 'dp'...  4.87 us
    ppermute x4, starting transfers between devices, across(): lax.ppermute(array, 'dp', [(i, i ^ distance) for i in range(dp_count)])  4.14 us
    all_to_all x1, waiting for transfers between devices, local(): lax.all_to_all(sorted_kv.reshape(dp_count, cap * BLK, 2 * kv_width), 'dp'...  3.68 us
    pallas_call x1, Pallas kernels, local(): pl.pallas_call(first_kernel, grid=(1,), out_shape=(out_shape, jax.ShapeDt...  3 us
    pallas_call x1, Pallas kernels, local(): pl.pallas_call(lambda *refs: sort_kernel(cap, piece_count, *refs), out_sh...  2.5 us
    pallas_call x1, Pallas kernels, local(): pl.pallas_call(last_kernel, grid=(1,), out_shape=(out_shape, jax.ShapeDty...  2.43 us
  transfers between devices with their start and end apart: 9, of which 1 were waited for; matrix products, arithmetic and copies ran while one was open for 0% of the time, Pallas kernels for 10%

profile of v4, /device:TPU:0, one launch (start us, length us, event | category | flops | bytes accessed | tf_op | source)
XLA Modules:
  0.0 51.0 jit_solution(3394437385518789738)
XLA Ops:
  0.6 2.5 %sort.1 = (bf16[16,8,1024]{2,1,0:T(8,128)(2,1)}, bf16[8,8,4096]{2,1,0:T(8,128)(2,1)}, bf16[8,8,4096]{2,1,0:T(8,128)(2,1)}) custom-call(s32[8,16]{1,0:T(8,128)} %refs_0_.5, bf16[16,8,512]{2,1,0:T(8,128)(2,1)} %bitcast.20, bf16[16,8,512]{2,1,0:T(8,128)(2,1)} %bitcast.21, bf16[16,8,4096]{2,1,0:T(8,128)(2,1)} %bitcast.17), custom_call_target="tpu_custom_call" | custom-call | tf_op jit(solution)/shard_map/sort/pallas_call | solution.py:262
  3.1 0.0 copy-start
  3.2 0.5 %collective-permute-start = (bf16[8,8,4096]{2,1,0:T(8,128)(2,1)}, bf16[8,8,4096]{2,1,0:T(8,128)(2,1)S(1)}, u32[]{:S(2)}, u32[]{:S(2)}) collective-permute-start(bf16[8,8,4096]{2,1,0:T(8,128)(2,1)} %get-tuple-element.18), channel_id=1, source_target_pairs={{0,4},{4,0},{8,12},{12,8},{16,20},{20,16},{24,28},{28,24},{1,5},{5... | collective-permute-start | bytes 1572872 | tf_op jit(solution)/shard_map/ppermute | solution.py:259
  3.7 4.9 %all-to-all-start = ((bf16[8,16,1024]{2,1,0:T(8,128)(2,1)}), bf16[8,16,1024]{2,1,0:T(8,128)(2,1)S(1)}, u32[]{:S(2)}, u32[]{:S(2)}) async-start(bf16[8,16,1024]{2,1,0:T(8,128)(2,1)} %bitcast.19), calls=%async_computation | async-start | bytes 524288 | tf_op jit(solution)/shard_map/all_to_all | solution.py:287
  8.5 0.0 collective-permute-done.refs_1_
  8.6 0.1 merge_query.1
  8.6 0.0 copy-start.2
  8.7 2.1 %collective-permute-start.1 = (bf16[4,8,4096]{2,1,0:T(8,128)(2,1)S(1)}, bf16[4,8,4096]{2,1,0:T(8,128)(2,1)S(1)}, u32[]{:S(2)}, u32[]{:S(2)}) collective-permute-start(bf16[4,8,4096]{2,1,0:T(8,128)(2,1)S(1)} %get-tuple-element.20), channel_id=1, source_target_pairs={{0,8},{4,12},{8,0},{12,4},{16,24},{20,28},{24,16},{28,20},{1,9},{5... | collective-permute-start | bytes 786440 | tf_op jit(solution)/shard_map/ppermute | solution.py:259
  10.7 1.5 %collective-permute-start.2 = (bf16[4,8,4096]{2,1,0:T(8,128)(2,1)S(1)}, bf16[4,8,4096]{2,1,0:T(8,128)(2,1)S(1)}, u32[]{:S(2)}, u32[]{:S(2)}) collective-permute-start(bf16[4,8,4096]{2,1,0:T(8,128)(2,1)S(1)} %get-tuple-element.21), channel_id=1, source_target_pairs={{0,16},{4,20},{8,24},{12,28},{16,0},{20,4},{24,8},{28,12},{1,17},{... | collective-permute-start | bytes 786440 | tf_op jit(solution)/shard_map/ppermute | solution.py:259
  12.2 0.1 collective-permute-start.3
  12.3 3.7 %all-to-all-done = bf16[8,16,1024]{2,1,0:T(8,128)(2,1)S(1)} async-done(((bf16[8,16,1024]{2,1,0:T(8,128)(2,1)}), bf16[8,16,1024]{2,1,0:T(8,128)(2,1)S(1)}, u32[]{:S(2)}, u32[]{:S(2)}) %all-to-all-start) | async-done | bytes 262176 | tf_op jit(solution)/shard_map/all_to_all | solution.py:287
  16.0 1.0 %unsort_kv.1 = (bf16[17,8,512]{2,1,0:T(8,128)(2,1)S(1)}, bf16[16,8,512]{2,1,0:T(8,128)(2,1)S(1)}) custom-call(s32[8,16]{1,0:T(8,128)S(1)} %copy-done.2, s32[1,128]{1,0:T(1,128)S(1)} %copy-done.3, bf16[16,8,1024]{2,1,0:T(8,128)(2,1)S(1)} %bitcast.13), custom_call_target="tpu_custom_call" | custom-call | flops 23000000512 | tf_op jit(solution)/shard_map/unsort_kv/pallas_call | solution.py:310
  17.0 3.5 %collective-permute-start.4 = (bf16[17,8,512]{2,1,0:T(8,128)(2,1)S(1)}, bf16[17,8,512]{2,1,0:T(8,128)(2,1)S(1)}, u32[]{:S(2)}, u32[]{:S(2)}) collective-permute-start(bf16[17,8,512]{2,1,0:T(8,128)(2,1)S(1)} %get-tuple-element.24.rest_0_), channel_id=1, source_target_pairs={{0,1},{1,2},{2,3},{4,5},{5,6},{6,7},{8,9},{9,10},{10,11},{12,13},{... | collective-permute-start | bytes 417800 | tf_op jit(solution)/shard_map/ppermute | solution.py:337
  20.5 3.5 %collective-permute-start.6 = (bf16[16,8,512]{2,1,0:T(8,128)(2,1)S(1)}, bf16[16,8,512]{2,1,0:T(8,128)(2,1)S(1)}, u32[]{:S(2)}, u32[]{:S(2)}) collective-permute-start(bf16[16,8,512]{2,1,0:T(8,128)(2,1)S(1)} %get-tuple-element.29.rest_0_), channel_id=1, source_target_pairs={{0,1},{1,2},{2,3},{4,5},{5,6},{6,7},{8,9},{9,10},{10,11},{12,13},{... | collective-permute-start | bytes 393224 | tf_op jit(solution)/shard_map/ppermute | solution.py:337
  24.0 0.0 collective-permute-done.4.rest_1_
  24.0 4.0 %collective-permute-start.5 = (bf16[17,8,512]{2,1,0:T(8,128)(2,1)S(1)}, bf16[17,8,512]{2,1,0:T(8,128)(2,1)S(1)}, u32[]{:S(2)}, u32[]{:S(2)}) collective-permute-start(bf16[17,8,512]{2,1,0:T(8,128)(2,1)S(1)} %collective-permute-done.4.rest_1_), channel_id=1, source_target_pairs={{0,1},{1,2},{2,3},{4,5},{5,6},{6,7},{8,9},{9,10},{10,11},{12,13},{... | collective-permute-start | bytes 417800 | tf_op jit(solution)/shard_map/ppermute | solution.py:337
  28.0 0.0 collective-permute-done.6.rest_1_
  28.0 0.0 collective-permute-done.1.refs_2_.refs_1_
  28.0 0.0 collective-permute-done.2.refs_3_.refs_2_
  28.0 0.0 collective-permute-done.3.refs_4_.refs_3_
  28.0 3.6 %collective-permute-start.7 = (bf16[16,8,512]{2,1,0:T(8,128)(2,1)S(1)}, bf16[16,8,512]{2,1,0:T(8,128)(2,1)S(1)}, u32[]{:S(2)}, u32[]{:S(2)}) collective-permute-start(bf16[16,8,512]{2,1,0:T(8,128)(2,1)S(1)} %after_query.1), channel_id=1, source_target_pairs={{0,1},{1,2},{2,3},{4,5},{5,6},{6,7},{8,9},{9,10},{10,11},{12,13},{... | collective-permute-start | bytes 393224 | tf_op jit(solution)/shard_map/ppermute | solution.py:337
  31.6 0.0 copy-start.1
  31.7 1.0 %unsort_query.1.query_ref = bf16[16,8,4096]{2,1,0:T(8,128)(2,1)S(1)} custom-call(s32[8,16]{1,0:T(8,128)S(1)} %copy-done.2, bf16[4,8,4096]{2,1,0:T(8,128)(2,1)S(1)} %get-tuple-element.19.refs_1_, bf16[4,8,4096]{2,1,0:T(8,128)(2,1)S(1)} %collective-permute-done.1.refs_2_.refs_1_, bf16[4,8,4096]{2,1,0:T(8,128)(2,1)S(1)} %collective-permute-done.2.refs_3_.refs_2_, ...), custom_call_target="tpu_custom_call" | custom-call | tf_op jit(solution)/shard_map/unsort_query/pallas_call | solution.py:300
  32.7 0.0 copy-start.4
  32.7 0.0 collective-permute-done.5.rest_2_
  32.7 0.6 %copy-done.4 = s32[1,16]{1,0:T(1,128)S(1)} copy-done((s32[1,16]{1,0:T(1,128)S(1)}, s32[1,16]{1,0:T(1,128)}, u32[]{:S(2)}) %copy-start.4) | copy-done | bytes 88
  33.4 3.0 %first_share.1 = (bf16[128,4096]{1,0:T(8,128)(2,1)}, f32[128,128]{1,0:T(8,128)S(1)}, f32[384,128]{1,0:T(8,128)S(1)}, f32[16,512]{1,0:T(8,128)S(1)}) custom-call(s32[1,16]{1,0:T(1,128)S(1)} %copy-done.4, s32[1,128]{1,0:T(1,128)S(1)} %copy-done.3, f32[1,4096]{1,0:T(1,128)S(1)} %bitcast.15, bf16[16,8,4096]{2,1,0:T(8,128)(2,1)S(1)} %unsort_query.1.query_ref, ...), custom_call_target="tpu_custom_call" | custom-call | tf_op jit(solution)/shard_map/first_share/pallas_call | solution.py:343
  36.4 0.0 collective-permute-done.7.rest_2_
  36.4 2.4 %last_share.1 = (bf16[128,4096]{1,0:T(8,128)(2,1)}, f32[32,640]{1,0:T(8,128)S(1)}) custom-call(s32[1,128]{1,0:T(1,128)S(1)} %copy-done.3, f32[1,4096]{1,0:T(1,128)S(1)} %bitcast.16, bf16[16,8,4096]{2,1,0:T(8,128)(2,1)S(1)} %unsort_query.1.query_ref, bf16[128,4096]{1,0:T(8,128)(2,1)} %get-tuple-element.25.before_ref, ...), custom_call_target="tpu_custom_call", output_to_operand_aliasing={{0}: (3, {})} | custom-call | tf_op jit(solution)/shard_map/last_share/pallas_call | solution.py:357
  38.8 0.1 copy.11
  38.9 11.4 %all_to_all.16 = f32[32,1,640]{2,1,0:T(1,128)S(1)} all-to-all(f32[32,1,640]{2,1,0:T(1,128)S(1)} %copy.11), channel_id=1, replica_groups=mesh['dp'=8,'ctx'=4] {'dp','ctx'}, dimensions={0} | all-to-all | bytes 163840 | tf_op jit(solution)/shard_map/all_to_all | solution.py:370
  50.3 0.7 %total.1 = f32[1,512]{1,0:T(1,128)} custom-call(f32[32,640]{1,0:T(8,128)S(1)} %bitcast.12), custom_call_target="tpu_custom_call" | custom-call | tf_op jit(solution)/shard_map/total/pallas_call | solution.py:371
  (8 shorter events, 0.0 us)
Async XLA Ops:
  3.1 5.4 %copy-start = (bf16[8,8,4096]{2,1,0:T(8,128)(2,1)S(1)}, bf16[8,8,4096]{2,1,0:T(8,128)(2,1)}, u32[]{:S(2)}) copy-start(bf16[8,8,4096]{2,1,0:T(8,128)(2,1)} %get-tuple-element.17.refs_0_) | copy-start | bytes 1572868
  3.2 5.4 %collective-permute-start = (bf16[8,8,4096]{2,1,0:T(8,128)(2,1)}, bf16[8,8,4096]{2,1,0:T(8,128)(2,1)S(1)}, u32[]{:S(2)}, u32[]{:S(2)}) collective-permute-start(bf16[8,8,4096]{2,1,0:T(8,128)(2,1)} %get-tuple-element.18), channel_id=1, source_target_pairs={{0,4},{4,0},{8,12},{12,8},{16,20},{20,16},{24,28},{28,24},{1,5},{5... | collective-permute-start | bytes 1572872 | tf_op jit(solution)/shard_map/ppermute | solution.py:259
  3.7 12.3 %all-to-all-start = ((bf16[8,16,1024]{2,1,0:T(8,128)(2,1)}), bf16[8,16,1024]{2,1,0:T(8,128)(2,1)S(1)}, u32[]{:S(2)}, u32[]{:S(2)}) async-start(bf16[8,16,1024]{2,1,0:T(8,128)(2,1)} %bitcast.19), calls=%async_computation | async-start | bytes 524288 | tf_op jit(solution)/shard_map/all_to_all | solution.py:287
  8.6 7.3 %copy-start.2 = (s32[8,16]{1,0:T(8,128)S(1)}, s32[8,16]{1,0:T(8,128)}, u32[]{:S(2)}) copy-start(s32[8,16]{1,0:T(8,128)} %refs_0_.5) | copy-start | bytes 1540
  8.7 19.3 %collective-permute-start.1 = (bf16[4,8,4096]{2,1,0:T(8,128)(2,1)S(1)}, bf16[4,8,4096]{2,1,0:T(8,128)(2,1)S(1)}, u32[]{:S(2)}, u32[]{:S(2)}) collective-permute-start(bf16[4,8,4096]{2,1,0:T(8,128)(2,1)S(1)} %get-tuple-element.20), channel_id=1, source_target_pairs={{0,8},{4,12},{8,0},{12,4},{16,24},{20,28},{24,16},{28,20},{1,9},{5... | collective-permute-start | bytes 786440 | tf_op jit(solution)/shard_map/ppermute | solution.py:259
  10.7 17.3 %collective-permute-start.2 = (bf16[4,8,4096]{2,1,0:T(8,128)(2,1)S(1)}, bf16[4,8,4096]{2,1,0:T(8,128)(2,1)S(1)}, u32[]{:S(2)}, u32[]{:S(2)}) collective-permute-start(bf16[4,8,4096]{2,1,0:T(8,128)(2,1)S(1)} %get-tuple-element.21), channel_id=1, source_target_pairs={{0,16},{4,20},{8,24},{12,28},{16,0},{20,4},{24,8},{28,12},{1,17},{... | collective-permute-start | bytes 786440 | tf_op jit(solution)/shard_map/ppermute | solution.py:259
  12.2 3.8 %copy-start.3 = (s32[1,128]{1,0:T(1,128)S(1)}, s32[1,128]{1,0:T(1,128)}, u32[]{:S(2)}) copy-start(s32[1,128]{1,0:T(1,128)} %seg_ref.3) | copy-start | bytes 1540
  12.2 15.8 %collective-permute-start.3 = (bf16[4,8,4096]{2,1,0:T(8,128)(2,1)S(1)}, bf16[4,8,4096]{2,1,0:T(8,128)(2,1)S(1)}, u32[]{:S(2)}, u32[]{:S(2)}) collective-permute-start(bf16[4,8,4096]{2,1,0:T(8,128)(2,1)S(1)} %get-tuple-element.22), channel_id=1, source_target_pairs={{0,24},{4,28},{8,16},{12,20},{16,8},{20,12},{24,0},{28,4},{1,25},{... | collective-permute-start | bytes 786440 | tf_op jit(solution)/shard_map/ppermute | solution.py:259
  17.0 7.0 %collective-permute-start.4 = (bf16[17,8,512]{2,1,0:T(8,128)(2,1)S(1)}, bf16[17,8,512]{2,1,0:T(8,128)(2,1)S(1)}, u32[]{:S(2)}, u32[]{:S(2)}) collective-permute-start(bf16[17,8,512]{2,1,0:T(8,128)(2,1)S(1)} %get-tuple-element.24.rest_0_), channel_id=1, source_target_pairs={{0,1},{1,2},{2,3},{4,5},{5,6},{6,7},{8,9},{9,10},{10,11},{12,13},{... | collective-permute-start | bytes 417800 | tf_op jit(solution)/shard_map/ppermute | solution.py:337
  20.5 7.5 %collective-permute-start.6 = (bf16[16,8,512]{2,1,0:T(8,128)(2,1)S(1)}, bf16[16,8,512]{2,1,0:T(8,128)(2,1)S(1)}, u32[]{:S(2)}, u32[]{:S(2)}) collective-permute-start(bf16[16,8,512]{2,1,0:T(8,128)(2,1)S(1)} %get-tuple-element.29.rest_0_), channel_id=1, source_target_pairs={{0,1},{1,2},{2,3},{4,5},{5,6},{6,7},{8,9},{9,10},{10,11},{12,13},{... | collective-permute-start | bytes 393224 | tf_op jit(solution)/shard_map/ppermute | solution.py:337
  24.0 8.7 %collective-permute-start.5 = (bf16[17,8,512]{2,1,0:T(8,128)(2,1)S(1)}, bf16[17,8,512]{2,1,0:T(8,128)(2,1)S(1)}, u32[]{:S(2)}, u32[]{:S(2)}) collective-permute-start(bf16[17,8,512]{2,1,0:T(8,128)(2,1)S(1)} %collective-permute-done.4.rest_1_), channel_id=1, source_target_pairs={{0,1},{1,2},{2,3},{4,5},{5,6},{6,7},{8,9},{9,10},{10,11},{12,13},{... | collective-permute-start | bytes 417800 | tf_op jit(solution)/shard_map/ppermute | solution.py:337
  28.0 8.3 %collective-permute-start.7 = (bf16[16,8,512]{2,1,0:T(8,128)(2,1)S(1)}, bf16[16,8,512]{2,1,0:T(8,128)(2,1)S(1)}, u32[]{:S(2)}, u32[]{:S(2)}) collective-permute-start(bf16[16,8,512]{2,1,0:T(8,128)(2,1)S(1)} %after_query.1), channel_id=1, source_target_pairs={{0,1},{1,2},{2,3},{4,5},{5,6},{6,7},{8,9},{9,10},{10,11},{12,13},{... | collective-permute-start | bytes 393224 | tf_op jit(solution)/shard_map/ppermute | solution.py:337
  31.6 1.1 %copy-start.1 = (f32[4096]{0:T(1024)S(1)}, f32[4096]{0:T(1024)}, u32[]{:S(2)}) copy-start(f32[4096]{0:T(1024)} %param.13) | copy-start | bytes 49156
  32.7 0.7 %copy-start.4 = (s32[1,16]{1,0:T(1,128)S(1)}, s32[1,16]{1,0:T(1,128)}, u32[]{:S(2)}) copy-start(s32[1,16]{1,0:T(1,128)} %bins_ref.1) | copy-start | bytes 196

commit v5 on v4

--- a/solution.py
+++ b/solution.py
@@ -110,9 +110,12 @@
             out_ref[column_ref[2 * piece * cap + place]] = pieces[piece][place]
 
 
-def unsort_kv_kernel(cap, dest_ref, seg_ref, got_ref, *rest):
-    outs, column_ref = rest[:-1], rest[-1]
+def unsort_kv_kernel(cap, dest_ref, bins_ref, seg_ref, got_ref, *rest):
+    outs, (bin_ref, column_ref) = rest[:-2], rest[-2:]
     find_columns(dest_ref, column_ref, cap, False)
+    lane = lax.broadcasted_iota(jnp.int32, (1, bin_ref.shape[1]), 1)
+    for seg in range(SEGS):
+        bin_ref[seg : seg + 1, :] = jnp.where(lane == bins_ref[0, seg], 1.0, 0.0)
     block_count = got_ref.shape[0]
     for slot in range(block_count):
         column = column_ref[slot]
@@ -157,85 +160,138 @@
     return lax.dot_general(keys, query, (((1,), (1,)), ((), ())), preferred_element_type=jnp.float32)
 
 
-def attend_share(share, weight_ref, query_ref, parts, out_ref, bias_ref):
-    block_count = query_ref.shape[0]
+def attend_share(share, query_ref, parts, out_ref, bias_ref):
     before = sum(SHARES[:share])
-    reward = jnp.zeros((block_count * BLK, HD), jnp.float32)
     for index in range(SHARES[share]):
-        lane = index * HD
-        keys = jnp.concatenate([rows_of(part, block_count, lane) for part in parts], axis=0)
-        lane = (SHARES[share] + index) * HD
-        values = jnp.concatenate([rows_of(part, block_count, lane) for part in parts], axis=0)
-        values = jnp.transpose(values)
+        keys, values = keys_and_values(share, index, query_ref.shape[0], parts)
         heads = range((before + index) * GROUP, (before + index + 1) * GROUP)
-        scores = [score(keys, query_ref, head) + bias_ref[...] for head in heads]
-        tops = [jnp.max(each, axis=0, keepdims=True) for each in scores]
-        weights = [jnp.exp2((each - top) * FACTOR) for each, top in zip(scores, tops)]
-        totals = [jnp.sum(each, axis=0, keepdims=True) for each in weights]
-        mixed = [
-            jnp.dot(values, each.astype(jnp.bfloat16), preferred_element_type=jnp.float32) for each in weights
-        ]
-        mixed = [each * (1.0 / total) for each, total in zip(mixed, totals)]
-        attended = [jnp.transpose(each.astype(jnp.bfloat16)) for each in mixed]
+        scores = [score(keys, query_ref, head) for head in heads]
+        mixed = attend_rows(scores, [values] * GROUP, bias_ref[...])
+        attended = [jnp.transpose(each) for each in mixed]
         for head, each in zip(heads, attended):
             first = (head - before * GROUP) * HD
             out_ref[:, first : first + HD] = each
-            reward = reward + each.astype(jnp.float32) * weight_ref[:, head * HD : (head + 1) * HD]
-    return reward
-
-
-def first_kernel(bins_ref, seg_ref, weight_ref, query_ref, *rest):
-    parts, (out_ref, reward_ref, bias_ref, bin_ref) = rest[:-4], rest[-4:]
+
+
+def keys_and_values(share, index, block_count, parts):
+    lane = index * HD
+    keys = jnp.concatenate([rows_of(part, block_count, lane) for part in parts], axis=0)
+    lane = (SHARES[share] + index) * HD
+    values = jnp.concatenate([rows_of(part, block_count, lane) for part in parts], axis=0)
+    return keys, jnp.transpose(values)
+
+
+def attend_rows(scores, values, bias):
+    scores = [each + bias for each in scores]
+    tops = [jnp.max(each, axis=0, keepdims=True) for each in scores]
+    weights = [jnp.exp2((each - top) * FACTOR) for each, top in zip(scores, tops)]
+    totals = [jnp.sum(each, axis=0, keepdims=True) for each in weights]
+    mixed = [
+        jnp.dot(value, each.astype(jnp.bfloat16), preferred_element_type=jnp.float32)
+        for value, each in zip(values, weights)
+    ]
+    return [(each * (1.0 / total)).astype(jnp.bfloat16) for each, total in zip(mixed, totals)]
+
+
+def last_rows(seg_row):
+    row_count = seg_row.shape[1]
+    position = lax.broadcasted_iota(jnp.int32, (1, row_count), 1)
+    after = jnp.concatenate([seg_row[:, 1:], seg_row[:, :1]], axis=1)
+    is_last = (after != seg_row) | (position == row_count - 1)
+    seg = lax.broadcasted_iota(jnp.int32, (GROUP * SEGS, row_count), 0) % SEGS
+    return jnp.where((seg_row == seg) & is_last, 1.0, 0.0).astype(jnp.bfloat16)
+
+
+def end_rewards(share, end_query_ref, end_bias_ref, end_weight_ref, parts, block_count):
+    before = sum(SHARES[:share])
+    groups = range(before, before + SHARES[share])
+    held = [keys_and_values(share, group - before, block_count, parts) for group in groups]
+    scores = [
+        lax.dot_general(
+            keys, end_query_ref[group], (((1,), (1,)), ((), ())), preferred_element_type=jnp.float32
+        )
+        for group, (keys, _) in zip(groups, held)
+    ]
+    attended = attend_rows(scores, [values for _, values in held], end_bias_ref[...])
+    products = [each.astype(jnp.float32) * end_weight_ref[group] for group, each in zip(groups, attended)]
+    return sum(jnp.sum(each, axis=0, keepdims=True) for each in products)
+
+
+def first_kernel(seg_ref, weight_ref, query_ref, *rest):
+    parts, rest = rest[:-6], rest[-6:]
+    out_ref, bias_ref, end_query_ref, end_bias_ref, end_weight_ref, reward_ref = rest
     row_count = seg_ref.shape[1]
+    block_count = query_ref.shape[0]
     for hop, part in enumerate(parts):
         bias_ref[hop * row_count : (hop + 1) * row_count, :] = allowed_bias(part, hop, seg_ref[...])
-    reward_ref[...] = attend_share(0, weight_ref, query_ref, parts, out_ref, bias_ref)
-    lane = lax.broadcasted_iota(jnp.int32, (1, bin_ref.shape[1]), 1)
-    for seg in range(SEGS):
-        bin_ref[seg : seg + 1, :] = jnp.where(lane == bins_ref[0, seg], 1.0, 0.0)
-
-
-def last_kernel(seg_ref, weight_ref, query_ref, before_ref, reward_ref, bias_ref, bin_ref, *rest):
-    parts, (out_ref, hist_ref) = rest[:-2], rest[-2:]
-    row_count = seg_ref.shape[1]
-    square = (row_count, row_count)
+    chosen = last_rows(seg_ref[...])
+    end_bias_ref[...] = lax.dot_general(
+        bias_ref[...].astype(jnp.bfloat16),
+        chosen,
+        (((1,), (1,)), ((), ())),
+        preferred_element_type=jnp.float32,
+    )
+    for group in range(HK):
+        rows, weights = [], []
+        for head in range(group * GROUP, (group + 1) * GROUP):
+            here = slice(head * HD, (head + 1) * HD)
+            query = query_ref[:, :, here].reshape(row_count, HD)
+            rows.append(jnp.dot(chosen[:SEGS], query, preferred_element_type=jnp.float32))
+            weights.append(jnp.broadcast_to(weight_ref[:, here], (SEGS, HD)))
+        end_query_ref[group] = jnp.concatenate(rows, axis=0).astype(jnp.bfloat16)
+        end_weight_ref[group] = jnp.transpose(jnp.concatenate(weights, axis=0))
+    reward_ref[...] = end_rewards(0, end_query_ref, end_bias_ref, end_weight_ref, parts, block_count)
+    attend_share(0, query_ref, parts, out_ref, bias_ref)
+
+
+def ends_kernel(seg_ref, end_query_ref, end_bias_ref, end_weight_ref, reward_ref, bin_ref, *rest):
+    parts, hist_ref = rest[:-1], rest[-1]
     seg_row = seg_ref[...]
-    reward = reward_ref[...] + attend_share(1, weight_ref, query_ref, parts, out_ref, bias_ref)
-
-    seg_col = jnp.transpose(jnp.broadcast_to(seg_row, square))
-    after = jnp.concatenate([seg_row[:, 1:], seg_row[:, row_count - 1 :]], axis=1)
-    after_col = jnp.transpose(jnp.broadcast_to(after, square))
-    row_reward = jnp.sum(reward, axis=1, keepdims=True)
-    kept = jnp.where(seg_col != after_col, row_reward, 0.0)
-    label = lax.broadcasted_iota(jnp.int32, square, 1)
-    by_seg = jnp.sum(jnp.where(seg_col == label, kept, 0.0), axis=0, keepdims=True)
-    hist = jnp.zeros((1, BINS), jnp.float32)
-    last_bin = jnp.zeros((1, BINS), jnp.float32)
-    last_seg = seg_row[:, row_count - 1 :]
-    for seg in range(SEGS):
-        bin_of = bin_ref[seg : seg + 1, :]
-        hist = hist + bin_of * by_seg[:, seg : seg + 1]
-        last_bin = last_bin + jnp.where(last_seg == seg, bin_of, 0.0)
-    bin_id = lax.broadcasted_iota(jnp.int32, (1, BINS), 1).astype(jnp.float32)
-    last_bin = jnp.sum(last_bin * bin_id, axis=1, keepdims=True)
+    row_count = seg_row.shape[1]
+    block_count = row_count // BLK
+    reward = reward_ref[...] + end_rewards(
+        1, end_query_ref, end_bias_ref, end_weight_ref, parts, block_count
+    )
+    ends = reward.shape[1]
+    by_seg = jnp.transpose(jnp.broadcast_to(reward, (ends, ends)))
+    by_seg = jnp.sum(by_seg.reshape(GROUP, SEGS, ends), axis=0)
+    seg = lax.broadcasted_iota(jnp.int32, (SEGS, ends), 0)
+    first_seg, last_seg = seg_row[:, :1], seg_row[:, row_count - 1 :]
+    seg_rows = jnp.broadcast_to(seg_row, (SEGS, row_count))
+    row_seg = lax.broadcasted_iota(jnp.int32, seg_rows.shape, 0)
+    present = jnp.max(jnp.where(seg_rows == row_seg, 1, 0), axis=1, keepdims=True)
+    certain = jnp.where((present > 0) & (seg != last_seg), by_seg, 0.0)
+    bin_of = bin_ref[...]
+    hist = jnp.sum(bin_of * jnp.concatenate([certain] * (BINS // ends), axis=1), axis=0, keepdims=True)
+    last_reward = jnp.sum(jnp.where(seg == last_seg, by_seg, 0.0), axis=0, keepdims=True)
+    bin_id = lax.broadcasted_iota(jnp.int32, (SEGS, BINS), 1).astype(jnp.float32)
+    row_id = lax.broadcasted_iota(jnp.int32, (SEGS, BINS), 0)
+    last_bin = jnp.where(row_id == last_seg, bin_of * bin_id, 0.0)
+    last_bin = jnp.sum(jnp.sum(last_bin, axis=0, keepdims=True), axis=1, keepdims=True)
     lane = lax.broadcasted_iota(jnp.int32, (1, HD), 1)
-    notes = jnp.where(lane == 0, row_reward[row_count - 1 :, :], 0.0)
+    notes = jnp.where(lane == 0, last_reward, 0.0)
     notes = notes + jnp.where(lane == 1, last_bin, 0.0)
-    notes = notes + jnp.where(lane == 2, seg_row[:, :1].astype(jnp.float32), 0.0)
+    notes = notes + jnp.where(lane == 2, first_seg.astype(jnp.float32), 0.0)
     notes = notes + jnp.where(lane == 3, last_seg.astype(jnp.float32), 0.0)
-    hist_ref[...] = jnp.broadcast_to(jnp.concatenate([hist, notes], axis=1), hist_ref.shape)
+    row = jnp.concatenate([hist, notes], axis=1)
+    hist_ref[...] = jnp.broadcast_to(row.reshape(1, 1, row.shape[1]), hist_ref.shape)
+
+
+def last_kernel(query_ref, before_ref, bias_ref, *rest):
+    attend_share(1, query_ref, rest[:-1], rest[-1], bias_ref)
 
 
 def total_kernel(ctx_count, rows_ref, out_ref):
     device_count = rows_ref.shape[0]
-    notes = rows_ref[:, BINS:]
+    rows = rows_ref[...].reshape(device_count, rows_ref.shape[2])
+    notes = rows[:, BINS:]
     reward, bin_of, first, last = (notes[:, k : k + 1] for k in range(4))
     following = jnp.concatenate([first[1:], first[:1]], axis=0)
     device = lax.broadcasted_iota(jnp.int32, (device_count, 1), 0)
     ends = (following != last) | (lax.rem(device, ctx_count) == ctx_count - 1)
     bin_id = lax.broadcasted_iota(jnp.int32, (device_count, BINS), 1).astype(jnp.float32)
     extra = jnp.where((bin_id == bin_of) & ends, reward, 0.0)
-    out_ref[...] = jnp.sum(rows_ref[:, :BINS] + extra, axis=0, keepdims=True)
+    out_ref[...] = jnp.sum(rows[:, :BINS] + extra, axis=0, keepdims=True)
 
 
 def local(roll_query, roll_keys, roll_values, pack_dest, segment_ids, reward_bins, reward_weight):
@@ -307,19 +363,20 @@
         name="unsort_query",
     )(pack_dest, *got_query)
 
-    own = pl.pallas_call(
+    *own, bin_of = pl.pallas_call(
         lambda *refs: unsort_kv_kernel(cap, *refs),
         out_shape=[
             jax.ShapeDtypeStruct((block_count + (share == 0), BLK, 2 * groups * HD), jnp.bfloat16)
             for share, groups in enumerate(SHARES)
-        ],
-        in_specs=[smem, vmem, vmem],
-        out_specs=[vmem] * len(SHARES),
+        ]
+        + [jax.ShapeDtypeStruct((SEGS, BINS), jnp.float32)],
+        in_specs=[smem, smem, vmem, vmem],
+        out_specs=[vmem] * (len(SHARES) + 1),
         scratch_shapes=[pltpu.SMEM((slot_count,), jnp.int32)],
         compiler_params=params(16),
         cost_estimate=cost(23000000000, 0),
         name="unsort_kv",
-    )(pack_dest, segment_ids, got_kv)
+    )(pack_dest, reward_bins, segment_ids, got_kv)
     parts = [own]
     forward = [(i, i + 1) for i in range(ctx_count - 1)]
     for _ in range(hop_count):
@@ -328,45 +385,53 @@
             arrays[-1] = pl.pallas_call(
                 after_kernel,
                 out_shape=jax.ShapeDtypeStruct(arrays[-1].shape, arrays[-1].dtype),
-                in_specs=[hbm] * (1 + (piece_count - 1)),
+                in_specs=[hbm] * 2,
                 out_specs=hbm,
                 input_output_aliases={0: 0},
                 compiler_params=params(1),
                 name="after_query",
-            )(arrays[-1], *got_query[1:])
+            )(arrays[-1], query)
         parts.append([lax.ppermute(array, "ctx", forward) for array in arrays])
 
     weight_row = reward_weight.reshape(1, q_width)
     out_shape = jax.ShapeDtypeStruct((row_count, q_width), jnp.bfloat16)
     part_count = len(parts)
     first_width, last_width = (groups * GROUP * HD for groups in SHARES)
-    attended, reward, bias, bin_of = pl.pallas_call(
+    ends = GROUP * SEGS
+    attended, bias, *end_state = pl.pallas_call(
         first_kernel,
         grid=(1,),
         out_shape=(
             out_shape,
-            jax.ShapeDtypeStruct((row_count, HD), jnp.float32),
             jax.ShapeDtypeStruct((part_count * row_count, row_count), jnp.float32),
-            jax.ShapeDtypeStruct((SEGS, BINS), jnp.float32),
+            jax.ShapeDtypeStruct((HK, ends, HD), jnp.bfloat16),
+            jax.ShapeDtypeStruct((part_count * row_count, ends), jnp.float32),
+            jax.ShapeDtypeStruct((HK, HD, ends), jnp.float32),
+            jax.ShapeDtypeStruct((1, ends), jnp.float32),
         ),
-        in_specs=[smem] + [vmem] * (3 + part_count),
-        out_specs=(pl.BlockSpec((row_count, first_width), lambda i: (0, 0)), vmem, vmem, vmem),
+        in_specs=[vmem] * (3 + part_count),
+        out_specs=(pl.BlockSpec((row_count, first_width), lambda i: (0, 0)),) + (vmem,) * 5,
         compiler_params=params(16),
         name="first_share",
-    )(reward_bins, segment_ids, weight_row, query, *[part[0] for part in parts])
-    attended, hist_rows = pl.pallas_call(
+    )(segment_ids, weight_row, query, *[part[0] for part in parts])
+    hist_rows = pl.pallas_call(
+        ends_kernel,
+        out_shape=jax.ShapeDtypeStruct((device_count, 1, BINS + HD), jnp.float32),
+        in_specs=[vmem] * (6 + part_count),
+        out_specs=vmem,
+        compiler_params=params(16),
+        name="ends",
+    )(segment_ids, *end_state, bin_of, *[part[1] for part in parts])
+    attended = pl.pallas_call(
         last_kernel,
         grid=(1,),
-        out_shape=(out_shape, jax.ShapeDtypeStruct((device_count, BINS + HD), jnp.float32)),
-        in_specs=[vmem] * 3 + [hbm] + [vmem] * (3 + part_count),
-        out_specs=(
-            pl.BlockSpec((row_count, last_width), lambda i: (0, first_width // last_width)),
-            vmem,
-        ),
-        input_output_aliases={3: 0},
+        out_shape=out_shape,
+        in_specs=[vmem, hbm] + [vmem] * (1 + part_count),
+        out_specs=pl.BlockSpec((row_count, last_width), lambda i: (0, first_width // last_width)),
+        input_output_aliases={1: 0},
         compiler_params=params(16),
         name="last_share",
-    )(segment_ids, weight_row, query, attended, reward, bias, bin_of, *[part[1] for part in parts])
+    )(query, attended, bias, *[part[1] for part in parts])
     gathered = lax.all_to_all(hist_rows, ("dp", "ctx"), split_axis=0, concat_axis=0, tiled=True)
     total = pl.pallas_call(
         lambda *refs: total_kernel(ctx_count, *refs),

time: 51.4 us -> 49.7 us (0.967)
  blocking collectives: 11.4 us -> 0 us
  waiting for transfers between devices: 3.7 us -> 8.96 us
  starting transfers between devices: 23.6 us -> 27.2 us
  Pallas kernels: 10.8 us -> 12.2 us
  local copies, waits for them, and re-layouts: 0.75 us -> 0.04 us
    all_to_all x1 -> x0, blocking collectives: 11.4 us -> none  [local(): lax.all_to_all(hist_rows, ('dp', 'ctx'), split_axis=0, concat_axis=0, til...]
    all_to_all x0 -> x1, waiting for transfers between devices: none -> 5.26 us  [local(): lax.all_to_all(hist_rows, ('dp', 'ctx'), split_axis=0, concat_axis=0, til...]
    all_to_all x0 -> x1, starting transfers between devices: none -> 3.65 us  [local(): lax.all_to_all(hist_rows, ('dp', 'ctx'), split_axis=0, concat_axis=0, til...]
    pallas_call x1 -> x2, Pallas kernels: 2.43 us -> 3.68 us  [the longest x1 2.45 us: local(): pl.pallas_call(last_kernel, grid=(1,), out_shape=out_shape, in_specs=[vme...]
    unnamed x12 -> x11, local copies, waits for them, and re-layouts: 0.67 us -> 0.04 us
  transfers between devices with their start and end apart: 9 -> 10, of which waited for: 1 -> 2; matrix products, arithmetic and copies ran while one was open for 0% -> 0% of each run, Pallas kernels for 10% -> 16%
where the time goes in v5:
time: 49.7 us; the launch traced here: 49.3 us
  starting transfers between devices  27.2 us (55%)
  Pallas kernels  12.2 us (25%)
  waiting for transfers between devices  8.96 us (18%)
  between operations  0.82 us (2%)
    ppermute x4, starting transfers between devices, local(): parts.append([lax.ppermute(array, 'ctx', forward) for array in arrays])  14.6 us
    all_to_all x1, waiting for transfers between devices, local(): lax.all_to_all(hist_rows, ('dp', 'ctx'), split_axis=0, concat_axis=0, til...  5.26 us
    all_to_all x1, starting transfers between devices, local(): lax.all_to_all(sorted_kv.reshape(dp_count, cap * BLK, 2 * kv_width), 'dp'...  4.87 us
    ppermute x4, starting transfers between devices, across(): lax.ppermute(array, 'dp', [(i, i ^ distance) for i in range(dp_count)])  4.14 us
    all_to_all x1, waiting for transfers between devices, local(): lax.all_to_all(sorted_kv.reshape(dp_count, cap * BLK, 2 * kv_width), 'dp'...  3.68 us
    all_to_all x1, starting transfers between devices, local(): lax.all_to_all(hist_rows, ('dp', 'ctx'), split_axis=0, concat_axis=0, til...  3.65 us
    pallas_call x1, Pallas kernels, local(): pl.pallas_call(first_kernel, grid=(1,), out_shape=(out_shape, jax.ShapeDt...  3.17 us
    pallas_call x1, Pallas kernels, local(): pl.pallas_call(lambda *refs: sort_kernel(cap, piece_count, *refs), out_sh...  2.5 us
  transfers between devices with their start and end apart: 10, of which 2 were waited for; matrix products, arithmetic and copies ran while one was open for 0% of the time, Pallas kernels for 16%

profile of v5, /device:TPU:0, one launch (start us, length us, event | category | flops | bytes accessed | tf_op | source)
XLA Modules:
  0.0 49.3 jit_solution(12809341069021576234)
XLA Ops:
  0.6 2.5 %sort.1 = (bf16[16,8,1024]{2,1,0:T(8,128)(2,1)}, bf16[8,8,4096]{2,1,0:T(8,128)(2,1)}, bf16[8,8,4096]{2,1,0:T(8,128)(2,1)}) custom-call(s32[8,16]{1,0:T(8,128)} %refs_0_.5, bf16[16,8,512]{2,1,0:T(8,128)(2,1)} %bitcast.13, bf16[16,8,512]{2,1,0:T(8,128)(2,1)} %bitcast.14, bf16[16,8,4096]{2,1,0:T(8,128)(2,1)} %bitcast.11), custom_call_target="tpu_custom_call" | custom-call | tf_op jit(solution)/shard_map/sort/pallas_call | solution.py:318
  3.1 0.0 copy-start
  3.2 0.5 %collective-permute-start = (bf16[8,8,4096]{2,1,0:T(8,128)(2,1)}, bf16[8,8,4096]{2,1,0:T(8,128)(2,1)S(1)}, u32[]{:S(2)}, u32[]{:S(2)}) collective-permute-start(bf16[8,8,4096]{2,1,0:T(8,128)(2,1)} %get-tuple-element.19), channel_id=1, source_target_pairs={{0,4},{4,0},{8,12},{12,8},{16,20},{20,16},{24,28},{28,24},{1,5},{5... | collective-permute-start | bytes 1572872 | tf_op jit(solution)/shard_map/ppermute | solution.py:315
  3.7 4.9 %all-to-all-start = ((bf16[8,16,1024]{2,1,0:T(8,128)(2,1)}), bf16[8,16,1024]{2,1,0:T(8,128)(2,1)S(1)}, u32[]{:S(2)}, u32[]{:S(2)}) async-start(bf16[8,16,1024]{2,1,0:T(8,128)(2,1)} %bitcast.12), calls=%async_computation | async-start | bytes 524288 | tf_op jit(solution)/shard_map/all_to_all | solution.py:343
  8.5 0.0 collective-permute-done.refs_1_
  8.6 0.1 merge_query.1
  8.6 0.0 copy-start.2
  8.7 2.1 %collective-permute-start.1 = (bf16[4,8,4096]{2,1,0:T(8,128)(2,1)S(1)}, bf16[4,8,4096]{2,1,0:T(8,128)(2,1)S(1)}, u32[]{:S(2)}, u32[]{:S(2)}) collective-permute-start(bf16[4,8,4096]{2,1,0:T(8,128)(2,1)S(1)} %get-tuple-element.21), channel_id=1, source_target_pairs={{0,8},{4,12},{8,0},{12,4},{16,24},{20,28},{24,16},{28,20},{1,9},{5... | collective-permute-start | bytes 786440 | tf_op jit(solution)/shard_map/ppermute | solution.py:315
  10.7 1.5 %collective-permute-start.2 = (bf16[4,8,4096]{2,1,0:T(8,128)(2,1)S(1)}, bf16[4,8,4096]{2,1,0:T(8,128)(2,1)S(1)}, u32[]{:S(2)}, u32[]{:S(2)}) collective-permute-start(bf16[4,8,4096]{2,1,0:T(8,128)(2,1)S(1)} %get-tuple-element.22), channel_id=1, source_target_pairs={{0,16},{4,20},{8,24},{12,28},{16,0},{20,4},{24,8},{28,12},{1,17},{... | collective-permute-start | bytes 786440 | tf_op jit(solution)/shard_map/ppermute | solution.py:315
  12.2 0.1 collective-permute-start.3
  12.3 3.7 %all-to-all-done = bf16[8,16,1024]{2,1,0:T(8,128)(2,1)S(1)} async-done(((bf16[8,16,1024]{2,1,0:T(8,128)(2,1)}), bf16[8,16,1024]{2,1,0:T(8,128)(2,1)S(1)}, u32[]{:S(2)}, u32[]{:S(2)}) %all-to-all-start) | async-done | bytes 262176 | tf_op jit(solution)/shard_map/all_to_all | solution.py:343
  16.0 0.0 copy-done.2
  16.0 1.0 %unsort_kv.1 = (bf16[17,8,512]{2,1,0:T(8,128)(2,1)S(1)}, bf16[16,8,512]{2,1,0:T(8,128)(2,1)S(1)}, f32[16,512]{1,0:T(8,128)S(1)}) custom-call(s32[8,16]{1,0:T(8,128)S(1)} %copy-done.2, s32[1,16]{1,0:T(1,128)S(1)} %copy-done.4, s32[1,128]{1,0:T(1,128)S(1)} %copy-done.3, bf16[16,8,1024]{2,1,0:T(8,128)(2,1)S(1)} %bitcast.8), custom_call_target="tpu_custom_call" | custom-call | flops 23000000512 | tf_op jit(solution)/shard_map/unsort_kv/pallas_call | solution.py:366
  17.0 3.5 %collective-permute-start.4 = (bf16[17,8,512]{2,1,0:T(8,128)(2,1)S(1)}, bf16[17,8,512]{2,1,0:T(8,128)(2,1)S(1)}, u32[]{:S(2)}, u32[]{:S(2)}) collective-permute-start(bf16[17,8,512]{2,1,0:T(8,128)(2,1)S(1)} %get-tuple-element.25.rest_0_), channel_id=1, source_target_pairs={{0,1},{1,2},{2,3},{4,5},{5,6},{6,7},{8,9},{9,10},{10,11},{12,13},{... | collective-permute-start | bytes 417800 | tf_op jit(solution)/shard_map/ppermute | solution.py:394
  20.5 3.5 %collective-permute-start.6 = (bf16[16,8,512]{2,1,0:T(8,128)(2,1)S(1)}, bf16[16,8,512]{2,1,0:T(8,128)(2,1)S(1)}, u32[]{:S(2)}, u32[]{:S(2)}) collective-permute-start(bf16[16,8,512]{2,1,0:T(8,128)(2,1)S(1)} %get-tuple-element.28.rest_0_), channel_id=1, source_target_pairs={{0,1},{1,2},{2,3},{4,5},{5,6},{6,7},{8,9},{9,10},{10,11},{12,13},{... | collective-permute-start | bytes 393224 | tf_op jit(solution)/shard_map/ppermute | solution.py:394
  24.0 0.0 collective-permute-done.4.rest_1_
  24.0 4.0 %collective-permute-start.5 = (bf16[17,8,512]{2,1,0:T(8,128)(2,1)S(1)}, bf16[17,8,512]{2,1,0:T(8,128)(2,1)S(1)}, u32[]{:S(2)}, u32[]{:S(2)}) collective-permute-start(bf16[17,8,512]{2,1,0:T(8,128)(2,1)S(1)} %collective-permute-done.4.rest_1_), channel_id=1, source_target_pairs={{0,1},{1,2},{2,3},{4,5},{5,6},{6,7},{8,9},{9,10},{10,11},{12,13},{... | collective-permute-start | bytes 417800 | tf_op jit(solution)/shard_map/ppermute | solution.py:394
  28.0 0.0 collective-permute-done.6.rest_1_
  28.0 0.0 collective-permute-done.1.refs_2_
  28.0 0.0 collective-permute-done.2.refs_3_
  28.0 0.0 collective-permute-done.3.refs_4_
  28.1 1.0 %unsort_query.1.query_ref.refs_1_ = bf16[16,8,4096]{2,1,0:T(8,128)(2,1)S(1)} custom-call(s32[8,16]{1,0:T(8,128)S(1)} %copy-done.2, bf16[4,8,4096]{2,1,0:T(8,128)(2,1)S(1)} %get-tuple-element.20.refs_1_, bf16[4,8,4096]{2,1,0:T(8,128)(2,1)S(1)} %collective-permute-done.1.refs_2_, bf16[4,8,4096]{2,1,0:T(8,128)(2,1)S(1)} %collective-permute-done.2.refs_3_, ...), custom_call_target="tpu_custom_call" | custom-call | tf_op jit(solution)/shard_map/unsort_query/pallas_call | solution.py:356
  29.1 0.0 copy-start.1
  29.1 3.6 %collective-permute-start.7 = (bf16[16,8,512]{2,1,0:T(8,128)(2,1)S(1)}, bf16[16,8,512]{2,1,0:T(8,128)(2,1)S(1)}, u32[]{:S(2)}, u32[]{:S(2)}) collective-permute-start(bf16[16,8,512]{2,1,0:T(8,128)(2,1)S(1)} %after_query.1), channel_id=1, source_target_pairs={{0,1},{1,2},{2,3},{4,5},{5,6},{6,7},{8,9},{9,10},{10,11},{12,13},{... | collective-permute-start | bytes 393224 | tf_op jit(solution)/shard_map/ppermute | solution.py:394
  32.7 0.0 collective-permute-done.5.rest_2_
  32.8 3.2 %first_share.1 = (bf16[128,4096]{1,0:T(8,128)(2,1)}, f32[384,128]{1,0:T(8,128)S(1)}, bf16[4,128,128]{2,1,0:T(8,128)(2,1)S(1)}, f32[384,128]{1,0:T(8,128)S(1)}, f...) custom-call(s32[1,128]{1,0:T(1,128)S(1)} %copy-done.3, f32[1,4096]{1,0:T(1,128)S(1)} %bitcast.9, ...), custom_call_target="tpu_custom_call" | custom-call | tf_op jit(solution)/shard_map/first_share/pallas_call | solution.py:401
  35.9 0.0 collective-permute-done.7.rest_2_
  35.9 1.2 %ends.1 = f32[32,1,640]{2,1,0:T(1,128)} custom-call(s32[1,128]{1,0:T(1,128)S(1)} %copy-done.3, bf16[4,128,128]{2,1,0:T(8,128)(2,1)S(1)} %get-tuple-element.29.end_query_ref, f32[384,128]{1,0:T(8,128)S(1)} %get-tuple-element.30.end_bias_ref, f32[4,128,128]{2,1,0:T(8,128)S(1)} %get-tuple-element.31.end_weight_ref, f32[1,128]{1,0:T(1,128)S(1)} %get-tuple-element.32.reward_ref, ...), custom_call_target="tpu_custom_call" | custom-call | tf_op jit(solution)/shard_map/ends/pallas_call | solution.py:417
  37.2 3.6 %all-to-all-start.1 = ((f32[32,1,640]{2,1,0:T(1,128)}), f32[32,1,640]{2,1,0:T(1,128)S(1)}, u32[]{:S(2)}, u32[]{:S(2)}) async-start(f32[32,1,640]{2,1,0:T(1,128)} %ends.1), calls=%async_computation.1 | async-start | bytes 163840 | tf_op jit(solution)/shard_map/all_to_all | solution.py:435
  40.8 2.4 %last_share.1 = bf16[128,4096]{1,0:T(8,128)(2,1)} custom-call(bf16[16,8,4096]{2,1,0:T(8,128)(2,1)S(1)} %unsort_query.1.query_ref.refs_1_, bf16[128,4096]{1,0:T(8,128)(2,1)} %get-tuple-element.26.before_ref, f32[384,128]{1,0:T(8,128)S(1)} %get-tuple-element.27.bias_ref, ...), custom_call_target="tpu_custom_call", output_to_operand_aliasing={{}: (1, {})} | custom-call | tf_op jit(solution)/shard_map/last_share/pallas_call | solution.py:425
  43.3 5.3 %all-to-all-done.1.refs_0_ = f32[32,1,640]{2,1,0:T(1,128)S(1)} async-done(((f32[32,1,640]{2,1,0:T(1,128)}), f32[32,1,640]{2,1,0:T(1,128)S(1)}, u32[]{:S(2)}, u32[]{:S(2)}) %all-to-all-start.1) | async-done | bytes 81952 | tf_op jit(solution)/shard_map/all_to_all | solution.py:435
  48.5 0.8 %total.1 = f32[1,512]{1,0:T(1,128)} custom-call(f32[32,1,640]{2,1,0:T(1,128)S(1)} %all-to-all-done.1.refs_0_), custom_call_target="tpu_custom_call" | custom-call | tf_op jit(solution)/shard_map/total/pallas_call | solution.py:436
  (8 shorter events, 0.0 us)
Async XLA Ops:
  3.1 5.4 %copy-start = (bf16[8,8,4096]{2,1,0:T(8,128)(2,1)S(1)}, bf16[8,8,4096]{2,1,0:T(8,128)(2,1)}, u32[]{:S(2)}) copy-start(bf16[8,8,4096]{2,1,0:T(8,128)(2,1)} %get-tuple-element.18.refs_0_) | copy-start | bytes 1572868
  3.2 5.4 %collective-permute-start = (bf16[8,8,4096]{2,1,0:T(8,128)(2,1)}, bf16[8,8,4096]{2,1,0:T(8,128)(2,1)S(1)}, u32[]{:S(2)}, u32[]{:S(2)}) collective-permute-start(bf16[8,8,4096]{2,1,0:T(8,128)(2,1)} %get-tuple-element.19), channel_id=1, source_target_pairs={{0,4},{4,0},{8,12},{12,8},{16,20},{20,16},{24,28},{28,24},{1,5},{5... | collective-permute-start | bytes 1572872 | tf_op jit(solution)/shard_map/ppermute | solution.py:315
  3.7 12.3 %all-to-all-start = ((bf16[8,16,1024]{2,1,0:T(8,128)(2,1)}), bf16[8,16,1024]{2,1,0:T(8,128)(2,1)S(1)}, u32[]{:S(2)}, u32[]{:S(2)}) async-start(bf16[8,16,1024]{2,1,0:T(8,128)(2,1)} %bitcast.12), calls=%async_computation | async-start | bytes 524288 | tf_op jit(solution)/shard_map/all_to_all | solution.py:343
  8.6 7.3 %copy-start.2 = (s32[8,16]{1,0:T(8,128)S(1)}, s32[8,16]{1,0:T(8,128)}, u32[]{:S(2)}) copy-start(s32[8,16]{1,0:T(8,128)} %refs_0_.5) | copy-start | bytes 1540
  8.7 19.4 %collective-permute-start.1 = (bf16[4,8,4096]{2,1,0:T(8,128)(2,1)S(1)}, bf16[4,8,4096]{2,1,0:T(8,128)(2,1)S(1)}, u32[]{:S(2)}, u32[]{:S(2)}) collective-permute-start(bf16[4,8,4096]{2,1,0:T(8,128)(2,1)S(1)} %get-tuple-element.21), channel_id=1, source_target_pairs={{0,8},{4,12},{8,0},{12,4},{16,24},{20,28},{24,16},{28,20},{1,9},{5... | collective-permute-start | bytes 786440 | tf_op jit(solution)/shard_map/ppermute | solution.py:315
  10.7 17.3 %collective-permute-start.2 = (bf16[4,8,4096]{2,1,0:T(8,128)(2,1)S(1)}, bf16[4,8,4096]{2,1,0:T(8,128)(2,1)S(1)}, u32[]{:S(2)}, u32[]{:S(2)}) collective-permute-start(bf16[4,8,4096]{2,1,0:T(8,128)(2,1)S(1)} %get-tuple-element.22), channel_id=1, source_target_pairs={{0,16},{4,20},{8,24},{12,28},{16,0},{20,4},{24,8},{28,12},{1,17},{... | collective-permute-start | bytes 786440 | tf_op jit(solution)/shard_map/ppermute | solution.py:315
  12.2 3.8 %copy-start.3 = (s32[1,128]{1,0:T(1,128)S(1)}, s32[1,128]{1,0:T(1,128)}, u32[]{:S(2)}) copy-start(s32[1,128]{1,0:T(1,128)} %seg_ref.3) | copy-start | bytes 1540
  12.2 3.8 %copy-start.4 = (s32[1,16]{1,0:T(1,128)S(1)}, s32[1,16]{1,0:T(1,128)}, u32[]{:S(2)}) copy-start(s32[1,16]{1,0:T(1,128)} %refs_1_.1) | copy-start | bytes 196
  12.2 15.8 %collective-permute-start.3 = (bf16[4,8,4096]{2,1,0:T(8,128)(2,1)S(1)}, bf16[4,8,4096]{2,1,0:T(8,128)(2,1)S(1)}, u32[]{:S(2)}, u32[]{:S(2)}) collective-permute-start(bf16[4,8,4096]{2,1,0:T(8,128)(2,1)S(1)} %get-tuple-element.23), channel_id=1, source_target_pairs={{0,24},{4,28},{8,16},{12,20},{16,8},{20,12},{24,0},{28,4},{1,25},{... | collective-permute-start | bytes 786440 | tf_op jit(solution)/shard_map/ppermute | solution.py:315
  17.0 7.0 %collective-permute-start.4 = (bf16[17,8,512]{2,1,0:T(8,128)(2,1)S(1)}, bf16[17,8,512]{2,1,0:T(8,128)(2,1)S(1)}, u32[]{:S(2)}, u32[]{:S(2)}) collective-permute-start(bf16[17,8,512]{2,1,0:T(8,128)(2,1)S(1)} %get-tuple-element.25.rest_0_), channel_id=1, source_target_pairs={{0,1},{1,2},{2,3},{4,5},{5,6},{6,7},{8,9},{9,10},{10,11},{12,13},{... | collective-permute-start | bytes 417800 | tf_op jit(solution)/shard_map/ppermute | solution.py:394
  20.5 7.5 %collective-permute-start.6 = (bf16[16,8,512]{2,1,0:T(8,128)(2,1)S(1)}, bf16[16,8,512]{2,1,0:T(8,128)(2,1)S(1)}, u32[]{:S(2)}, u32[]{:S(2)}) collective-permute-start(bf16[16,8,512]{2,1,0:T(8,128)(2,1)S(1)} %get-tuple-element.28.rest_0_), channel_id=1, source_target_pairs={{0,1},{1,2},{2,3},{4,5},{5,6},{6,7},{8,9},{9,10},{10,11},{12,13},{... | collective-permute-start | bytes 393224 | tf_op jit(solution)/shard_map/ppermute | solution.py:394
  24.0 8.7 %collective-permute-start.5 = (bf16[17,8,512]{2,1,0:T(8,128)(2,1)S(1)}, bf16[17,8,512]{2,1,0:T(8,128)(2,1)S(1)}, u32[]{:S(2)}, u32[]{:S(2)}) collective-permute-start(bf16[17,8,512]{2,1,0:T(8,128)(2,1)S(1)} %collective-permute-done.4.rest_1_), channel_id=1, source_target_pairs={{0,1},{1,2},{2,3},{4,5},{5,6},{6,7},{8,9},{9,10},{10,11},{12,13},{... | collective-permute-start | bytes 417800 | tf_op jit(solution)/shard_map/ppermute | solution.py:394
  29.1 3.7 %copy-start.1 = (f32[4096]{0:T(1024)S(1)}, f32[4096]{0:T(1024)}, u32[]{:S(2)}) copy-start(f32[4096]{0:T(1024)} %param.13) | copy-start | bytes 49156
  29.1 6.8 %collective-permute-start.7 = (bf16[16,8,512]{2,1,0:T(8,128)(2,1)S(1)}, bf16[16,8,512]{2,1,0:T(8,128)(2,1)S(1)}, u32[]{:S(2)}, u32[]{:S(2)}) collective-permute-start(bf16[16,8,512]{2,1,0:T(8,128)(2,1)S(1)} %after_query.1), channel_id=1, source_target_pairs={{0,1},{1,2},{2,3},{4,5},{5,6},{6,7},{8,9},{9,10},{10,11},{12,13},{... | collective-permute-start | bytes 393224 | tf_op jit(solution)/shard_map/ppermute | solution.py:394
  37.2 11.4 %all-to-all-start.1 = ((f32[32,1,640]{2,1,0:T(1,128)}), f32[32,1,640]{2,1,0:T(1,128)S(1)}, u32[]{:S(2)}, u32[]{:S(2)}) async-start(f32[32,1,640]{2,1,0:T(1,128)} %ends.1), calls=%async_computation.1 | async-start | bytes 163840 | tf_op jit(solution)/shard_map/all_to_all | solution.py:435

commit v6 on v5

--- a/solution.py
+++ b/solution.py
@@ -15,6 +15,7 @@
 SEGS = 16
 BINS = 512
 NEG = -1e30
+FIRST_LANE, LAST_LANE, BIN_LANE = 2 * SEGS - 2, 2 * SEGS - 1, 2 * SEGS
 SHARES = (2, HK - 2)
 FACTOR = math.log2(math.e) / math.sqrt(HD)
 
@@ -27,7 +28,7 @@
     return pl.CostEstimate(flops=flops, bytes_accessed=nbytes, transcendentals=0)
 
 
-def find_blocks(dest_ref, block_ref, count_ref, cap, relative):
+def find_blocks(dest_ref, block_ref, place_ref, count_ref, cap):
     dp_count, block_count = dest_ref.shape
     me = lax.axis_index("dp")
     for target in range(dp_count):
@@ -36,8 +37,8 @@
         target = dest_ref[me, block]
         rank = count_ref[target]
         count_ref[target] = rank + 1
-        place = (target ^ me) if relative else target
-        block_ref[place * cap + rank] = block
+        block_ref[target * cap + rank] = block
+        place_ref[(target ^ me) * cap + rank] = block
 
 
 def find_columns(dest_ref, column_ref, cap, relative):
@@ -71,8 +72,7 @@
     for arrival in arrivals:
         arrival.start()
     arrivals[0].wait()
-    find_blocks(dest_ref, block_ref, count_ref, cap, False)
-    find_blocks(dest_ref, place_ref, count_ref, cap, True)
+    find_blocks(dest_ref, block_ref, place_ref, count_ref, cap)
     arrivals[1].wait()
     arrivals[2].wait()
     width = key_ref.shape[2]
@@ -113,9 +113,11 @@
 def unsort_kv_kernel(cap, dest_ref, bins_ref, seg_ref, got_ref, *rest):
     outs, (bin_ref, column_ref) = rest[:-2], rest[-2:]
     find_columns(dest_ref, column_ref, cap, False)
-    lane = lax.broadcasted_iota(jnp.int32, (1, bin_ref.shape[1]), 1)
+    lane = lax.broadcasted_iota(jnp.int32, (1, HD), 1)
+    bins = jnp.zeros((1, HD), jnp.int32)
     for seg in range(SEGS):
-        bin_ref[seg : seg + 1, :] = jnp.where(lane == bins_ref[0, seg], 1.0, 0.0)
+        bins = jnp.where(lane == BIN_LANE + seg, bins_ref[0, seg], bins)
+    bin_ref[...] = bins.astype(jnp.float32)
     block_count = got_ref.shape[0]
     for slot in range(block_count):
         column = column_ref[slot]
@@ -252,29 +254,18 @@
     reward = reward_ref[...] + end_rewards(
         1, end_query_ref, end_bias_ref, end_weight_ref, parts, block_count
     )
-    ends = reward.shape[1]
-    by_seg = jnp.transpose(jnp.broadcast_to(reward, (ends, ends)))
-    by_seg = jnp.sum(by_seg.reshape(GROUP, SEGS, ends), axis=0)
-    seg = lax.broadcasted_iota(jnp.int32, (SEGS, ends), 0)
+    by_seg = reward[:, :SEGS]
+    for head in range(1, GROUP):
+        by_seg = by_seg + reward[:, head * SEGS : (head + 1) * SEGS]
+    by_seg = jnp.concatenate([by_seg, jnp.zeros((1, HD - SEGS), jnp.float32)], axis=1)
+    lane = lax.broadcasted_iota(jnp.int32, (1, HD), 1)
+    seg_rows = jnp.transpose(jnp.broadcast_to(seg_row, (row_count, row_count)))
+    present = jnp.max(jnp.where(seg_rows == lane, 1, 0), axis=0, keepdims=True)
     first_seg, last_seg = seg_row[:, :1], seg_row[:, row_count - 1 :]
-    seg_rows = jnp.broadcast_to(seg_row, (SEGS, row_count))
-    row_seg = lax.broadcasted_iota(jnp.int32, seg_rows.shape, 0)
-    present = jnp.max(jnp.where(seg_rows == row_seg, 1, 0), axis=1, keepdims=True)
-    certain = jnp.where((present > 0) & (seg != last_seg), by_seg, 0.0)
-    bin_of = bin_ref[...]
-    hist = jnp.sum(bin_of * jnp.concatenate([certain] * (BINS // ends), axis=1), axis=0, keepdims=True)
-    last_reward = jnp.sum(jnp.where(seg == last_seg, by_seg, 0.0), axis=0, keepdims=True)
-    bin_id = lax.broadcasted_iota(jnp.int32, (SEGS, BINS), 1).astype(jnp.float32)
-    row_id = lax.broadcasted_iota(jnp.int32, (SEGS, BINS), 0)
-    last_bin = jnp.where(row_id == last_seg, bin_of * bin_id, 0.0)
-    last_bin = jnp.sum(jnp.sum(last_bin, axis=0, keepdims=True), axis=1, keepdims=True)
-    lane = lax.broadcasted_iota(jnp.int32, (1, HD), 1)
-    notes = jnp.where(lane == 0, last_reward, 0.0)
-    notes = notes + jnp.where(lane == 1, last_bin, 0.0)
-    notes = notes + jnp.where(lane == 2, first_seg.astype(jnp.float32), 0.0)
-    notes = notes + jnp.where(lane == 3, last_seg.astype(jnp.float32), 0.0)
-    row = jnp.concatenate([hist, notes], axis=1)
-    hist_ref[...] = jnp.broadcast_to(row.reshape(1, 1, row.shape[1]), hist_ref.shape)
+    row = bin_ref[...] + jnp.where(present > 0, by_seg, 0.0)
+    row = row + jnp.where(lane == FIRST_LANE, first_seg.astype(jnp.float32), 0.0)
+    row = row + jnp.where(lane == LAST_LANE, last_seg.astype(jnp.float32), 0.0)
+    hist_ref[...] = jnp.broadcast_to(row.reshape(1, 1, HD), hist_ref.shape)
 
 
 def last_kernel(query_ref, before_ref, bias_ref, *rest):
@@ -283,15 +274,24 @@
 
 def total_kernel(ctx_count, rows_ref, out_ref):
     device_count = rows_ref.shape[0]
-    rows = rows_ref[...].reshape(device_count, rows_ref.shape[2])
-    notes = rows[:, BINS:]
-    reward, bin_of, first, last = (notes[:, k : k + 1] for k in range(4))
+    rows = rows_ref[...]
+    first = rows[:, :, FIRST_LANE : FIRST_LANE + 1]
+    last = rows[:, :, LAST_LANE : LAST_LANE + 1]
     following = jnp.concatenate([first[1:], first[:1]], axis=0)
-    device = lax.broadcasted_iota(jnp.int32, (device_count, 1), 0)
+    device = lax.broadcasted_iota(jnp.int32, first.shape, 0)
     ends = (following != last) | (lax.rem(device, ctx_count) == ctx_count - 1)
-    bin_id = lax.broadcasted_iota(jnp.int32, (device_count, BINS), 1).astype(jnp.float32)
-    extra = jnp.where((bin_id == bin_of) & ends, reward, 0.0)
-    out_ref[...] = jnp.sum(rows[:, :BINS] + extra, axis=0, keepdims=True)
+    lane = lax.broadcasted_iota(jnp.int32, rows.shape, 2)
+    kept = (lane < SEGS) & ((lane.astype(jnp.float32) != last) | ends)
+    rewards = jnp.where(kept, rows, 0.0)
+    groups = (device_count // ctx_count, ctx_count, 1, HD)
+    rewards = jnp.sum(rewards.reshape(groups), axis=1).reshape(groups[0], HD)
+    bins = rows.reshape(groups)[:, 0].reshape(groups[0], HD)
+    bin_id = lax.broadcasted_iota(jnp.int32, (groups[0], BINS), 1).astype(jnp.float32)
+    hist = jnp.zeros((groups[0], BINS), jnp.float32)
+    for seg in range(SEGS):
+        bin_of = bins[:, BIN_LANE + seg : BIN_LANE + seg + 1]
+        hist = hist + jnp.where(bin_id == bin_of, rewards[:, seg : seg + 1], 0.0)
+    out_ref[...] = jnp.sum(hist, axis=0, keepdims=True)
 
 
 def local(roll_query, roll_keys, roll_values, pack_dest, segment_ids, reward_bins, reward_weight):
@@ -369,7 +369,7 @@
             jax.ShapeDtypeStruct((block_count + (share == 0), BLK, 2 * groups * HD), jnp.bfloat16)
             for share, groups in enumerate(SHARES)
         ]
-        + [jax.ShapeDtypeStruct((SEGS, BINS), jnp.float32)],
+        + [jax.ShapeDtypeStruct((1, HD), jnp.float32)],
         in_specs=[smem, smem, vmem, vmem],
         out_specs=[vmem] * (len(SHARES) + 1),
         scratch_shapes=[pltpu.SMEM((slot_count,), jnp.int32)],
@@ -416,7 +416,7 @@
     )(segment_ids, weight_row, query, *[part[0] for part in parts])
     hist_rows = pl.pallas_call(
         ends_kernel,
-        out_shape=jax.ShapeDtypeStruct((device_count, 1, BINS + HD), jnp.float32),
+        out_shape=jax.ShapeDtypeStruct((device_count, 1, HD), jnp.float32),
         in_specs=[vmem] * (6 + part_count),
         out_specs=vmem,
         compiler_params=params(16),

time: 49.7 us -> 49.4 us (level)
  waiting for transfers between devices: 8.96 us -> 8.42 us
    all_to_all x1, waiting for transfers between devices: 5.26 us -> 4.72 us  [local(): lax.all_to_all(hist_rows, ('dp', 'ctx'), split_axis=0, concat_axis=0, til...]
where the time goes in v6:
time: 49.4 us; the launch traced here: 49 us
  starting transfers between devices  27.2 us (55%)
  Pallas kernels  12.5 us (25%)
  waiting for transfers between devices  8.42 us (17%)
  between operations  0.82 us (2%)
    ppermute x4, starting transfers between devices, local(): parts.append([lax.ppermute(array, 'ctx', forward) for array in arrays])  14.6 us
    all_to_all x1, starting transfers between devices, local(): lax.all_to_all(sorted_kv.reshape(dp_count, cap * BLK, 2 * kv_width), 'dp'...  4.87 us
    all_to_all x1, waiting for transfers between devices, local(): lax.all_to_all(hist_rows, ('dp', 'ctx'), split_axis=0, concat_axis=0, til...  4.72 us
    ppermute x4, starting transfers between devices, across(): lax.ppermute(array, 'dp', [(i, i ^ distance) for i in range(dp_count)])  4.14 us
    all_to_all x1, waiting for transfers between devices, local(): lax.all_to_all(sorted_kv.reshape(dp_count, cap * BLK, 2 * kv_width), 'dp'...  3.68 us
    all_to_all x1, starting transfers between devices, local(): lax.all_to_all(hist_rows, ('dp', 'ctx'), split_axis=0, concat_axis=0, til...  3.63 us
    pallas_call x1, Pallas kernels, local(): pl.pallas_call(first_kernel, grid=(1,), out_shape=(out_shape, jax.ShapeDt...  3.19 us
    pallas_call x1, Pallas kernels, local(): pl.pallas_call(lambda *refs: sort_kernel(cap, piece_count, *refs), out_sh...  2.5 us
  transfers between devices with their start and end apart: 10, of which 2 were waited for; matrix products, arithmetic and copies ran while one was open for 0% of the time, Pallas kernels for 16%

profile of v6, /device:TPU:0, one launch (start us, length us, event | category | flops | bytes accessed | tf_op | source)
XLA Modules:
  0.0 49.0 jit_solution(4470456306441069000)
XLA Ops:
  0.6 2.5 %sort.1 = (bf16[16,8,1024]{2,1,0:T(8,128)(2,1)}, bf16[8,8,4096]{2,1,0:T(8,128)(2,1)}, bf16[8,8,4096]{2,1,0:T(8,128)(2,1)}) custom-call(s32[8,16]{1,0:T(8,128)} %refs_0_.5, bf16[16,8,512]{2,1,0:T(8,128)(2,1)} %bitcast.13, bf16[16,8,512]{2,1,0:T(8,128)(2,1)} %bitcast.14, bf16[16,8,4096]{2,1,0:T(8,128)(2,1)} %bitcast.11), custom_call_target="tpu_custom_call" | custom-call | tf_op jit(solution)/shard_map/sort/pallas_call | solution.py:318
  3.1 0.0 copy-start
  3.2 0.5 %collective-permute-start = (bf16[8,8,4096]{2,1,0:T(8,128)(2,1)}, bf16[8,8,4096]{2,1,0:T(8,128)(2,1)S(1)}, u32[]{:S(2)}, u32[]{:S(2)}) collective-permute-start(bf16[8,8,4096]{2,1,0:T(8,128)(2,1)} %get-tuple-element.19), channel_id=1, source_target_pairs={{0,4},{4,0},{8,12},{12,8},{16,20},{20,16},{24,28},{28,24},{1,5},{5... | collective-permute-start | bytes 1572872 | tf_op jit(solution)/shard_map/ppermute | solution.py:315
  3.7 4.9 %all-to-all-start = ((bf16[8,16,1024]{2,1,0:T(8,128)(2,1)}), bf16[8,16,1024]{2,1,0:T(8,128)(2,1)S(1)}, u32[]{:S(2)}, u32[]{:S(2)}) async-start(bf16[8,16,1024]{2,1,0:T(8,128)(2,1)} %bitcast.12), calls=%async_computation | async-start | bytes 524288 | tf_op jit(solution)/shard_map/all_to_all | solution.py:343
  8.5 0.0 collective-permute-done.refs_1_
  8.6 0.1 merge_query.1
  8.6 0.0 copy-start.2
  8.7 2.1 %collective-permute-start.1 = (bf16[4,8,4096]{2,1,0:T(8,128)(2,1)S(1)}, bf16[4,8,4096]{2,1,0:T(8,128)(2,1)S(1)}, u32[]{:S(2)}, u32[]{:S(2)}) collective-permute-start(bf16[4,8,4096]{2,1,0:T(8,128)(2,1)S(1)} %get-tuple-element.21), channel_id=1, source_target_pairs={{0,8},{4,12},{8,0},{12,4},{16,24},{20,28},{24,16},{28,20},{1,9},{5... | collective-permute-start | bytes 786440 | tf_op jit(solution)/shard_map/ppermute | solution.py:315
  10.7 1.5 %collective-permute-start.2 = (bf16[4,8,4096]{2,1,0:T(8,128)(2,1)S(1)}, bf16[4,8,4096]{2,1,0:T(8,128)(2,1)S(1)}, u32[]{:S(2)}, u32[]{:S(2)}) collective-permute-start(bf16[4,8,4096]{2,1,0:T(8,128)(2,1)S(1)} %get-tuple-element.22), channel_id=1, source_target_pairs={{0,16},{4,20},{8,24},{12,28},{16,0},{20,4},{24,8},{28,12},{1,17},{... | collective-permute-start | bytes 786440 | tf_op jit(solution)/shard_map/ppermute | solution.py:315
  12.2 0.1 collective-permute-start.3
  12.3 3.7 %all-to-all-done = bf16[8,16,1024]{2,1,0:T(8,128)(2,1)S(1)} async-done(((bf16[8,16,1024]{2,1,0:T(8,128)(2,1)}), bf16[8,16,1024]{2,1,0:T(8,128)(2,1)S(1)}, u32[]{:S(2)}, u32[]{:S(2)}) %all-to-all-start) | async-done | bytes 262176 | tf_op jit(solution)/shard_map/all_to_all | solution.py:343
  16.0 0.0 copy-done.2
  16.0 1.0 %unsort_kv.1 = (bf16[17,8,512]{2,1,0:T(8,128)(2,1)S(1)}, bf16[16,8,512]{2,1,0:T(8,128)(2,1)S(1)}, f32[1,128]{1,0:T(1,128)S(1)}) custom-call(s32[8,16]{1,0:T(8,128)S(1)} %copy-done.2, s32[1,16]{1,0:T(1,128)S(1)} %copy-done.4, s32[1,128]{1,0:T(1,128)S(1)} %copy-done.3, bf16[16,8,1024]{2,1,0:T(8,128)(2,1)S(1)} %bitcast.8), custom_call_target="tpu_custom_call" | custom-call | flops 23000000512 | tf_op jit(solution)/shard_map/unsort_kv/pallas_call | solution.py:366
  17.0 3.5 %collective-permute-start.4 = (bf16[17,8,512]{2,1,0:T(8,128)(2,1)S(1)}, bf16[17,8,512]{2,1,0:T(8,128)(2,1)S(1)}, u32[]{:S(2)}, u32[]{:S(2)}) collective-permute-start(bf16[17,8,512]{2,1,0:T(8,128)(2,1)S(1)} %get-tuple-element.25.rest_0_), channel_id=1, source_target_pairs={{0,1},{1,2},{2,3},{4,5},{5,6},{6,7},{8,9},{9,10},{10,11},{12,13},{... | collective-permute-start | bytes 417800 | tf_op jit(solution)/shard_map/ppermute | solution.py:394
  20.5 3.5 %collective-permute-start.6 = (bf16[16,8,512]{2,1,0:T(8,128)(2,1)S(1)}, bf16[16,8,512]{2,1,0:T(8,128)(2,1)S(1)}, u32[]{:S(2)}, u32[]{:S(2)}) collective-permute-start(bf16[16,8,512]{2,1,0:T(8,128)(2,1)S(1)} %get-tuple-element.28.rest_0_), channel_id=1, source_target_pairs={{0,1},{1,2},{2,3},{4,5},{5,6},{6,7},{8,9},{9,10},{10,11},{12,13},{... | collective-permute-start | bytes 393224 | tf_op jit(solution)/shard_map/ppermute | solution.py:394
  24.0 0.0 collective-permute-done.4.rest_1_
  24.0 4.0 %collective-permute-start.5 = (bf16[17,8,512]{2,1,0:T(8,128)(2,1)S(1)}, bf16[17,8,512]{2,1,0:T(8,128)(2,1)S(1)}, u32[]{:S(2)}, u32[]{:S(2)}) collective-permute-start(bf16[17,8,512]{2,1,0:T(8,128)(2,1)S(1)} %collective-permute-done.4.rest_1_), channel_id=1, source_target_pairs={{0,1},{1,2},{2,3},{4,5},{5,6},{6,7},{8,9},{9,10},{10,11},{12,13},{... | collective-permute-start | bytes 417800 | tf_op jit(solution)/shard_map/ppermute | solution.py:394
  28.0 0.0 collective-permute-done.6.rest_1_
  28.0 0.0 collective-permute-done.1.refs_2_
  28.0 0.0 collective-permute-done.2.refs_3_
  28.0 0.0 collective-permute-done.3.refs_4_
  28.0 1.0 %unsort_query.1.query_ref.refs_1_ = bf16[16,8,4096]{2,1,0:T(8,128)(2,1)S(1)} custom-call(s32[8,16]{1,0:T(8,128)S(1)} %copy-done.2, bf16[4,8,4096]{2,1,0:T(8,128)(2,1)S(1)} %get-tuple-element.20.refs_1_, bf16[4,8,4096]{2,1,0:T(8,128)(2,1)S(1)} %collective-permute-done.1.refs_2_, bf16[4,8,4096]{2,1,0:T(8,128)(2,1)S(1)} %collective-permute-done.2.refs_3_, ...), custom_call_target="tpu_custom_call" | custom-call | tf_op jit(solution)/shard_map/unsort_query/pallas_call | solution.py:356
  29.1 0.0 copy-start.1
  29.1 3.6 %collective-permute-start.7 = (bf16[16,8,512]{2,1,0:T(8,128)(2,1)S(1)}, bf16[16,8,512]{2,1,0:T(8,128)(2,1)S(1)}, u32[]{:S(2)}, u32[]{:S(2)}) collective-permute-start(bf16[16,8,512]{2,1,0:T(8,128)(2,1)S(1)} %after_query.1), channel_id=1, source_target_pairs={{0,1},{1,2},{2,3},{4,5},{5,6},{6,7},{8,9},{9,10},{10,11},{12,13},{... | collective-permute-start | bytes 393224 | tf_op jit(solution)/shard_map/ppermute | solution.py:394
  32.7 0.0 collective-permute-done.5.rest_2_
  32.7 3.2 %first_share.1 = (bf16[128,4096]{1,0:T(8,128)(2,1)}, f32[384,128]{1,0:T(8,128)S(1)}, bf16[4,128,128]{2,1,0:T(8,128)(2,1)S(1)}, f32[384,128]{1,0:T(8,128)S(1)}, f...) custom-call(s32[1,128]{1,0:T(1,128)S(1)} %copy-done.3, f32[1,4096]{1,0:T(1,128)S(1)} %bitcast.9, ...), custom_call_target="tpu_custom_call" | custom-call | tf_op jit(solution)/shard_map/first_share/pallas_call | solution.py:401
  35.9 0.0 collective-permute-done.7.rest_2_
  35.9 1.2 %ends.1 = f32[32,1,128]{2,1,0:T(1,128)} custom-call(s32[1,128]{1,0:T(1,128)S(1)} %copy-done.3, bf16[4,128,128]{2,1,0:T(8,128)(2,1)S(1)} %get-tuple-element.29.end_query_ref, f32[384,128]{1,0:T(8,128)S(1)} %get-tuple-element.30.end_bias_ref, f32[4,128,128]{2,1,0:T(8,128)S(1)} %get-tuple-element.31.end_weight_ref, f32[1,128]{1,0:T(1,128)S(1)} %get-tuple-element.32.reward_ref, ...), custom_call_target="tpu_custom_call" | custom-call | tf_op jit(solution)/shard_map/ends/pallas_call | solution.py:417
  37.1 3.6 %all-to-all-start.1 = ((f32[32,1,128]{2,1,0:T(1,128)}), f32[32,1,128]{2,1,0:T(1,128)S(1)}, u32[]{:S(2)}, u32[]{:S(2)}) async-start(f32[32,1,128]{2,1,0:T(1,128)} %ends.1), calls=%async_computation.1 | async-start | bytes 32768 | tf_op jit(solution)/shard_map/all_to_all | solution.py:435
  40.7 2.5 %last_share.1 = bf16[128,4096]{1,0:T(8,128)(2,1)} custom-call(bf16[16,8,4096]{2,1,0:T(8,128)(2,1)S(1)} %unsort_query.1.query_ref.refs_1_, bf16[128,4096]{1,0:T(8,128)(2,1)} %get-tuple-element.26.before_ref, f32[384,128]{1,0:T(8,128)S(1)} %get-tuple-element.27.bias_ref, ...), custom_call_target="tpu_custom_call", output_to_operand_aliasing={{}: (1, {})} | custom-call | tf_op jit(solution)/shard_map/last_share/pallas_call | solution.py:425
  43.2 4.7 %all-to-all-done.1.refs_0_ = f32[32,1,128]{2,1,0:T(1,128)S(1)} async-done(((f32[32,1,128]{2,1,0:T(1,128)}), f32[32,1,128]{2,1,0:T(1,128)S(1)}, u32[]{:S(2)}, u32[]{:S(2)}) %all-to-all-start.1) | async-done | bytes 16416 | tf_op jit(solution)/shard_map/all_to_all | solution.py:435
  47.9 1.1 %total.1 = f32[1,512]{1,0:T(1,128)} custom-call(f32[32,1,128]{2,1,0:T(1,128)S(1)} %all-to-all-done.1.refs_0_), custom_call_target="tpu_custom_call" | custom-call | tf_op jit(solution)/shard_map/total/pallas_call | solution.py:436
  (8 shorter events, 0.0 us)
Async XLA Ops:
  3.1 5.4 %copy-start = (bf16[8,8,4096]{2,1,0:T(8,128)(2,1)S(1)}, bf16[8,8,4096]{2,1,0:T(8,128)(2,1)}, u32[]{:S(2)}) copy-start(bf16[8,8,4096]{2,1,0:T(8,128)(2,1)} %get-tuple-element.18.refs_0_) | copy-start | bytes 1572868
  3.2 5.4 %collective-permute-start = (bf16[8,8,4096]{2,1,0:T(8,128)(2,1)}, bf16[8,8,4096]{2,1,0:T(8,128)(2,1)S(1)}, u32[]{:S(2)}, u32[]{:S(2)}) collective-permute-start(bf16[8,8,4096]{2,1,0:T(8,128)(2,1)} %get-tuple-element.19), channel_id=1, source_target_pairs={{0,4},{4,0},{8,12},{12,8},{16,20},{20,16},{24,28},{28,24},{1,5},{5... | collective-permute-start | bytes 1572872 | tf_op jit(solution)/shard_map/ppermute | solution.py:315
  3.7 12.3 %all-to-all-start = ((bf16[8,16,1024]{2,1,0:T(8,128)(2,1)}), bf16[8,16,1024]{2,1,0:T(8,128)(2,1)S(1)}, u32[]{:S(2)}, u32[]{:S(2)}) async-start(bf16[8,16,1024]{2,1,0:T(8,128)(2,1)} %bitcast.12), calls=%async_computation | async-start | bytes 524288 | tf_op jit(solution)/shard_map/all_to_all | solution.py:343
  8.6 7.3 %copy-start.2 = (s32[8,16]{1,0:T(8,128)S(1)}, s32[8,16]{1,0:T(8,128)}, u32[]{:S(2)}) copy-start(s32[8,16]{1,0:T(8,128)} %refs_0_.5) | copy-start | bytes 1540
  8.7 19.4 %collective-permute-start.1 = (bf16[4,8,4096]{2,1,0:T(8,128)(2,1)S(1)}, bf16[4,8,4096]{2,1,0:T(8,128)(2,1)S(1)}, u32[]{:S(2)}, u32[]{:S(2)}) collective-permute-start(bf16[4,8,4096]{2,1,0:T(8,128)(2,1)S(1)} %get-tuple-element.21), channel_id=1, source_target_pairs={{0,8},{4,12},{8,0},{12,4},{16,24},{20,28},{24,16},{28,20},{1,9},{5... | collective-permute-start | bytes 786440 | tf_op jit(solution)/shard_map/ppermute | solution.py:315
  10.7 17.3 %collective-permute-start.2 = (bf16[4,8,4096]{2,1,0:T(8,128)(2,1)S(1)}, bf16[4,8,4096]{2,1,0:T(8,128)(2,1)S(1)}, u32[]{:S(2)}, u32[]{:S(2)}) collective-permute-start(bf16[4,8,4096]{2,1,0:T(8,128)(2,1)S(1)} %get-tuple-element.22), channel_id=1, source_target_pairs={{0,16},{4,20},{8,24},{12,28},{16,0},{20,4},{24,8},{28,12},{1,17},{... | collective-permute-start | bytes 786440 | tf_op jit(solution)/shard_map/ppermute | solution.py:315
  12.2 3.8 %copy-start.3 = (s32[1,128]{1,0:T(1,128)S(1)}, s32[1,128]{1,0:T(1,128)}, u32[]{:S(2)}) copy-start(s32[1,128]{1,0:T(1,128)} %seg_ref.3) | copy-start | bytes 1540
  12.2 3.8 %copy-start.4 = (s32[1,16]{1,0:T(1,128)S(1)}, s32[1,16]{1,0:T(1,128)}, u32[]{:S(2)}) copy-start(s32[1,16]{1,0:T(1,128)} %refs_1_.1) | copy-start | bytes 196
  12.2 15.8 %collective-permute-start.3 = (bf16[4,8,4096]{2,1,0:T(8,128)(2,1)S(1)}, bf16[4,8,4096]{2,1,0:T(8,128)(2,1)S(1)}, u32[]{:S(2)}, u32[]{:S(2)}) collective-permute-start(bf16[4,8,4096]{2,1,0:T(8,128)(2,1)S(1)} %get-tuple-element.23), channel_id=1, source_target_pairs={{0,24},{4,28},{8,16},{12,20},{16,8},{20,12},{24,0},{28,4},{1,25},{... | collective-permute-start | bytes 786440 | tf_op jit(solution)/shard_map/ppermute | solution.py:315
  17.0 7.0 %collective-permute-start.4 = (bf16[17,8,512]{2,1,0:T(8,128)(2,1)S(1)}, bf16[17,8,512]{2,1,0:T(8,128)(2,1)S(1)}, u32[]{:S(2)}, u32[]{:S(2)}) collective-permute-start(bf16[17,8,512]{2,1,0:T(8,128)(2,1)S(1)} %get-tuple-element.25.rest_0_), channel_id=1, source_target_pairs={{0,1},{1,2},{2,3},{4,5},{5,6},{6,7},{8,9},{9,10},{10,11},{12,13},{... | collective-permute-start | bytes 417800 | tf_op jit(solution)/shard_map/ppermute | solution.py:394
  20.5 7.5 %collective-permute-start.6 = (bf16[16,8,512]{2,1,0:T(8,128)(2,1)S(1)}, bf16[16,8,512]{2,1,0:T(8,128)(2,1)S(1)}, u32[]{:S(2)}, u32[]{:S(2)}) collective-permute-start(bf16[16,8,512]{2,1,0:T(8,128)(2,1)S(1)} %get-tuple-element.28.rest_0_), channel_id=1, source_target_pairs={{0,1},{1,2},{2,3},{4,5},{5,6},{6,7},{8,9},{9,10},{10,11},{12,13},{... | collective-permute-start | bytes 393224 | tf_op jit(solution)/shard_map/ppermute | solution.py:394
  24.0 8.7 %collective-permute-start.5 = (bf16[17,8,512]{2,1,0:T(8,128)(2,1)S(1)}, bf16[17,8,512]{2,1,0:T(8,128)(2,1)S(1)}, u32[]{:S(2)}, u32[]{:S(2)}) collective-permute-start(bf16[17,8,512]{2,1,0:T(8,128)(2,1)S(1)} %collective-permute-done.4.rest_1_), channel_id=1, source_target_pairs={{0,1},{1,2},{2,3},{4,5},{5,6},{6,7},{8,9},{9,10},{10,11},{12,13},{... | collective-permute-start | bytes 417800 | tf_op jit(solution)/shard_map/ppermute | solution.py:394
  29.1 3.7 %copy-start.1 = (f32[4096]{0:T(1024)S(1)}, f32[4096]{0:T(1024)}, u32[]{:S(2)}) copy-start(f32[4096]{0:T(1024)} %param.13) | copy-start | bytes 49156
  29.1 6.8 %collective-permute-start.7 = (bf16[16,8,512]{2,1,0:T(8,128)(2,1)S(1)}, bf16[16,8,512]{2,1,0:T(8,128)(2,1)S(1)}, u32[]{:S(2)}, u32[]{:S(2)}) collective-permute-start(bf16[16,8,512]{2,1,0:T(8,128)(2,1)S(1)} %after_query.1), channel_id=1, source_target_pairs={{0,1},{1,2},{2,3},{4,5},{5,6},{6,7},{8,9},{9,10},{10,11},{12,13},{... | collective-permute-start | bytes 393224 | tf_op jit(solution)/shard_map/ppermute | solution.py:394
  37.1 10.8 %all-to-all-start.1 = ((f32[32,1,128]{2,1,0:T(1,128)}), f32[32,1,128]{2,1,0:T(1,128)S(1)}, u32[]{:S(2)}, u32[]{:S(2)}) async-start(f32[32,1,128]{2,1,0:T(1,128)} %ends.1), calls=%async_computation.1 | async-start | bytes 32768 | tf_op jit(solution)/shard_map/all_to_all | solution.py:435

commit v7 on v6

--- a/solution.py
+++ b/solution.py
@@ -164,15 +164,15 @@
 
 def attend_share(share, query_ref, parts, out_ref, bias_ref):
     before = sum(SHARES[:share])
-    for index in range(SHARES[share]):
-        keys, values = keys_and_values(share, index, query_ref.shape[0], parts)
-        heads = range((before + index) * GROUP, (before + index + 1) * GROUP)
-        scores = [score(keys, query_ref, head) for head in heads]
-        mixed = attend_rows(scores, [values] * GROUP, bias_ref[...])
-        attended = [jnp.transpose(each) for each in mixed]
-        for head, each in zip(heads, attended):
-            first = (head - before * GROUP) * HD
-            out_ref[:, first : first + HD] = each
+    held = [keys_and_values(share, index, query_ref.shape[0], parts) for index in range(SHARES[share])]
+    heads = range(before * GROUP, (before + SHARES[share]) * GROUP)
+    owners = [held[head // GROUP - before] for head in heads]
+    scores = [score(keys, query_ref, head) for head, (keys, _) in zip(heads, owners)]
+    mixed = attend_rows(scores, [values for _, values in owners], bias_ref[...])
+    attended = [jnp.transpose(each) for each in mixed]
+    for head, each in zip(heads, attended):
+        first = (head - before * GROUP) * HD
+        out_ref[:, first : first + HD] = each
 
 
 def keys_and_values(share, index, block_count, parts):

time: 49.4 us -> 49.4 us (level)
  transfers between devices with their start and end apart: 10 -> 10, of which waited for: 2 -> 2; matrix products, arithmetic and copies ran while one was open for 0% -> 0% of each run, Pallas kernels for 16% -> 15%
where the time goes in v7:
time: 49.4 us; the launch traced here: 49 us
  starting transfers between devices  27.4 us (55%)
  Pallas kernels  12.3 us (25%)
  waiting for transfers between devices  8.44 us (17%)
  between operations  0.82 us (2%)
    ppermute x4, starting transfers between devices, local(): parts.append([lax.ppermute(array, 'ctx', forward) for array in arrays])  14.6 us
    all_to_all x1, starting transfers between devices, local(): lax.all_to_all(sorted_kv.reshape(dp_count, cap * BLK, 2 * kv_width), 'dp'...  4.87 us
    all_to_all x1, waiting for transfers between devices, local(): lax.all_to_all(hist_rows, ('dp', 'ctx'), split_axis=0, concat_axis=0, til...  4.74 us
    ppermute x4, starting transfers between devices, across(): lax.ppermute(array, 'dp', [(i, i ^ distance) for i in range(dp_count)])  4.14 us
    all_to_all x1, starting transfers between devices, local(): lax.all_to_all(hist_rows, ('dp', 'ctx'), split_axis=0, concat_axis=0, til...  3.85 us
    all_to_all x1, waiting for transfers between devices, local(): lax.all_to_all(sorted_kv.reshape(dp_count, cap * BLK, 2 * kv_width), 'dp'...  3.68 us
    pallas_call x1, Pallas kernels, local(): pl.pallas_call(first_kernel, grid=(1,), out_shape=(out_shape, jax.ShapeDt...  2.97 us
    pallas_call x1, Pallas kernels, local(): pl.pallas_call(lambda *refs: sort_kernel(cap, piece_count, *refs), out_sh...  2.5 us
  transfers between devices with their start and end apart: 10, of which 2 were waited for; matrix products, arithmetic and copies ran while one was open for 0% of the time, Pallas kernels for 15%

profile of v7, /device:TPU:0, one launch (start us, length us, event | category | flops | bytes accessed | tf_op | source)
XLA Modules:
  0.0 49.0 jit_solution(74898306524785956)
XLA Ops:
  0.6 2.5 %sort.1 = (bf16[16,8,1024]{2,1,0:T(8,128)(2,1)}, bf16[8,8,4096]{2,1,0:T(8,128)(2,1)}, bf16[8,8,4096]{2,1,0:T(8,128)(2,1)}) custom-call(s32[8,16]{1,0:T(8,128)} %refs_0_.5, bf16[16,8,512]{2,1,0:T(8,128)(2,1)} %bitcast.13, bf16[16,8,512]{2,1,0:T(8,128)(2,1)} %bitcast.14, bf16[16,8,4096]{2,1,0:T(8,128)(2,1)} %bitcast.11), custom_call_target="tpu_custom_call" | custom-call | tf_op jit(solution)/shard_map/sort/pallas_call | solution.py:318
  3.1 0.0 copy-start
  3.2 0.5 %collective-permute-start = (bf16[8,8,4096]{2,1,0:T(8,128)(2,1)}, bf16[8,8,4096]{2,1,0:T(8,128)(2,1)S(1)}, u32[]{:S(2)}, u32[]{:S(2)}) collective-permute-start(bf16[8,8,4096]{2,1,0:T(8,128)(2,1)} %get-tuple-element.19), channel_id=1, source_target_pairs={{0,4},{4,0},{8,12},{12,8},{16,20},{20,16},{24,28},{28,24},{1,5},{5... | collective-permute-start | bytes 1572872 | tf_op jit(solution)/shard_map/ppermute | solution.py:315
  3.7 4.9 %all-to-all-start = ((bf16[8,16,1024]{2,1,0:T(8,128)(2,1)}), bf16[8,16,1024]{2,1,0:T(8,128)(2,1)S(1)}, u32[]{:S(2)}, u32[]{:S(2)}) async-start(bf16[8,16,1024]{2,1,0:T(8,128)(2,1)} %bitcast.12), calls=%async_computation | async-start | bytes 524288 | tf_op jit(solution)/shard_map/all_to_all | solution.py:343
  8.5 0.0 collective-permute-done.refs_1_
  8.6 0.1 merge_query.1
  8.6 0.0 copy-start.2
  8.7 2.1 %collective-permute-start.1 = (bf16[4,8,4096]{2,1,0:T(8,128)(2,1)S(1)}, bf16[4,8,4096]{2,1,0:T(8,128)(2,1)S(1)}, u32[]{:S(2)}, u32[]{:S(2)}) collective-permute-start(bf16[4,8,4096]{2,1,0:T(8,128)(2,1)S(1)} %get-tuple-element.21), channel_id=1, source_target_pairs={{0,8},{4,12},{8,0},{12,4},{16,24},{20,28},{24,16},{28,20},{1,9},{5... | collective-permute-start | bytes 786440 | tf_op jit(solution)/shard_map/ppermute | solution.py:315
  10.7 1.5 %collective-permute-start.2 = (bf16[4,8,4096]{2,1,0:T(8,128)(2,1)S(1)}, bf16[4,8,4096]{2,1,0:T(8,128)(2,1)S(1)}, u32[]{:S(2)}, u32[]{:S(2)}) collective-permute-start(bf16[4,8,4096]{2,1,0:T(8,128)(2,1)S(1)} %get-tuple-element.22), channel_id=1, source_target_pairs={{0,16},{4,20},{8,24},{12,28},{16,0},{20,4},{24,8},{28,12},{1,17},{... | collective-permute-start | bytes 786440 | tf_op jit(solution)/shard_map/ppermute | solution.py:315
  12.2 0.1 collective-permute-start.3
  12.3 3.7 %all-to-all-done = bf16[8,16,1024]{2,1,0:T(8,128)(2,1)S(1)} async-done(((bf16[8,16,1024]{2,1,0:T(8,128)(2,1)}), bf16[8,16,1024]{2,1,0:T(8,128)(2,1)S(1)}, u32[]{:S(2)}, u32[]{:S(2)}) %all-to-all-start) | async-done | bytes 262176 | tf_op jit(solution)/shard_map/all_to_all | solution.py:343
  16.0 0.0 copy-done.2
  16.0 1.0 %unsort_kv.1 = (bf16[17,8,512]{2,1,0:T(8,128)(2,1)S(1)}, bf16[16,8,512]{2,1,0:T(8,128)(2,1)S(1)}, f32[1,128]{1,0:T(1,128)S(1)}) custom-call(s32[8,16]{1,0:T(8,128)S(1)} %copy-done.2, s32[1,16]{1,0:T(1,128)S(1)} %copy-done.4, s32[1,128]{1,0:T(1,128)S(1)} %copy-done.3, bf16[16,8,1024]{2,1,0:T(8,128)(2,1)S(1)} %bitcast.8), custom_call_target="tpu_custom_call" | custom-call | flops 23000000512 | tf_op jit(solution)/shard_map/unsort_kv/pallas_call | solution.py:366
  17.0 3.5 %collective-permute-start.4 = (bf16[17,8,512]{2,1,0:T(8,128)(2,1)S(1)}, bf16[17,8,512]{2,1,0:T(8,128)(2,1)S(1)}, u32[]{:S(2)}, u32[]{:S(2)}) collective-permute-start(bf16[17,8,512]{2,1,0:T(8,128)(2,1)S(1)} %get-tuple-element.25.rest_0_), channel_id=1, source_target_pairs={{0,1},{1,2},{2,3},{4,5},{5,6},{6,7},{8,9},{9,10},{10,11},{12,13},{... | collective-permute-start | bytes 417800 | tf_op jit(solution)/shard_map/ppermute | solution.py:394
  20.5 3.5 %collective-permute-start.6 = (bf16[16,8,512]{2,1,0:T(8,128)(2,1)S(1)}, bf16[16,8,512]{2,1,0:T(8,128)(2,1)S(1)}, u32[]{:S(2)}, u32[]{:S(2)}) collective-permute-start(bf16[16,8,512]{2,1,0:T(8,128)(2,1)S(1)} %get-tuple-element.28.rest_0_), channel_id=1, source_target_pairs={{0,1},{1,2},{2,3},{4,5},{5,6},{6,7},{8,9},{9,10},{10,11},{12,13},{... | collective-permute-start | bytes 393224 | tf_op jit(solution)/shard_map/ppermute | solution.py:394
  24.0 0.0 collective-permute-done.4.rest_1_
  24.0 4.0 %collective-permute-start.5 = (bf16[17,8,512]{2,1,0:T(8,128)(2,1)S(1)}, bf16[17,8,512]{2,1,0:T(8,128)(2,1)S(1)}, u32[]{:S(2)}, u32[]{:S(2)}) collective-permute-start(bf16[17,8,512]{2,1,0:T(8,128)(2,1)S(1)} %collective-permute-done.4.rest_1_), channel_id=1, source_target_pairs={{0,1},{1,2},{2,3},{4,5},{5,6},{6,7},{8,9},{9,10},{10,11},{12,13},{... | collective-permute-start | bytes 417800 | tf_op jit(solution)/shard_map/ppermute | solution.py:394
  28.0 0.0 collective-permute-done.6.rest_1_
  28.0 0.0 collective-permute-done.1.refs_2_
  28.0 0.0 collective-permute-done.2.refs_3_
  28.0 0.0 collective-permute-done.3.refs_4_
  28.0 1.0 %unsort_query.1.query_ref.refs_1_ = bf16[16,8,4096]{2,1,0:T(8,128)(2,1)S(1)} custom-call(s32[8,16]{1,0:T(8,128)S(1)} %copy-done.2, bf16[4,8,4096]{2,1,0:T(8,128)(2,1)S(1)} %get-tuple-element.20.refs_1_, bf16[4,8,4096]{2,1,0:T(8,128)(2,1)S(1)} %collective-permute-done.1.refs_2_, bf16[4,8,4096]{2,1,0:T(8,128)(2,1)S(1)} %collective-permute-done.2.refs_3_, ...), custom_call_target="tpu_custom_call" | custom-call | tf_op jit(solution)/shard_map/unsort_query/pallas_call | solution.py:356
  29.1 0.0 copy-start.1
  29.1 3.6 %collective-permute-start.7 = (bf16[16,8,512]{2,1,0:T(8,128)(2,1)S(1)}, bf16[16,8,512]{2,1,0:T(8,128)(2,1)S(1)}, u32[]{:S(2)}, u32[]{:S(2)}) collective-permute-start(bf16[16,8,512]{2,1,0:T(8,128)(2,1)S(1)} %after_query.1), channel_id=1, source_target_pairs={{0,1},{1,2},{2,3},{4,5},{5,6},{6,7},{8,9},{9,10},{10,11},{12,13},{... | collective-permute-start | bytes 393224 | tf_op jit(solution)/shard_map/ppermute | solution.py:394
  32.7 0.0 collective-permute-done.5.rest_2_
  32.7 3.0 %first_share.1 = (bf16[128,4096]{1,0:T(8,128)(2,1)}, f32[384,128]{1,0:T(8,128)S(1)}, bf16[4,128,128]{2,1,0:T(8,128)(2,1)S(1)}, f32[384,128]{1,0:T(8,128)S(1)}, f...) custom-call(s32[1,128]{1,0:T(1,128)S(1)} %copy-done.3, f32[1,4096]{1,0:T(1,128)S(1)} %bitcast.9, ...), custom_call_target="tpu_custom_call" | custom-call | tf_op jit(solution)/shard_map/first_share/pallas_call | solution.py:401
  35.7 0.0 collective-permute-done.7.rest_2_
  35.7 1.2 %ends.1 = f32[32,1,128]{2,1,0:T(1,128)} custom-call(s32[1,128]{1,0:T(1,128)S(1)} %copy-done.3, bf16[4,128,128]{2,1,0:T(8,128)(2,1)S(1)} %get-tuple-element.29.end_query_ref, f32[384,128]{1,0:T(8,128)S(1)} %get-tuple-element.30.end_bias_ref, f32[4,128,128]{2,1,0:T(8,128)S(1)} %get-tuple-element.31.end_weight_ref, f32[1,128]{1,0:T(1,128)S(1)} %get-tuple-element.32.reward_ref, ...), custom_call_target="tpu_custom_call" | custom-call | tf_op jit(solution)/shard_map/ends/pallas_call | solution.py:417
  36.9 3.8 %all-to-all-start.1 = ((f32[32,1,128]{2,1,0:T(1,128)}), f32[32,1,128]{2,1,0:T(1,128)S(1)}, u32[]{:S(2)}, u32[]{:S(2)}) async-start(f32[32,1,128]{2,1,0:T(1,128)} %ends.1), calls=%async_computation.1 | async-start | bytes 32768 | tf_op jit(solution)/shard_map/all_to_all | solution.py:435
  40.7 2.4 %last_share.1 = bf16[128,4096]{1,0:T(8,128)(2,1)} custom-call(bf16[16,8,4096]{2,1,0:T(8,128)(2,1)S(1)} %unsort_query.1.query_ref.refs_1_, bf16[128,4096]{1,0:T(8,128)(2,1)} %get-tuple-element.26.before_ref, f32[384,128]{1,0:T(8,128)S(1)} %get-tuple-element.27.bias_ref, ...), custom_call_target="tpu_custom_call", output_to_operand_aliasing={{}: (1, {})} | custom-call | tf_op jit(solution)/shard_map/last_share/pallas_call | solution.py:425
  43.2 4.7 %all-to-all-done.1.refs_0_ = f32[32,1,128]{2,1,0:T(1,128)S(1)} async-done(((f32[32,1,128]{2,1,0:T(1,128)}), f32[32,1,128]{2,1,0:T(1,128)S(1)}, u32[]{:S(2)}, u32[]{:S(2)}) %all-to-all-start.1) | async-done | bytes 16416 | tf_op jit(solution)/shard_map/all_to_all | solution.py:435
  47.9 1.1 %total.1 = f32[1,512]{1,0:T(1,128)} custom-call(f32[32,1,128]{2,1,0:T(1,128)S(1)} %all-to-all-done.1.refs_0_), custom_call_target="tpu_custom_call" | custom-call | tf_op jit(solution)/shard_map/total/pallas_call | solution.py:436
  (8 shorter events, 0.0 us)
Async XLA Ops:
  3.1 5.4 %copy-start = (bf16[8,8,4096]{2,1,0:T(8,128)(2,1)S(1)}, bf16[8,8,4096]{2,1,0:T(8,128)(2,1)}, u32[]{:S(2)}) copy-start(bf16[8,8,4096]{2,1,0:T(8,128)(2,1)} %get-tuple-element.18.refs_0_) | copy-start | bytes 1572868
  3.2 5.4 %collective-permute-start = (bf16[8,8,4096]{2,1,0:T(8,128)(2,1)}, bf16[8,8,4096]{2,1,0:T(8,128)(2,1)S(1)}, u32[]{:S(2)}, u32[]{:S(2)}) collective-permute-start(bf16[8,8,4096]{2,1,0:T(8,128)(2,1)} %get-tuple-element.19), channel_id=1, source_target_pairs={{0,4},{4,0},{8,12},{12,8},{16,20},{20,16},{24,28},{28,24},{1,5},{5... | collective-permute-start | bytes 1572872 | tf_op jit(solution)/shard_map/ppermute | solution.py:315
  3.7 12.3 %all-to-all-start = ((bf16[8,16,1024]{2,1,0:T(8,128)(2,1)}), bf16[8,16,1024]{2,1,0:T(8,128)(2,1)S(1)}, u32[]{:S(2)}, u32[]{:S(2)}) async-start(bf16[8,16,1024]{2,1,0:T(8,128)(2,1)} %bitcast.12), calls=%async_computation | async-start | bytes 524288 | tf_op jit(solution)/shard_map/all_to_all | solution.py:343
  8.6 7.3 %copy-start.2 = (s32[8,16]{1,0:T(8,128)S(1)}, s32[8,16]{1,0:T(8,128)}, u32[]{:S(2)}) copy-start(s32[8,16]{1,0:T(8,128)} %refs_0_.5) | copy-start | bytes 1540
  8.7 19.4 %collective-permute-start.1 = (bf16[4,8,4096]{2,1,0:T(8,128)(2,1)S(1)}, bf16[4,8,4096]{2,1,0:T(8,128)(2,1)S(1)}, u32[]{:S(2)}, u32[]{:S(2)}) collective-permute-start(bf16[4,8,4096]{2,1,0:T(8,128)(2,1)S(1)} %get-tuple-element.21), channel_id=1, source_target_pairs={{0,8},{4,12},{8,0},{12,4},{16,24},{20,28},{24,16},{28,20},{1,9},{5... | collective-permute-start | bytes 786440 | tf_op jit(solution)/shard_map/ppermute | solution.py:315
  10.7 17.3 %collective-permute-start.2 = (bf16[4,8,4096]{2,1,0:T(8,128)(2,1)S(1)}, bf16[4,8,4096]{2,1,0:T(8,128)(2,1)S(1)}, u32[]{:S(2)}, u32[]{:S(2)}) collective-permute-start(bf16[4,8,4096]{2,1,0:T(8,128)(2,1)S(1)} %get-tuple-element.22), channel_id=1, source_target_pairs={{0,16},{4,20},{8,24},{12,28},{16,0},{20,4},{24,8},{28,12},{1,17},{... | collective-permute-start | bytes 786440 | tf_op jit(solution)/shard_map/ppermute | solution.py:315
  12.2 3.8 %copy-start.3 = (s32[1,128]{1,0:T(1,128)S(1)}, s32[1,128]{1,0:T(1,128)}, u32[]{:S(2)}) copy-start(s32[1,128]{1,0:T(1,128)} %seg_ref.3) | copy-start | bytes 1540
  12.2 3.8 %copy-start.4 = (s32[1,16]{1,0:T(1,128)S(1)}, s32[1,16]{1,0:T(1,128)}, u32[]{:S(2)}) copy-start(s32[1,16]{1,0:T(1,128)} %refs_1_.1) | copy-start | bytes 196
  12.2 15.8 %collective-permute-start.3 = (bf16[4,8,4096]{2,1,0:T(8,128)(2,1)S(1)}, bf16[4,8,4096]{2,1,0:T(8,128)(2,1)S(1)}, u32[]{:S(2)}, u32[]{:S(2)}) collective-permute-start(bf16[4,8,4096]{2,1,0:T(8,128)(2,1)S(1)} %get-tuple-element.23), channel_id=1, source_target_pairs={{0,24},{4,28},{8,16},{12,20},{16,8},{20,12},{24,0},{28,4},{1,25},{... | collective-permute-start | bytes 786440 | tf_op jit(solution)/shard_map/ppermute | solution.py:315
  17.0 7.0 %collective-permute-start.4 = (bf16[17,8,512]{2,1,0:T(8,128)(2,1)S(1)}, bf16[17,8,512]{2,1,0:T(8,128)(2,1)S(1)}, u32[]{:S(2)}, u32[]{:S(2)}) collective-permute-start(bf16[17,8,512]{2,1,0:T(8,128)(2,1)S(1)} %get-tuple-element.25.rest_0_), channel_id=1, source_target_pairs={{0,1},{1,2},{2,3},{4,5},{5,6},{6,7},{8,9},{9,10},{10,11},{12,13},{... | collective-permute-start | bytes 417800 | tf_op jit(solution)/shard_map/ppermute | solution.py:394
  20.5 7.5 %collective-permute-start.6 = (bf16[16,8,512]{2,1,0:T(8,128)(2,1)S(1)}, bf16[16,8,512]{2,1,0:T(8,128)(2,1)S(1)}, u32[]{:S(2)}, u32[]{:S(2)}) collective-permute-start(bf16[16,8,512]{2,1,0:T(8,128)(2,1)S(1)} %get-tuple-element.28.rest_0_), channel_id=1, source_target_pairs={{0,1},{1,2},{2,3},{4,5},{5,6},{6,7},{8,9},{9,10},{10,11},{12,13},{... | collective-permute-start | bytes 393224 | tf_op jit(solution)/shard_map/ppermute | solution.py:394
  24.0 8.7 %collective-permute-start.5 = (bf16[17,8,512]{2,1,0:T(8,128)(2,1)S(1)}, bf16[17,8,512]{2,1,0:T(8,128)(2,1)S(1)}, u32[]{:S(2)}, u32[]{:S(2)}) collective-permute-start(bf16[17,8,512]{2,1,0:T(8,128)(2,1)S(1)} %collective-permute-done.4.rest_1_), channel_id=1, source_target_pairs={{0,1},{1,2},{2,3},{4,5},{5,6},{6,7},{8,9},{9,10},{10,11},{12,13},{... | collective-permute-start | bytes 417800 | tf_op jit(solution)/shard_map/ppermute | solution.py:394
  29.1 3.7 %copy-start.1 = (f32[4096]{0:T(1024)S(1)}, f32[4096]{0:T(1024)}, u32[]{:S(2)}) copy-start(f32[4096]{0:T(1024)} %param.13) | copy-start | bytes 49156
  29.1 6.6 %collective-permute-start.7 = (bf16[16,8,512]{2,1,0:T(8,128)(2,1)S(1)}, bf16[16,8,512]{2,1,0:T(8,128)(2,1)S(1)}, u32[]{:S(2)}, u32[]{:S(2)}) collective-permute-start(bf16[16,8,512]{2,1,0:T(8,128)(2,1)S(1)} %after_query.1), channel_id=1, source_target_pairs={{0,1},{1,2},{2,3},{4,5},{5,6},{6,7},{8,9},{9,10},{10,11},{12,13},{... | collective-permute-start | bytes 393224 | tf_op jit(solution)/shard_map/ppermute | solution.py:394
  36.9 11.0 %all-to-all-start.1 = ((f32[32,1,128]{2,1,0:T(1,128)}), f32[32,1,128]{2,1,0:T(1,128)S(1)}, u32[]{:S(2)}, u32[]{:S(2)}) async-start(f32[32,1,128]{2,1,0:T(1,128)} %ends.1), calls=%async_computation.1 | async-start | bytes 32768 | tf_op jit(solution)/shard_map/all_to_all | solution.py:435
